TPU v7x, 32 devices: a whole 2x2x4 slice. The times are simulated.
32 devices in a mesh: dp: 4 (over x, core), seq: 8 (over z, y).
Axes of the slice: x: 2, y: 2, z: 4, core: 2. Of those that a mesh axis runs over, the one named last changes fastest.
Arguments:
- tokens: bfloat16 [4096, 512], P(('dp', 'seq')), may hold values from -6 to 6
- seg_start: int32 [4096], P(('dp', 'seq')), may hold values from 0 to 4032, as said below
- norm_one: float32 [512], replicated, may hold values from 0.5 to 1.5
- w_in: bfloat16 [512, 2048], replicated, may hold values from -0.25 to 0.25
- conv_w: float32 [4, 1024], replicated, may hold values from -3 to 3
- conv_b: float32 [1024], replicated, may hold values from -2.5 to 2.5
- w_xproj: bfloat16 [1024, 64], replicated, may hold values from -0.1875 to 0.1875
- w_dt: bfloat16 [32, 1024], replicated, may hold values from -2 to 2
- dt_bias: float32 [1024], replicated, may hold values from -13 to -3
- a_log: float32 [1024, 16], replicated, may hold values from 0 to 2
- d_skip: float32 [1024], replicated, may hold values from 0.5 to 1.5
- w_out: bfloat16 [1024, 512], replicated, may hold values from -0.75 to 0.75
- norm_two: float32 [512], replicated, may hold values from 0.5 to 1.5
- w_qkv: bfloat16 [512, 1536], replicated, may hold values from -0.25 to 0.25
- w_proj: bfloat16 [512, 512], replicated, may hold values from -1.5 to 1.5
- cotangent: bfloat16 [4096, 512], P(('dp', 'seq')), may hold values from -6 to 6
Outputs:
- out: bfloat16 [4096, 512], P(('dp', 'seq'))
- grad_tokens: float32 [4096, 512], P(('dp', 'seq'))
- grad_norm_one: float32 [512], replicated
- grad_w_in: float32 [512, 2048], replicated
- grad_conv_w: float32 [4, 1024], replicated
- grad_conv_b: float32 [1024], replicated
- grad_w_xproj: float32 [1024, 64], replicated
- grad_w_dt: float32 [32, 1024], replicated
- grad_dt_bias: float32 [1024], replicated
- grad_a_log: float32 [1024, 16], replicated
- grad_d_skip: float32 [1024], replicated
- grad_w_out: float32 [1024, 512], replicated
- grad_norm_two: float32 [512], replicated
- grad_w_qkv: float32 [512, 1536], replicated
- grad_w_proj: float32 [512, 512], replicated
Inputs may be any that keep to these rules, and one draw needn't show every extreme that they name: seg_start[t] is the index of the first token of token t's sequence: never falling, at most t, equal to t at every start, and every batch group of 1024 tokens begins a sequence. Each group holds one to three sequences: a head of at most 64 tokens (possibly none), a main sequence that starts within the group's first 64 tokens and ends within its last 64 tokens, and a tail of at most 64 tokens (possibly none). The first group is one sequence of 1024 tokens; the last group's last sequence has exactly 64 tokens.
All inputs are finite; a program needn't handle non-finite values.
Results may differ from a plain program's by a relative error of at most 0.014.
The roundings to bfloat16 on the way count: a program that leaves them out, or rounds other values in their place, can miss the bound.
Values may be sent and summed in bfloat16 or wider, within the bound.
No kernel may reach another device: no remote copies, remote signals or barrier semaphores. Data moves between devices by JAX's collectives and lax.ppermute only.
A program may use at most 256 MiB of HBM per device.

v0:
```python
import functools

import jax
import jax.numpy as jnp
from jax import lax
from jax.experimental import pallas as pl
from jax.experimental.pallas import tpu as pltpu
from jax.sharding import PartitionSpec as P

H = 8
HD = 64
LANES = 128
HALO = 16
SMALL = 128
RESET = 1e30
EPSILON = 1e-05
LOG2E = 1.4426950408889634
LN2 = 0.6931471805599453
BF = jnp.bfloat16
F32 = jnp.float32
VMEM_LIMIT = 48 * 1024 * 1024


def dot(a, b):
    return jnp.dot(a, b, preferred_element_type=F32)


def dot_nt(a, b):
    return lax.dot_general(a, b, (((1,), (1,)), ((), ())), preferred_element_type=F32)


def dot_tn(a, b):
    return lax.dot_general(a, b, (((0,), (0,)), ((), ())), preferred_element_type=F32)


def tile(j):
    return slice(j * LANES, (j + 1) * LANES)


def softplus(x):
    u = jnp.exp(-jnp.abs(x))
    series = u * (1.0 - u * (0.5 - u * (1.0 / 3.0 - u * 0.25)))
    return jnp.maximum(x, 0.0) + jnp.where(u < 0.015, series, jnp.log(1.0 + u))


def rms_parts(x):
    return lax.rsqrt(jnp.mean(x * x, axis=-1, keepdims=True) + EPSILON)


def rms_back(x, gain, grad):
    r = rms_parts(x)
    scaled = grad * gain
    inner = jnp.mean(x * scaled, axis=-1, keepdims=True)
    return r * scaled - x * (r * r * r * inner), grad * x * r


def to_rows(ref, j, value):
    ref[pl.ds(j, value.shape[0], stride=8), :] = value


def from_rows(ref, j, count):
    return ref[pl.ds(j, count, stride=8), :]


def block(ref, t):
    return ref[pl.ds(pl.multiple_of(t * 8, 8), 8), :]


def offsets_in_sequence(seg_ref, seq_size):
    count = seg_ref.shape[1]
    base = (lax.axis_index("dp") * seq_size + lax.axis_index("seq")) * count
    places = base + lax.broadcasted_iota(jnp.int32, (1, count), 1)
    row = (places - seg_ref[...]).astype(F32)
    return jnp.transpose(jnp.broadcast_to(row, (LANES, count)))


def conv_tile(ext_ref, w_ref, b_ref, offset, j, count):
    taps = w_ref.shape[0]
    pre = jnp.broadcast_to(b_ref[:, tile(j)], (count, LANES))
    for k in range(taps):
        rows = ext_ref[pl.ds(HALO - taps + 1 + k, count), tile(j)]
        pre = pre + jnp.where(offset >= taps - 1 - k, w_ref[k : k + 1, tile(j)] * rows, 0.0)
    return pre


def forward_kernel(
    seq_size, tok, halo, cot, n1, w_in, conv_w, conv_b, w_xp, w_dt, dtb, a_log, seg,
    o_msg, o_nc, o_inner, o_gate, o_mixed, o_bc, o_low, o_pre, o_s, o_dx, o_a,
    ext, smem, sem,
):
    count, width = tok.shape
    states = a_log.shape[0]
    inner_width = conv_w.shape[1]
    tiles = inner_width // LANES
    rank = w_dt.shape[0]
    x = jnp.concatenate([halo[...], tok[...]], axis=0).astype(F32)
    normed = (x * rms_parts(x) * n1[...]).astype(BF)
    o_nc[:, :width] = normed[HALO:]
    o_nc[:, width:] = cot[...]
    inner = dot(normed, w_in[:, :inner_width]).astype(BF)
    o_inner[...] = inner
    ext[...] = inner.astype(F32)
    o_gate[...] = dot(normed[HALO:], w_in[:, inner_width:]).astype(BF)
    offset = offsets_in_sequence(seg, seq_size)
    for j in range(tiles):
        pre = conv_tile(ext, conv_w, conv_b, offset, j, count)
        o_mixed[:, tile(j)] = (pre * jax.nn.sigmoid(pre)).astype(BF)
    selector = dot(o_mixed[...], w_xp[...])
    low = selector[:, :rank].astype(BF)
    o_low[...] = low
    o_bc[...] = selector[:, rank:]
    copy = pltpu.make_async_copy(o_bc, smem, sem)
    copy.start()
    o_pre[...] = dot(low, w_dt[...]) + dtb[...]
    for j in range(tiles):
        step = softplus(o_pre[:, tile(j)])
        to_rows(o_s, j, jnp.where(offset == 0.0, RESET, step))
        to_rows(o_dx, j, step * o_mixed[:, tile(j)].astype(F32))
        to_rows(o_a, j, -LOG2E * jnp.exp(a_log[:, tile(j)]))
    copy.wait()

    def one(t, carry):
        total, state = carry
        s, dx = block(o_s, t), block(o_dx, t)
        return total + s, tuple(
            jnp.exp2(s * block(o_a, n)) * state[n] + dx * smem[t, n] for n in range(states)
        )

    zero = jnp.zeros((8, LANES), F32)
    total, state = lax.fori_loop(0, count, one, (zero, (zero,) * states), unroll=4)
    high = total.astype(BF).astype(F32)
    seg_local = (seg[...] - lax.axis_index("dp") * (seq_size * count)).astype(F32)
    seg_high = jnp.floor(seg_local * (1.0 / 64.0))
    last = jnp.concatenate([seg_high, seg_local - 64.0 * seg_high, jnp.zeros((14, LANES), F32)], axis=0)
    blocks = [jnp.concatenate([state[n], state[n + 1]], axis=0) for n in range(0, states, 2)]
    blocks += [jnp.concatenate([high, total - high], axis=0), last]
    for i, value in enumerate(blocks):
        value = value.astype(BF)
        for d in range(seq_size):
            o_msg[d, 16 * i : 16 * i + 16, :] = value


def total_step(msg, d, states):
    rows = msg[d, states * 8 : states * 8 + 16, :].astype(F32)
    return rows[:8] + rows[8:]


def state_rows(msg, d, n):
    rows = msg[d, 16 * (n // 2) : 16 * (n // 2) + 16, :].astype(F32)
    return rows[:8] if n % 2 == 0 else rows[8:]


def middle_kernel(
    msg, s_ref, dx_ref, bc, a_ref, mixed, gate, d_skip, tok, w_out, n2, w_qkv, cot, w_proj,
    o_qkvg, o_start, o_ssm, o_gn, o_after,
    y_ref, smem, sem,
):
    count, inner_width = mixed.shape
    width = tok.shape[1]
    tiles = inner_width // LANES
    states = a_ref.shape[0] // 8
    copy = pltpu.make_async_copy(bc, smem, sem)
    copy.start()
    zero = jnp.zeros((8, LANES), F32)

    def join(d, carry):
        total = total_step(msg, d, states)
        return tuple(
            jnp.exp2(block(a_ref, n) * total) * carry[n] + state_rows(msg, d, n)
            for n in range(states)
        )

    start = lax.fori_loop(0, lax.axis_index("seq"), join, (zero,) * states)
    for n in range(states):
        o_start[8 * n : 8 * n + 8, :] = start[n]
    copy.wait()

    def one(t, state):
        s, dx = block(s_ref, t), block(dx_ref, t)
        state = tuple(
            jnp.exp2(s * block(a_ref, n)) * state[n] + dx * smem[t, n] for n in range(states)
        )
        parts = [state[n] * smem[t, states + n] for n in range(states)]
        while len(parts) > 1:
            parts = [a + b for a, b in zip(parts[::2], parts[1::2])]
        y_ref[pl.ds(pl.multiple_of(t * 8, 8), 8), :] = parts[0]
        return state

    lax.fori_loop(0, count, one, start, unroll=4)
    for j in range(tiles):
        ssm = from_rows(y_ref, j, count) + d_skip[:, tile(j)] * mixed[:, tile(j)].astype(F32)
        o_ssm[:, tile(j)] = ssm
        v = gate[:, tile(j)].astype(F32)
        o_gn[:, tile(j)] = (ssm * (v * jax.nn.sigmoid(v))).astype(BF)
    after = tok[...].astype(F32) + dot(o_gn[:, :inner_width], w_out[...])
    o_after[...] = after
    normed = (after * rms_parts(after) * n2[...]).astype(BF)
    o_gn[:, inner_width:] = normed
    qkv = dot(normed, w_qkv[...])
    gatt = dot_nt(cot[...], w_proj[...])
    copies = o_qkvg.shape[0] // H
    left = lax.broadcasted_iota(jnp.int32, (count, LANES), 1) < HD
    for p in range(H // 2):
        q, k, v = (qkv[:, i * width + p * LANES : i * width + (p + 1) * LANES] for i in range(3))
        g = gatt[:, tile(p)]
        first = (jnp.where(left, q, pltpu.roll(k, HD, 1)), jnp.where(left, v, pltpu.roll(g, HD, 1)))
        second = (jnp.where(left, pltpu.roll(q, HD, 1), k), jnp.where(left, pltpu.roll(v, HD, 1), g))
        for h, pair in ((2 * p, first), (2 * p + 1, second)):
            for i, value in enumerate(pair):
                value = value.astype(BF)
                for r in range(copies):
                    o_qkvg[h * copies + r, :, tile(i)] = value


def attention_kernel(qkvg, msg, o_back, qz, kr, gz, vr, dk, dv):
    seq_size, count = qkvg.shape[0], qkvg.shape[1]
    rows = seq_size * count
    starts_at = msg.shape[1] - 16
    left = lax.broadcasted_iota(jnp.int32, (count, LANES), 1) < HD
    for d in range(seq_size):
        at = slice(d * count, (d + 1) * count)
        a, b = qkvg[d, :, :LANES].astype(F32), qkvg[d, :, LANES:].astype(F32)
        qz[at, :] = jnp.where(left, a, 0.0).astype(BF)
        kr[at, :] = pltpu.roll(a, HD, 1).astype(BF)
        gz[at, :] = jnp.where(left, 0.0, b).astype(BF)
        vr[at, :] = pltpu.roll(b, HD, 1).astype(BF)
    dk[...] = jnp.zeros_like(dk)
    dv[...] = jnp.zeros_like(dv)
    scale = HD**-0.5

    def queries(b, length):
        at = pl.ds(b * count if isinstance(b, int) else pl.multiple_of(b * count, count), count)
        tail = msg[b, starts_at : starts_at + 16, :].astype(F32)
        starts = jnp.broadcast_to(tail[0:1] * 64.0 + tail[1:2], (LANES, LANES))
        first = jnp.transpose(starts)[:, :1].astype(jnp.int32)
        column = lax.broadcasted_iota(jnp.int32, (count, length), 1)
        row = b * count + lax.broadcasted_iota(jnp.int32, (count, 1), 0)
        visible = (column <= row) & (column >= first)
        scores = jnp.where(visible, dot_nt(qz[at, :], kr[:length, :]) * scale, -1e30)
        weight = jnp.exp(scores - jnp.max(scores, axis=1, keepdims=True))
        probs = weight * (1.0 / jnp.sum(weight, axis=1, keepdims=True))
        low = probs.astype(BF)
        grad_probs = dot_nt(gz[at, :], vr[:length, :])
        delta = jnp.sum(probs * grad_probs, axis=1, keepdims=True)
        grad_scores = (probs * (grad_probs - delta)).astype(BF)
        dk[:length, :] += dot_tn(grad_scores, kr[at, :])
        dv[:length, :] += dot_tn(low, vr[at, :])
        dq = dot(grad_scores, kr[:length, :])
        attended = dot(low, vr[:length, :])
        o_back[b, :, :LANES] = (dq * scale).astype(BF)
        o_back[b, :, LANES:] = attended.astype(BF)

    if seq_size <= 8:
        for b in range(seq_size):
            queries(b, (b + 1) * count)
    else:
        lax.fori_loop(0, seq_size, lambda b, _: (queries(b, rows), 0)[1], 0)
    for d in range(seq_size):
        at = slice(d * count, (d + 1) * count)
        o_back[d, :, :LANES] = jnp.where(left, o_back[d, :, :LANES].astype(F32), dk[at, :] * scale).astype(BF)
        o_back[d, :, LANES:] = jnp.where(left, dv[at, :], o_back[d, :, LANES:].astype(F32)).astype(BF)


def backward_kernel(
    back, after, cot, w_proj, w_qkv, n2, w_out, gate, ssm, s_ref, bc, a_ref,
    o_out, o_after, o_n2, o_gate, o_g, o_msg,
    turned, smem, sem,
):
    seq_size, count = back.shape[0], back.shape[1]
    width = after.shape[1]
    inner_width = gate.shape[1]
    tiles = inner_width // LANES
    states = a_ref.shape[0] // 8
    copies = seq_size // H
    copy = pltpu.make_async_copy(bc, smem, sem)
    copy.start()
    left = lax.broadcasted_iota(jnp.int32, (count, LANES), 1) < HD
    dq, dk, dv, att = [], [], [], []
    for p in range(H // 2):
        a0, b0 = (back[2 * p * copies, :, tile(i)].astype(F32) for i in range(2))
        a1, b1 = (back[(2 * p + 1) * copies, :, tile(i)].astype(F32) for i in range(2))
        dq.append(jnp.where(left, a0, pltpu.roll(a1, HD, 1)))
        dk.append(jnp.where(left, pltpu.roll(a0, HD, 1), a1))
        dv.append(jnp.where(left, b0, pltpu.roll(b1, HD, 1)))
        att.append(jnp.where(left, pltpu.roll(b0, HD, 1), b1))
    attended = jnp.concatenate(att, axis=1).astype(BF)
    o_out[...] = (after[...] + dot(attended, w_proj[...])).astype(BF)
    grad_qkv = jnp.concatenate(dq + dk + dv, axis=1).astype(BF)
    grad_x, grad_gain = rms_back(after[...], n2[...], dot_nt(grad_qkv, w_qkv[...]))
    o_n2[...] = jnp.sum(grad_gain, axis=0, keepdims=True)
    grad_after = cot[...].astype(F32) + grad_x
    o_after[...] = grad_after
    branch = grad_after.astype(BF)
    grad_gated = dot_nt(branch, w_out[...])
    gate_rows = inner_width // seq_size
    branch_rows = width // seq_size
    for j in range(tiles):
        v = gate[:, tile(j)].astype(F32)
        sig = jax.nn.sigmoid(v)
        grad = grad_gated[:, tile(j)]
        to_rows(o_g, j, grad * (v * sig))
        grad_gate = grad * ssm[:, tile(j)] * (sig * (1.0 + v * (1.0 - sig)))
        o_gate[:, tile(j)] = grad_gate.astype(BF)
        turned[tile(j), :] = jnp.transpose(grad_gate).astype(BF)
    for d in range(seq_size):
        o_msg[d, states * 8 : states * 8 + gate_rows, :] = turned[d * gate_rows : (d + 1) * gate_rows, :]
    for j in range(width // LANES):
        turned[tile(j), :] = jnp.transpose(grad_after[:, tile(j)]).astype(BF)
    for d in range(seq_size):
        o_msg[d, states * 8 + gate_rows :, :] = turned[d * branch_rows : (d + 1) * branch_rows, :]
    copy.wait()

    def one(i, later):
        t = count - 1 - i
        s, g = block(s_ref, t), block(o_g, t)
        return tuple(
            jnp.exp2(s * block(a_ref, n)) * (g * smem[t, states + n] + later[n])
            for n in range(states)
        )

    leaving = lax.fori_loop(0, count, one, (jnp.zeros((8, LANES), F32),) * states, unroll=4)
    for n in range(0, states, 2):
        value = jnp.concatenate([leaving[n], leaving[n + 1]], axis=0).astype(BF)
        for d in range(seq_size):
            o_msg[d, 8 * n : 8 * n + 16, :] = value


def fold8(values, sub):
    low4, low2, low1 = sub < 4, (sub & 2) == 0, (sub & 1) == 0
    four = []
    for k in range(4):
        a, b = values[k], values[k + 4]
        four.append(jnp.where(low4, a, b) + pltpu.roll(jnp.where(low4, b, a), 4, 0))
    two = []
    for k in range(2):
        a, b = four[k], four[k + 2]
        two.append(jnp.where(low2, a + pltpu.roll(a, 6, 0), b + pltpu.roll(b, 2, 0)))
    a, b = two
    return jnp.where(low1, a + pltpu.roll(a, 7, 0), b + pltpu.roll(b, 1, 0))


def adjoint_kernel(
    seq_size, back, msg, start, s_ref, dx_ref, g_ref, bc, a_ref, mixed, low, step_pre, inner, conv_w, conv_b, seg,
    w_dt, w_xp, d_skip, grad_gate, w_in, tok, halo, n1, grad_after, grad_n2,
    o_msg, o_tok, o_halo,
    held, gs_ref, ai_ref, sums, small, ext, gext, smem, sem,
):
    count, inner_width = mixed.shape
    width = tok.shape[1]
    tiles = inner_width // LANES
    states = a_ref.shape[0] // 8
    rank = w_dt.shape[0]
    taps = conv_w.shape[0]
    copy = pltpu.make_async_copy(bc, smem, sem)
    copy.start()
    zero = jnp.zeros((8, LANES), F32)
    for n in range(states):
        held[8 * n : 8 * n + 8, :] = start[8 * n : 8 * n + 8, :]
    copy.wait()

    def again(t, state):
        s, dx = block(s_ref, t), block(dx_ref, t)
        state = tuple(
            jnp.exp2(s * block(a_ref, n)) * state[n] + dx * smem[t, n] for n in range(states)
        )
        for n in range(states):
            held[pl.ds(pl.multiple_of(((t + 1) * states + n) * 8, 8), 8), :] = state[n]
        return state

    lax.fori_loop(0, count, again, tuple(start[8 * n : 8 * n + 8, :] for n in range(states)), unroll=2)

    def join(i, carry):
        d = seq_size - 1 - i
        total = total_step(msg, d, states)
        return tuple(
            jnp.exp2(block(a_ref, n) * total) * carry[n] + state_rows(back, d, n)
            for n in range(states)
        )

    leaving = lax.fori_loop(0, seq_size - 1 - lax.axis_index("seq"), join, (zero,) * states)
    sub = lax.broadcasted_iota(jnp.int32, (8, LANES), 0)

    def one(i, carry):
        later, grad_a = carry
        t = count - 1 - i
        s, dx, g = block(s_ref, t), block(dx_ref, t), block(g_ref, t)
        new_later, new_grad_a, with_b, with_c = [], [], [], []
        grad_step, adjoint_in = zero, zero
        for n in range(states):
            a = block(a_ref, n)
            adjoint = g * smem[t, states + n] + later[n]
            passed = jnp.exp2(s * a) * adjoint
            before = held[pl.ds(pl.multiple_of((t * states + n) * 8, 8), 8), :]
            now = held[pl.ds(pl.multiple_of(((t + 1) * states + n) * 8, 8), 8), :]
            grad_decay = passed * before
            grad_step = grad_step + grad_decay * a
            adjoint_in = adjoint_in + adjoint * smem[t, n]
            new_later.append(passed)
            new_grad_a.append(grad_a[n] + grad_decay * s)
            with_b.append(adjoint * dx)
            with_c.append(g * now)
        here = pl.ds(pl.multiple_of(t * 8, 8), 8)
        gs_ref[here, :] = grad_step
        ai_ref[here, :] = adjoint_in
        for i, part in enumerate((with_b[:8], with_b[8:], with_c[:8], with_c[8:])):
            sums[pl.ds(pl.multiple_of(t * 32 + 8 * i, 8), 8), :] = fold8(part, sub)
        return tuple(new_later), tuple(new_grad_a)

    _, grad_a = lax.fori_loop(0, count, one, (leaving, (zero,) * states))
    small[...] = jnp.zeros_like(small)
    for n in range(states):
        small[(104 + n) * 8 : (105 + n) * 8, :] = grad_a[n] * (LN2 * block(a_ref, n))
    lane = lax.broadcasted_iota(jnp.int32, (count, rank + 2 * states), 1)
    grad_bc = jnp.zeros((count, rank + 2 * states), F32)
    for q in range(2 * states):
        total = jnp.sum(sums[pl.ds(q, count, stride=2 * states), :], axis=1, keepdims=True)
        grad_bc = jnp.where(lane == rank + q, total, grad_bc)
    offset = offsets_in_sequence(seg, seq_size)
    halves = []
    for j in range(tiles):
        mix = mixed[:, tile(j)].astype(F32)
        pre = step_pre[:, tile(j)]
        grad_step = LN2 * from_rows(gs_ref, j, count) + mix * from_rows(ai_ref, j, count)
        grad_pre = grad_step * jax.nn.sigmoid(pre)
        small[101 * 8 + j : 101 * 8 + j + 1, :] = jnp.sum(grad_pre, axis=0, keepdims=True)
        grad_ssm = from_rows(g_ref, j, count)
        small[102 * 8 + j : 102 * 8 + j + 1, :] = jnp.sum(grad_ssm * mix, axis=0, keepdims=True)
        halves.append(grad_pre.astype(BF))
    half = jnp.concatenate(halves, axis=1)
    grad_w_dt = dot_tn(low[...], half)
    padded_dt = jnp.concatenate([w_dt[...], jnp.zeros((2 * states, inner_width), BF)], axis=0)
    grad_selector = (dot_nt(half, padded_dt) + grad_bc).astype(BF)
    grad_w_xp = dot_tn(grad_selector, mixed[...])
    from_selector = dot_nt(grad_selector, w_xp[...])
    ext[...] = inner[...].astype(F32)
    gext[...] = jnp.zeros_like(gext)
    for j in range(tiles):
        to_rows(small.at[pl.ds(0, 64 * 8)], j, grad_w_xp[:, tile(j)])
        to_rows(small.at[pl.ds(64 * 8, 32 * 8)], j, grad_w_dt[:, tile(j)])
        pre = conv_tile(ext, conv_w, conv_b, offset, j, count)
        sig = jax.nn.sigmoid(pre)
        grad_mixed = (
            softplus(step_pre[:, tile(j)]) * from_rows(ai_ref, j, count)
            + from_rows(g_ref, j, count) * d_skip[:, tile(j)]
            + from_selector[:, tile(j)]
        )
        grad_pre = grad_mixed * (sig * (1.0 + pre * (1.0 - sig)))
        small[100 * 8 + j : 100 * 8 + j + 1, :] = jnp.sum(grad_pre, axis=0, keepdims=True)
        for k in range(taps):
            shifted = pl.ds(HALO - taps + 1 + k, count)
            usable = jnp.where(offset >= taps - 1 - k, grad_pre, 0.0)
            row = (96 + k) * 8 + j
            small[row : row + 1, :] = jnp.sum(usable * ext[shifted, tile(j)], axis=0, keepdims=True)
            gext[shifted, tile(j)] += conv_w[k : k + 1, tile(j)] * usable
    piece = inner_width // seq_size
    per = small.shape[0] // seq_size
    grad_inner = gext[...].astype(BF)
    for j in range(tiles):
        value = jnp.transpose(gext[HALO:, tile(j)]).astype(BF)
        for i in range(LANES // piece):
            o_msg[j * (LANES // piece) + i, :piece, :] = value[i * piece : (i + 1) * piece]
    for d in range(seq_size):
        rows = gext[:HALO, d * piece : (d + 1) * piece]
        if piece < LANES:
            rows = jnp.concatenate([rows, jnp.zeros((HALO, LANES - piece), F32)], axis=1)
        o_msg[d, piece : piece + HALO, :] = rows.astype(BF)
    grad_normed = dot_nt(grad_inner, w_in[:, :inner_width])
    own = dot_nt(grad_gate[...], w_in[:, inner_width:])
    grad_normed = jnp.concatenate([grad_normed[:HALO], grad_normed[HALO:] + own], axis=0)
    x = jnp.concatenate([halo[...], tok[...]], axis=0).astype(F32)
    grad_x, grad_gain = rms_back(x, n1[...], grad_normed)
    o_tok[...] = grad_after[...] + grad_x[HALO:]
    o_halo[...] = grad_x[HALO - 8 : HALO]
    grad_gain = jnp.sum(grad_gain, axis=0, keepdims=True)
    for j in range(width // LANES):
        small[103 * 8 + j : 103 * 8 + j + 1, :] = grad_gain[:, tile(j)]
        small[103 * 8 + 4 + j : 103 * 8 + 5 + j, :] = grad_n2[:, tile(j)]
    for d in range(seq_size):
        o_msg[d, piece + HALO :, :] = small[d * per : (d + 1) * per, :].astype(BF)


def early_products_kernel(width, back, nc, gn, adj, o_head, o_gate, o_out):
    seq_size, count = back.shape[0], back.shape[1]
    rows = seq_size * count
    inner_width = gn.shape[1] - width
    gate_rows, branch_rows = o_gate.shape[0], o_out.shape[0]
    at = adj.shape[1] - gate_rows - branch_rows
    both = back[...].reshape(rows, 2 * LANES)
    first = dot_tn(both[:, :LANES], gn[:, inner_width:])
    second = dot_tn(both[:, LANES:], gn[:, inner_width:])
    third = dot_tn(both[:, LANES:], nc[:, width:])
    o_head[:HD, :] = third[HD:].astype(BF)
    o_head[HD : 3 * HD, :] = first.astype(BF)
    o_head[3 * HD :, :] = second[:HD].astype(BF)
    gate = jnp.zeros((gate_rows, width), F32)
    out = jnp.zeros((branch_rows, inner_width), F32)
    for d in range(seq_size):
        src = slice(d * count, (d + 1) * count)
        gate = gate + dot(adj[d, at : at + gate_rows, :], nc[src, :width])
        out = out + dot(adj[d, at + gate_rows :, :], gn[src, :inner_width])
    o_gate[...] = gate.astype(BF)
    o_out[...] = out.astype(BF)


def late_products_kernel(width, tail, nc, o_in, o_small):
    seq_size = tail.shape[0]
    count = nc.shape[0] // seq_size
    piece = o_in.shape[0]
    grad = jnp.zeros((piece, width), F32)
    small = jnp.zeros(o_small.shape, F32)
    for d in range(seq_size):
        grad = grad + dot(tail[d, :piece, :], nc[d * count : (d + 1) * count, :width])
        small = small + tail[d, piece + HALO :, :].astype(F32)
        if d:
            borrowed = dot_tn(tail[d, piece : piece + HALO, :], nc[d * count - HALO : d * count, :width])
            grad = grad + borrowed[:piece]
    o_in[...] = grad.astype(BF)
    o_small[...] = small.astype(BF)


def call(kernel, outs, scratch, *args, name=None):
    return pl.pallas_call(
        kernel,
        out_shape=[jax.ShapeDtypeStruct(s, d) for s, d in outs],
        scratch_shapes=scratch,
        compiler_params=pltpu.CompilerParams(vmem_limit_bytes=VMEM_LIMIT),
        name=name,
    )(*args)


def exchange(value, axes):
    return lax.all_to_all(value, axes, 0, 0, tiled=True)


def everywhere(value):
    axes = ("dp", "seq")
    count = lax.axis_size(axes)
    return exchange(jnp.broadcast_to(value[None], (count,) + value.shape), axes)


def body(
    tokens, seg_start, norm_one, w_in, conv_w, conv_b, w_xproj, w_dt, dt_bias, a_log, d_skip,
    w_out, norm_two, w_qkv, w_proj, cotangent,
):
    count, width = tokens.shape
    inner_width = w_in.shape[1] // 2
    states = a_log.shape[1]
    rank = w_dt.shape[0]
    groups, seq_size = lax.axis_size("dp"), lax.axis_size("seq")
    rows = count * seq_size
    ext_rows = HALO + count
    piece = inner_width // seq_size
    branch = width // seq_size
    copies = seq_size // H
    line = lambda v: v.reshape(1, -1)
    seg = line(seg_start)
    n1, n2, cb, dtb, skip = (line(v) for v in (norm_one, norm_two, conv_b, dt_bias, d_skip))
    vmem, smem = pltpu.VMEM, pltpu.SMEM((count, 2 * states), F32)
    sem = pltpu.SemaphoreType.DMA
    blocks = ((count * 8, LANES), F32)
    onward = [(i, i + 1) for i in range(seq_size - 1)]
    halo = lax.ppermute(tokens[count - HALO :], "seq", onward)
    msg, nc, inner, gate, mixed, bc, low, step_pre, s, dx, a = call(
        functools.partial(forward_kernel, seq_size),
        [
            ((seq_size, states * 8 + 32, LANES), BF), ((count, 2 * width), BF), ((ext_rows, inner_width), BF),
            ((count, inner_width), BF), ((count, inner_width), BF), ((count, 2 * states), F32), ((count, rank), BF),
            ((count, inner_width), F32), blocks, blocks, ((states * 8, LANES), F32),
        ],
        [vmem((ext_rows, inner_width), F32), smem, sem],
        tokens, halo, cotangent, n1, w_in, conv_w, cb, w_xproj, w_dt, dtb, a_log.T, seg,
        name="forward",
    )
    nc_all = lax.all_gather(nc, "seq", axis=0, tiled=True)
    msg = exchange(msg, "seq")
    qkvg, start, ssm, gn, after = call(
        middle_kernel,
        [
            ((seq_size, count, 2 * LANES), BF), ((states * 8, LANES), F32), ((count, inner_width), F32),
            ((count, inner_width + width), BF), ((count, width), F32),
        ],
        [vmem(*blocks), smem, sem],
        msg, s, dx, bc, a, mixed, gate, skip, tokens, w_out, n2, w_qkv, cotangent, w_proj,
        name="middle",
    )
    gn_all = lax.all_gather(gn, "seq", axis=0, tiled=True)
    qkvg = exchange(qkvg, "seq")
    (back,) = call(
        attention_kernel,
        [((seq_size, count, 2 * LANES), BF)],
        [vmem((rows, LANES), BF)] * 4 + [vmem((rows, LANES), F32)] * 2,
        qkvg, msg, name="attention",
    )
    back_own = exchange(back, "seq")
    out, grad_after, grad_n2, grad_gate, g, adj = call(
        backward_kernel,
        [
            ((count, width), BF), ((count, width), F32), ((1, width), F32), ((count, inner_width), BF), blocks,
            ((seq_size, states * 8 + piece + branch, LANES), BF),
        ],
        [vmem((inner_width, LANES), BF), smem, sem],
        back_own, after, cotangent, w_proj, w_qkv, n2, w_out, gate, ssm, s, bc, a,
        name="backward",
    )
    adj = exchange(adj, "seq")
    head, gate_part, out_part = call(
        functools.partial(early_products_kernel, width),
        [((4 * HD, width), BF), ((piece, width), BF), ((branch, inner_width), BF)],
        [],
        back, nc_all, gn_all, adj, name="early_products",
    )
    if copies > 1:
        own = 4 * HD // copies
        head = lax.dynamic_slice_in_dim(head, lax.axis_index("seq") % copies * own, own, 0)
    early = jnp.concatenate([v.reshape(groups, -1, LANES) for v in (head, gate_part, out_part)], axis=1)
    early = jnp.sum(exchange(early, "dp").astype(F32), axis=0).astype(BF)
    early = lax.all_gather(early, ("dp", "seq"))
    tail, grad_tokens, grad_halo = call(
        functools.partial(adjoint_kernel, seq_size),
        [
            ((seq_size, piece + HALO + SMALL * 8 // seq_size, LANES), BF), ((count, width), F32), ((8, width), F32),
        ],
        [
            vmem(((count + 1) * states * 8, LANES), F32), vmem(*blocks), vmem(*blocks),
            vmem((count * 2 * states, LANES), F32), vmem((SMALL * 8, LANES), F32),
            vmem((ext_rows, inner_width), F32), vmem((ext_rows, inner_width), F32), smem, sem,
        ],
        adj, msg, start, s, dx, g, bc, a, mixed, low, step_pre, inner, conv_w, cb, seg,
        w_dt, w_xproj, skip, grad_gate, w_in, tokens, halo, n1, grad_after, grad_n2,
        name="adjoint",
    )
    tail = exchange(tail, "seq")
    returned = lax.ppermute(grad_halo, "seq", [(i + 1, i) for i in range(seq_size - 1)])
    grad_tokens = grad_tokens.at[count - 8 :].add(returned)
    in_part, small = call(
        functools.partial(late_products_kernel, width),
        [((piece, width), BF), ((SMALL * 8 // seq_size, LANES), BF)],
        [],
        tail, nc_all, name="late_products",
    )
    late = jnp.concatenate([v.reshape(groups, -1, LANES) for v in (in_part, small)], axis=1)
    late = jnp.sum(exchange(late, "dp").astype(F32), axis=0).astype(BF)
    late = everywhere(late)

    def whole(gathered, first, last):
        part = gathered.reshape(groups, seq_size, -1, LANES)[:, :, first:last]
        return part.swapaxes(0, 1).reshape(seq_size, -1)

    def cut(sizes):
        ends, total = [], 0
        for n in sizes:
            ends.append((total, total + n // LANES // groups))
            total = ends[-1][1]
        return ends

    at_head, at_gate, at_out = cut((4 * HD * width // copies, piece * width, branch * inner_width))
    at_in, at_small = cut((piece * width, SMALL * 8 // seq_size * LANES))
    heads = whole(early, *at_head).reshape(H, 4, HD, width)
    grad_w_proj = heads[:, 0].reshape(H * HD, width).astype(F32)
    grad_w_qkv = heads[:, 1:].transpose(3, 1, 0, 2).reshape(width, 3 * width).astype(F32)
    grad_w_out = whole(early, *at_out).reshape(width, inner_width).T.astype(F32)
    grad_w_in = jnp.concatenate(
        [whole(late, *at_in).reshape(inner_width, width), whole(early, *at_gate).reshape(inner_width, width)], axis=0
    ).T.astype(F32)
    small = whole(late, *at_small).reshape(SMALL, inner_width).astype(F32)
    return (
        out,
        grad_tokens,
        small[103, :width],
        grad_w_in,
        small[96:100],
        small[100],
        small[:64].T,
        small[64:96],
        small[101],
        small[104:120].T,
        small[102],
        grad_w_out,
        small[103, width:],
        grad_w_qkv,
        grad_w_proj,
    )


def solution(mesh):
    split, copied = P(("dp", "seq"), None), P()
    return jax.shard_map(
        body,
        mesh=mesh,
        in_specs=(split, P(("dp", "seq"))) + (copied,) * 13 + (split,),
        out_specs=(split, split) + (copied,) * 13,
        check_vma=False,
    )
```

profile of v0, /device:TPU:13, one launch (start us, length us, event | category | flops | bytes accessed | tf_op | source)
XLA Modules:
  0.0 341.4 jit_solution(153775631767018567)
XLA Ops:
  8.0 3.1 collective-permute-start
  11.2 1.1 copy.41.w_xp
  12.5 1.6 copy-done.2
  14.1 0.9 copy-done.7
  21.0 4.7 %forward.1 = (bf16[8,160,128]{2,1,0:T(8,128)(2,1)S(1)}, bf16[128,1024]{1,0:T(8,128)(2,1)S(1)}, bf16[144,1024]{1,0:T(8,128)(2,1)S(1)}, bf16[128,1024]{1,0:T(8,128...) custom-call(bf16[128,512]{1,0:T(8,128)(2,1)S(1)} %copy-done.7, ...), custom_call_target="tpu_custom_call" | custom-call | tf_op jit(solution)/shard_map/forward/pallas_call | solution.py:522
  31.3 13.7 %all_to_all.40.msg = bf16[8,160,128]{2,1,0:T(8,128)(2,1)S(1)} all-to-all(bf16[8,160,128]{2,1,0:T(8,128)(2,1)} %copy-done.29), channel_id=1, replica_groups=mesh['dp'=4,'seq'=8] {'seq'}, dimensions={0} | all-to-all | bytes 655360 | tf_op jit(solution)/shard_map/all_to_all | solution.py:532
  45.1 0.9 copy-done.12
  46.0 0.9 copy-done.15
  49.2 6.8 %middle.1 = (bf16[8,128,256]{2,1,0:T(8,128)(2,1)S(1)}, f32[128,128]{1,0:T(8,128)S(1)}, f32[128,1024]{1,0:T(8,128)S(1)}, bf16[128,1536]{1,0:T(8,128)(2,1)S(1)}, f32[128,512]{1,0:T(8,128)S(1)}) custom-call(bf16[8,160,128]{2,1,0:T(8,128)(2,1)S(1)} %all_to_all.40.msg, f32[1024,128]{1,0:T(8,128)S(1)} %get-tuple-element.58.s_ref, ...), custom_call_target="tpu_custom_call" | custom-call | tf_op jit(solution)/shard_map/middle/pallas_call | solution.py:522
  59.7 30.3 %all_to_all.41.qkvg = bf16[8,128,256]{2,1,0:T(8,128)(2,1)S(1)} all-to-all(bf16[8,128,256]{2,1,0:T(8,128)(2,1)} %copy-done.27), channel_id=1, replica_groups=mesh['dp'=4,'seq'=8] {'seq'}, dimensions={0} | all-to-all | bytes 1048576 | tf_op jit(solution)/shard_map/all_to_all | solution.py:532
  90.0 5.5 %attention.1.back = bf16[8,128,256]{2,1,0:T(8,128)(2,1)S(1)} custom-call(bf16[8,128,256]{2,1,0:T(8,128)(2,1)S(1)} %all_to_all.41.qkvg, bf16[8,160,128]{2,1,0:T(8,128)(2,1)S(1)} %all_to_all.40.msg), custom_call_target="tpu_custom_call" | custom-call | tf_op jit(solution)/shard_map/attention/pallas_call | solution.py:522
  95.6 26.9 %all_to_all.42.back = bf16[8,128,256]{2,1,0:T(8,128)(2,1)S(1)} all-to-all(bf16[8,128,256]{2,1,0:T(8,128)(2,1)S(1)} %attention.1.back), channel_id=1, replica_groups=mesh['dp'=4,'seq'=8] {'seq'}, dimensions={0} | all-to-all | bytes 1048576 | tf_op jit(solution)/shard_map/all_to_all | solution.py:532
  122.5 0.9 copy-done.16
  125.0 6.3 %backward.1 = (bf16[128,512]{1,0:T(8,128)(2,1)}, f32[128,512]{1,0:T(8,128)S(1)}, f32[1,512]{1,0:T(1,128)S(1)}, bf16[128,1024]{1,0:T(8,128)(2,1)S(1)}, f32[1024,1...) custom-call(bf16[8,128,256]{2,1,0:T(8,128)(2,1)S(1)} %all_to_all.42.back, f32[128,512]{1,0:T(8,128)S(1)} %copy-done.37, ...), custom_call_target="tpu_custom_call" | custom-call | tf_op jit(solution)/shard_map/backward/pallas_call | solution.py:522
  134.1 38.0 %all_to_all.43.back.adj = bf16[8,320,128]{2,1,0:T(8,128)(2,1)S(1)} all-to-all(bf16[8,320,128]{2,1,0:T(8,128)(2,1)S(1)} %get-tuple-element.68), channel_id=1, replica_groups=mesh['dp'=4,'seq'=8] {'seq'}, dimensions={0} | all-to-all | bytes 1310720 | tf_op jit(solution)/shard_map/all_to_all | solution.py:532
  172.0 1.6 all-gather.7.cloned.1.call-done.gn
  173.6 1.6 copy-done
  175.2 3.0 early_products.1
  180.4 1.9 reshape.118
  182.3 1.6 reshape.119
  183.9 1.6 reshape.120
  185.5 1.1 pad_maximum_fusion
  186.6 11.4 %all_to_all.44 = bf16[4,512,128]{2,1,0:T(8,128)(2,1)} all-to-all(bf16[4,512,128]{2,1,0:T(8,128)(2,1)S(1)} %pad_maximum_fusion), channel_id=1, replica_groups=mesh['dp'=4,'seq'=8] {'dp'}, dimensions={0} | all-to-all | bytes 1048576 | tf_op jit(solution)/shard_map/all_to_all | solution.py:532
  198.1 1.8 reduce_sum.25
  200.0 1.0 copy-done.22
  201.1 1.0 copy-done.24
  202.1 0.9 copy-done.35
  204.5 19.6 %adjoint.1 = (bf16[8,272,128]{2,1,0:T(8,128)(2,1)S(1)}, f32[128,512]{1,0:T(8,128)}, f32[8,512]{1,0:T(8,128)S(1)}) custom-call(bf16[8,320,128]{2,1,0:T(8,128)(2,1)S(1)} %all_to_all.43.back.adj, bf16[8,160,128]{2,1,0:T(8,128)(2,1)S(1)} %all_to_all.40.msg, f32[128,128]{1,0:T(8,128)S(1)} %copy-done.45, f32[1024,128]{1,0:T(8,128)S(1)} %get-tuple-element.58.s_ref, ...), custom_call_target="tpu_custom_call" | custom-call | tf_op jit(solution)/shard_map/adjoint/pallas_call | solution.py:522
  224.1 23.4 %all_to_all.45.tail = bf16[8,272,128]{2,1,0:T(8,128)(2,1)S(1)} all-to-all(bf16[8,272,128]{2,1,0:T(8,128)(2,1)S(1)} %get-tuple-element.79), channel_id=1, replica_groups=mesh['dp'=4,'seq'=8] {'seq'}, dimensions={0} | all-to-all | bytes 1114112 | tf_op jit(solution)/shard_map/all_to_all | solution.py:532
  248.3 10.2 %all_to_all.46 = bf16[4,160,128]{2,1,0:T(8,128)(2,1)S(1)} all-to-all(bf16[4,160,128]{2,1,0:T(8,128)(2,1)S(1)} %pad_maximum_fusion.1), channel_id=1, replica_groups=mesh['dp'=4,'seq'=8] {'dp'}, dimensions={0} | all-to-all | bytes 327680 | tf_op jit(solution)/shard_map/all_to_all | solution.py:532
  258.6 1.2 broadcast_in_dim.2
  259.8 4.3 %all-to-all-start.6 = ((bf16[32,160,128]{2,1,0:T(8,128)(2,1)}), bf16[32,160,128]{2,1,0:T(8,128)(2,1)S(1)}, u32[]{:S(2)}, u32[]{:S(2)}) async-start(bf16[32,160,128]{2,1,0:T(8,128)(2,1)} %broadcast_in_dim.2), calls=%async_computation.6 | async-start | bytes 2621440 | tf_op jit(solution)/shard_map/all_to_all | solution.py:532
  264.2 2.2 collective-permute-start.1
  266.3 28.4 %collective-permute-done.1 = f32[8,512]{1,0:T(8,128)S(1)} collective-permute-done((f32[8,512]{1,0:T(8,128)S(1)}, f32[8,512]{1,0:T(8,128)S(1)}, u32[]{:S(2)}, u32[]{:S(2)}) %collective-permute-start.1) | collective-permute-done | bytes 16416 | tf_op jit(solution)/shard_map/ppermute | solution.py:633
  294.8 1.3 add_dynamic-update-slice_fusion
  296.5 1.5 reshape_reshape.11
  302.0 3.3 slice_bitcast_fusion
  305.2 1.2 convert_bitcast_fusion.1
  306.5 4.3 %reshape_reshape.13 = bf16[8,4,64,512]{3,2,0,1:T(8,128)(2,1)} reshape(bf16[8,4,256,128]{3,2,0,1:T(8,128)(2,1)} %slice_bitcast_fusion) | data formatting | bytes 4194304 | tf_op jit(solution)/shard_map/reshape;reshape | solution.py:658
  310.8 3.5 %slice_convert_fusion = f32[8,3,64,512]{3,2,0,1:T(8,128)} fusion(bf16[8,4,64,512]{3,2,0,1:T(8,128)(2,1)} %reshape_reshape.13), kind=kLoop, calls=%fused_computation.3 | loop fusion | flops 786432 | bytes 4718592 | tf_op jit(solution)/shard_map/convert_element_type | solution.py:660
  314.3 1.5 copy.48
  315.8 1.7 reshape.124
  317.5 1.8 copy.50
  319.3 1.1 bitcast_convert_fusion
  320.5 3.6 %copy.51 = f32[512,1536]{1,0:T(8,128)} copy(f32[512,1536]{0,1:T(8,128)} %bitcast.66) | data formatting | bytes 6291456
  324.2 1.4 reshape_reshape.12
  325.7 3.8 %convert_bitcast_fusion = f32[512,2048]{0,1:T(8,128)} fusion(bf16[1024,512]{1,0:T(8,128)(2,1)} %reshape_reshape.12, bf16[1024,512]{1,0:T(8,128)(2,1)S(1)} %copy-done.68), kind=kLoop, calls=%fused_computation | loop fusion | flops 4194304 | bytes 6291456 | tf_op jit(solution)/shard_map/convert_element_type | solution.py:664
  329.5 5.3 %copy.49 = f32[512,2048]{1,0:T(8,128)} copy(f32[512,2048]{0,1:T(8,128)} %convert_bitcast_fusion) | data formatting | bytes 8388608
  (162 shorter events, 31.7 us)
Async XLA Ops:
  7.2 37.9 %copy-start.8 = (bf16[128,512]{1,0:T(8,128)(2,1)S(1)}, bf16[128,512]{1,0:T(8,128)(2,1)}, u32[]{:S(2)}) copy-start(bf16[128,512]{1,0:T(8,128)(2,1)} %tok.5) | copy-start | bytes 393220
  7.2 37.8 %copy-start.10 = (bf16[128,512]{1,0:T(8,128)(2,1)S(1)}, bf16[128,512]{1,0:T(8,128)(2,1)}, u32[]{:S(2)}) copy-start(bf16[128,512]{1,0:T(8,128)(2,1)} %cot.5) | copy-start | bytes 393220
  7.2 164.8 %all-gather.5.cloned.1.call-start = ((), (), s32[]{:S(2)}) async-start(), calls=%async_computation.8 | async-start | bytes 2359296 | tf_op jit(solution)/shard_map/all_gather | solution.py:574
  8.0 4.5 %collective-permute-start = (bf16[16,512]{1,0:T(8,128)(2,1)S(1)}, bf16[16,512]{1,0:T(8,128)(2,1)S(1)}, u32[]{:S(2)}, u32[]{:S(2)}) collective-permute-start(bf16[16,512]{1,0:T(8,128)(2,1)S(1)} %slice.76), channel_id=1, source_target_pairs={{0,1},{1,2},{2,3},{3,4},{4,5},{5,6},{6,7},{8,9},{9,10},{10,11},{11... | collective-permute-start | bytes 49160 | tf_op jit(solution)/shard_map/ppermute | solution.py:562
  12.5 1.6 copy-start.2
  14.1 0.9 copy-start.7
  15.0 0.9 copy-start.9
  15.9 0.8 copy-start.38
  17.5 0.8 copy-start.48
  21.0 24.0 %copy-start.3 = (bf16[1024,512]{1,0:T(8,128)(2,1)S(1)}, bf16[1024,512]{1,0:T(8,128)(2,1)}, u32[]{:S(2)}) copy-start(bf16[1024,512]{1,0:T(8,128)(2,1)} %w_out.3) | copy-start | bytes 3145732
  21.0 24.0 %copy-start.4 = (bf16[512,512]{1,0:T(8,128)(2,1)S(1)}, bf16[512,512]{1,0:T(8,128)(2,1)}, u32[]{:S(2)}) copy-start(bf16[512,512]{1,0:T(8,128)(2,1)} %w_proj.3) | copy-start | bytes 1572868
  31.3 24.7 %copy-start.5 = (f32[1024,128]{1,0:T(8,128)}, f32[1024,128]{1,0:T(8,128)S(1)}, u32[]{:S(2)}) copy-start(f32[1024,128]{1,0:T(8,128)S(1)} %get-tuple-element.59.dx_ref) | copy-start | bytes 1572868
  31.3 142.3 %all-gather.7.cloned.1.call-start = ((), (), s32[]{:S(2)}) async-start(), calls=%async_computation.9 | async-start | bytes 3538944 | tf_op jit(solution)/shard_map/all_gather | solution.py:586
  45.0 1.0 copy-start.12
  46.0 1.0 copy-start.15
  47.0 0.8 copy-start.18
  55.9 0.8 copy-start.25
  59.6 242.3 %all-gather.9.cloned.1.call-start = ((), (), s32[]{:S(2)}) async-start(), calls=%async_computation.10 | async-start | bytes 4325376 | tf_op jit(solution)/shard_map/all_gather | solution.py:617
  59.7 62.8 %copy-start.26 = (f32[128,1024]{1,0:T(8,128)S(1)}, f32[128,1024]{1,0:T(8,128)}, u32[]{:S(2)}) copy-start(f32[128,1024]{1,0:T(8,128)} %copy-done.25) | copy-start | bytes 1572868
  59.7 62.8 %copy-start.37 = (f32[128,512]{1,0:T(8,128)S(1)}, f32[128,512]{1,0:T(8,128)}, u32[]{:S(2)}) copy-start(f32[128,512]{1,0:T(8,128)} %copy-done.36) | copy-start | bytes 786436
  122.5 1.0 copy-start.16
  123.5 0.8 copy-start.19
  131.3 0.8 copy-start.23
  173.6 1.6 copy-start
  180.3 19.6 %copy-start.6 = (f32[1024,128]{1,0:T(8,128)S(1)}, f32[1024,128]{1,0:T(8,128)}, u32[]{:S(2)}) copy-start(f32[1024,128]{1,0:T(8,128)} %copy-done.5) | copy-start | bytes 1572868
  180.3 19.7 %copy-start.13 = (bf16[128,1024]{1,0:T(8,128)(2,1)S(1)}, bf16[128,1024]{1,0:T(8,128)(2,1)}, u32[]{:S(2)}) copy-start(bf16[128,1024]{1,0:T(8,128)(2,1)} %copy-done.11) | copy-start | bytes 786436
  180.3 19.7 %copy-start.20 = (f32[128,128]{1,0:T(8,128)S(1)}, f32[128,128]{1,0:T(8,128)}, u32[]{:S(2)}) copy-start(f32[128,128]{1,0:T(8,128)} %copy-done.17) | copy-start | bytes 196612
  180.3 19.7 %copy-start.31 = (bf16[144,1024]{1,0:T(8,128)(2,1)S(1)}, bf16[144,1024]{1,0:T(8,128)(2,1)}, u32[]{:S(2)}) copy-start(bf16[144,1024]{1,0:T(8,128)(2,1)} %copy-done.30) | copy-start | bytes 884740
  180.3 19.7 %copy-start.33 = (f32[128,512]{1,0:T(8,128)S(1)}, f32[128,512]{1,0:T(8,128)}, u32[]{:S(2)}) copy-start(f32[128,512]{1,0:T(8,128)} %copy-done.32) | copy-start | bytes 786436
  180.3 19.7 %copy-start.39 = (bf16[32,1024]{1,0:T(8,128)(2,1)S(1)}, bf16[32,1024]{1,0:T(8,128)(2,1)}, u32[]{:S(2)}) copy-start(bf16[32,1024]{1,0:T(8,128)(2,1)} %w_dt.3) | copy-start | bytes 196612
  180.3 19.7 %copy-start.45 = (f32[128,128]{1,0:T(8,128)S(1)}, f32[128,128]{1,0:T(8,128)}, u32[]{:S(2)}) copy-start(f32[128,128]{1,0:T(8,128)} %copy-done.44) | copy-start | bytes 196612
  180.3 19.7 %copy-start.47 = (f32[4,1024]{1,0:T(4,128)S(1)}, f32[4,1024]{1,0:T(4,128)}, u32[]{:S(2)}) copy-start(f32[4,1024]{1,0:T(4,128)} %conv_w.3) | copy-start | bytes 49156
  180.3 19.7 %copy-start.52 = (f32[1024]{0:T(1024)S(1)}, f32[1024]{0:T(1024)}, u32[]{:S(2)}) copy-start(f32[1024]{0:T(1024)} %param.23) | copy-start | bytes 12292
  180.3 19.7 %copy-start.54 = (f32[1024]{0:T(1024)S(1)}, f32[1024]{0:T(1024)}, u32[]{:S(2)}) copy-start(f32[1024]{0:T(1024)} %param.28) | copy-start | bytes 12292
  180.3 19.7 %copy-start.58 = (f32[512]{0:T(512)S(1)}, f32[512]{0:T(512)}, u32[]{:S(2)}) copy-start(f32[512]{0:T(512)} %param.20) | copy-start | bytes 6148
  180.4 19.7 %copy-start.61 = (f32[1,512]{1,0:T(1,128)S(1)}, f32[1,512]{1,0:T(1,128)}, u32[]{:S(2)}) copy-start(f32[1,512]{1,0:T(1,128)} %copy-done.60) | copy-start | bytes 6148
  200.0 1.0 copy-start.22
  201.1 1.0 copy-start.24
  202.1 0.9 copy-start.35
  204.5 43.1 %copy-start.1 = (bf16[1024,1024]{1,0:T(8,128)(2,1)S(1)}, bf16[1024,1024]{1,0:T(8,128)(2,1)}, u32[]{:S(2)}) copy-start(bf16[1024,1024]{1,0:T(8,128)(2,1)} %all-gather.5.cloned.1.call-done.nc) | copy-start | bytes 6291460
  224.1 24.1 %copy-start.64 = (f32[8,512]{1,0:T(8,128)}, f32[8,512]{1,0:T(8,128)S(1)}, u32[]{:S(2)}) copy-start(f32[8,512]{1,0:T(8,128)S(1)} %get-tuple-element.78) | copy-start | bytes 49156
  258.6 5.6 %copy-start.65 = (f32[8,512]{1,0:T(8,128)S(1)}, f32[8,512]{1,0:T(8,128)}, u32[]{:S(2)}) copy-start(f32[8,512]{1,0:T(8,128)} %copy-done.64) | copy-start | bytes 49156
  259.8 36.3 %all-to-all-start.6 = ((bf16[32,160,128]{2,1,0:T(8,128)(2,1)}), bf16[32,160,128]{2,1,0:T(8,128)(2,1)S(1)}, u32[]{:S(2)}, u32[]{:S(2)}) async-start(bf16[32,160,128]{2,1,0:T(8,128)(2,1)} %broadcast_in_dim.2), calls=%async_computation.6 | async-start | bytes 2621440 | tf_op jit(solution)/shard_map/all_to_all | solution.py:532
  264.2 30.6 %collective-permute-start.1 = (f32[8,512]{1,0:T(8,128)S(1)}, f32[8,512]{1,0:T(8,128)S(1)}, u32[]{:S(2)}, u32[]{:S(2)}) collective-permute-start(f32[8,512]{1,0:T(8,128)S(1)} %copy-done.65), channel_id=1, source_target_pairs={{1,0},{2,1},{3,2},{4,3},{5,4},{6,5},{7,6},{9,8},{10,9},{11,10},{12... | collective-permute-start | bytes 49160 | tf_op jit(solution)/shard_map/ppermute | solution.py:633
  302.0 3.3 copy-start.67
  317.5 1.8 slice-start
  320.5 3.6 %copy-start.66 = (bf16[8,4,128,128]{3,2,0,1:T(8,128)(2,1)S(1)}, bf16[8,4,128,128]{3,2,0,1:T(8,128)(2,1)}, u32[]{:S(2)}) copy-start(bf16[8,4,128,128]{3,2,0,1:T(8,128)(2,1)} %get-tuple-element.118) | copy-start | bytes 3145732
  324.2 1.5 copy-start.68
  (28 other events, 19.3 us)
Sparse Core Ops, SparseCore 0:
  31.4 59.0 all-gather.4
  92.6 80.9 all-gather.6
  200.0 69.1 all-gather.8
where the time goes:
time: 346 us; the launch traced here: 341 us
  blocking collectives  154 us (45%)
  local copies, waits for them, and re-layouts  72.4 us (21%)
  Pallas kernels  46.6 us (13%)
  waiting for transfers between devices  30.3 us (9%)
  between operations  14.3 us (4%)
  other arithmetic  14 us (4%)
  starting transfers between devices  9.75 us (3%)
    all_to_all x7, blocking collectives, exchange(): return lax.all_to_all(value, axes, 0, 0, tiled=True)  154 us
    unnamed x142, local copies, waits for them, and re-layouts  47.1 us
    pallas_call x7, Pallas kernels, call(): pl.pallas_call(kernel, out_shape=[jax.ShapeDtypeStruct(s, d) for s, d in...  46.6 us
    ppermute x1, waiting for transfers between devices, body(): lax.ppermute(grad_halo, 'seq', [(i + 1, i) for i in range(seq_size - 1)])  28.4 us
  transfers between devices with their start and end apart: 6, of which 3 were waited for; matrix products, arithmetic and copies ran while one was open for 3% of the time, Pallas kernels for 11%

commit v1 on v0

--- a/solution.py
+++ b/solution.py
@@ -2,6 +2,7 @@
 
 import jax
 import jax.numpy as jnp
+import numpy as np
 from jax import lax
 from jax.experimental import pallas as pl
 from jax.experimental.pallas import tpu as pltpu
@@ -18,7 +19,6 @@
 LN2 = 0.6931471805599453
 BF = jnp.bfloat16
 F32 = jnp.float32
-VMEM_LIMIT = 48 * 1024 * 1024
 
 
 def dot(a, b):
@@ -84,39 +84,48 @@
 
 
 def forward_kernel(
-    seq_size, tok, halo, cot, n1, w_in, conv_w, conv_b, w_xp, w_dt, dtb, a_log, seg,
-    o_msg, o_nc, o_inner, o_gate, o_mixed, o_bc, o_low, o_pre, o_s, o_dx, o_a,
+    seq_size, tok, halo, n1, w_in, conv_w, conv_b, w_xp, w_dt, dtb, a_log, seg,
+    o_msg, o_normed, o_inner, o_gate, o_mixed, o_bc, o_low, o_pre, o_s, o_dx, o_a,
     ext, smem, sem,
 ):
-    count, width = tok.shape
+    tok, halo, n1, seg = ready(tok, halo, n1, seg)
+    count = tok.shape[0]
     states = a_log.shape[0]
     inner_width = conv_w.shape[1]
     tiles = inner_width // LANES
     rank = w_dt.shape[0]
     x = jnp.concatenate([halo[...], tok[...]], axis=0).astype(F32)
     normed = (x * rms_parts(x) * n1[...]).astype(BF)
-    o_nc[:, :width] = normed[HALO:]
-    o_nc[:, width:] = cot[...]
+    o_normed[...] = normed[HALO:]
+    sent(o_normed)
+    w_in = ready(w_in)
     inner = dot(normed, w_in[:, :inner_width]).astype(BF)
     o_inner[...] = inner
+    sent(o_inner)
     ext[...] = inner.astype(F32)
     o_gate[...] = dot(normed[HALO:], w_in[:, inner_width:]).astype(BF)
+    sent(o_gate)
+    conv_w, conv_b, w_xp, w_dt, dtb, a_log = ready(conv_w, conv_b, w_xp, w_dt, dtb, a_log)
     offset = offsets_in_sequence(seg, seq_size)
     for j in range(tiles):
         pre = conv_tile(ext, conv_w, conv_b, offset, j, count)
         o_mixed[:, tile(j)] = (pre * jax.nn.sigmoid(pre)).astype(BF)
-    selector = dot(o_mixed[...], w_xp[...])
+    sent(o_mixed)
+    selector = dot_nt(o_mixed[...], w_xp[...])
     low = selector[:, :rank].astype(BF)
     o_low[...] = low
     o_bc[...] = selector[:, rank:]
-    copy = pltpu.make_async_copy(o_bc, smem, sem)
+    sent(o_low, o_bc)
+    copy = pltpu.make_async_copy(o_bc.ref, smem, sem)
     copy.start()
     o_pre[...] = dot(low, w_dt[...]) + dtb[...]
+    sent(o_pre)
     for j in range(tiles):
         step = softplus(o_pre[:, tile(j)])
         to_rows(o_s, j, jnp.where(offset == 0.0, RESET, step))
         to_rows(o_dx, j, step * o_mixed[:, tile(j)].astype(F32))
         to_rows(o_a, j, -LOG2E * jnp.exp(a_log[:, tile(j)]))
+    sent(o_s, o_dx, o_a)
     copy.wait()
 
     def one(t, carry):
@@ -151,16 +160,12 @@
 
 
 def middle_kernel(
-    msg, s_ref, dx_ref, bc, a_ref, mixed, gate, d_skip, tok, w_out, n2, w_qkv, cot, w_proj,
-    o_qkvg, o_start, o_ssm, o_gn, o_after,
-    y_ref, smem, sem,
+    msg, a_ref, bc, s_ref, dx_ref, mixed, gate, d_skip, tok, w_out, n2, w_qkv, cot, w_proj, normed_one,
+    o_qkvg, o_start, o_ssm, o_normed, o_after,
+    gated, y_ref,
 ):
-    count, inner_width = mixed.shape
-    width = tok.shape[1]
-    tiles = inner_width // LANES
+    msg, a_ref = ready(msg, a_ref)
     states = a_ref.shape[0] // 8
-    copy = pltpu.make_async_copy(bc, smem, sem)
-    copy.start()
     zero = jnp.zeros((8, LANES), F32)
 
     def join(d, carry):
@@ -173,7 +178,9 @@
     start = lax.fori_loop(0, lax.axis_index("seq"), join, (zero,) * states)
     for n in range(states):
         o_start[8 * n : 8 * n + 8, :] = start[n]
-    copy.wait()
+    sent(o_start)
+    s_ref, dx_ref, smem = ready(s_ref, dx_ref, bc)
+    count = smem.shape[0]
 
     def one(t, state):
         s, dx = block(s_ref, t), block(dx_ref, t)
@@ -187,15 +194,26 @@
         return state
 
     lax.fori_loop(0, count, one, start, unroll=4)
+    mixed, gate, d_skip, tok, w_out, n2 = ready(mixed, gate, d_skip, tok, w_out, n2)
+    inner_width, width = mixed.shape[1], tok.shape[1]
+    tiles = inner_width // LANES
     for j in range(tiles):
         ssm = from_rows(y_ref, j, count) + d_skip[:, tile(j)] * mixed[:, tile(j)].astype(F32)
         o_ssm[:, tile(j)] = ssm
         v = gate[:, tile(j)].astype(F32)
-        o_gn[:, tile(j)] = (ssm * (v * jax.nn.sigmoid(v))).astype(BF)
-    after = tok[...].astype(F32) + dot(o_gn[:, :inner_width], w_out[...])
+        gated[:, tile(j)] = (ssm * (v * jax.nn.sigmoid(v))).astype(BF)
+    sent(o_ssm)
+    piece = inner_width // o_qkvg.shape[0]
+    for d in range(o_qkvg.shape[0]):
+        o_qkvg[d, :, 2 * LANES : 2 * LANES + piece] = gated[:, d * piece : (d + 1) * piece]
+    after = tok[...].astype(F32) + dot(gated[...], w_out[...])
     o_after[...] = after
+    sent(o_after)
     normed = (after * rms_parts(after) * n2[...]).astype(BF)
-    o_gn[:, inner_width:] = normed
+    normed_one, w_qkv, cot, w_proj = ready(normed_one, w_qkv, cot, w_proj)
+    o_normed[:, :width] = normed_one[...]
+    o_normed[:, width:] = normed
+    sent(o_normed)
     qkv = dot(normed, w_qkv[...])
     gatt = dot_nt(cot[...], w_proj[...])
     copies = o_qkvg.shape[0] // H
@@ -212,14 +230,14 @@
                     o_qkvg[h * copies + r, :, tile(i)] = value
 
 
-def attention_kernel(qkvg, msg, o_back, qz, kr, gz, vr, dk, dv):
+def attention_kernel(qkvg, ends, o_back, qz, kr, gz, vr, dk, dv):
+    qkvg, ends = ready(qkvg, ends)
     seq_size, count = qkvg.shape[0], qkvg.shape[1]
     rows = seq_size * count
-    starts_at = msg.shape[1] - 16
     left = lax.broadcasted_iota(jnp.int32, (count, LANES), 1) < HD
     for d in range(seq_size):
         at = slice(d * count, (d + 1) * count)
-        a, b = qkvg[d, :, :LANES].astype(F32), qkvg[d, :, LANES:].astype(F32)
+        a, b = qkvg[d, :, :LANES].astype(F32), qkvg[d, :, LANES : 2 * LANES].astype(F32)
         qz[at, :] = jnp.where(left, a, 0.0).astype(BF)
         kr[at, :] = pltpu.roll(a, HD, 1).astype(BF)
         gz[at, :] = jnp.where(left, 0.0, b).astype(BF)
@@ -230,7 +248,7 @@
 
     def queries(b, length):
         at = pl.ds(b * count if isinstance(b, int) else pl.multiple_of(b * count, count), count)
-        tail = msg[b, starts_at : starts_at + 16, :].astype(F32)
+        tail = ends[b].astype(F32)
         starts = jnp.broadcast_to(tail[0:1] * 64.0 + tail[1:2], (LANES, LANES))
         first = jnp.transpose(starts)[:, :1].astype(jnp.int32)
         column = lax.broadcasted_iota(jnp.int32, (count, length), 1)
@@ -262,18 +280,13 @@
 
 
 def backward_kernel(
-    back, after, cot, w_proj, w_qkv, n2, w_out, gate, ssm, s_ref, bc, a_ref,
-    o_out, o_after, o_n2, o_gate, o_g, o_msg,
-    turned, smem, sem,
+    back, after, w_proj, w_qkv, n2, cot, w_out, gate, ssm, s_ref, a_ref, bc,
+    o_out, o_after, o_branch, o_n2, o_gate, o_g, o_msg,
+    turned,
 ):
+    back = ready(back)
     seq_size, count = back.shape[0], back.shape[1]
-    width = after.shape[1]
-    inner_width = gate.shape[1]
-    tiles = inner_width // LANES
-    states = a_ref.shape[0] // 8
     copies = seq_size // H
-    copy = pltpu.make_async_copy(bc, smem, sem)
-    copy.start()
     left = lax.broadcasted_iota(jnp.int32, (count, LANES), 1) < HD
     dq, dk, dv, att = [], [], [], []
     for p in range(H // 2):
@@ -284,16 +297,26 @@
         dv.append(jnp.where(left, b0, pltpu.roll(b1, HD, 1)))
         att.append(jnp.where(left, pltpu.roll(b0, HD, 1), b1))
     attended = jnp.concatenate(att, axis=1).astype(BF)
+    after, w_proj = ready(after, w_proj)
+    width = after.shape[1]
     o_out[...] = (after[...] + dot(attended, w_proj[...])).astype(BF)
+    sent(o_out)
+    w_qkv, n2, cot = ready(w_qkv, n2, cot)
     grad_qkv = jnp.concatenate(dq + dk + dv, axis=1).astype(BF)
     grad_x, grad_gain = rms_back(after[...], n2[...], dot_nt(grad_qkv, w_qkv[...]))
     o_n2[...] = jnp.sum(grad_gain, axis=0, keepdims=True)
     grad_after = cot[...].astype(F32) + grad_x
     o_after[...] = grad_after
     branch = grad_after.astype(BF)
+    o_branch[...] = branch
+    sent(o_n2, o_after, o_branch)
+    w_out, gate, ssm = ready(w_out, gate, ssm)
+    inner_width = gate.shape[1]
+    tiles = inner_width // LANES
+    a_ref = ready(a_ref)
+    states = a_ref.shape[0] // 8
     grad_gated = dot_nt(branch, w_out[...])
     gate_rows = inner_width // seq_size
-    branch_rows = width // seq_size
     for j in range(tiles):
         v = gate[:, tile(j)].astype(F32)
         sig = jax.nn.sigmoid(v)
@@ -303,12 +326,9 @@
         o_gate[:, tile(j)] = grad_gate.astype(BF)
         turned[tile(j), :] = jnp.transpose(grad_gate).astype(BF)
     for d in range(seq_size):
-        o_msg[d, states * 8 : states * 8 + gate_rows, :] = turned[d * gate_rows : (d + 1) * gate_rows, :]
-    for j in range(width // LANES):
-        turned[tile(j), :] = jnp.transpose(grad_after[:, tile(j)]).astype(BF)
-    for d in range(seq_size):
-        o_msg[d, states * 8 + gate_rows :, :] = turned[d * branch_rows : (d + 1) * branch_rows, :]
-    copy.wait()
+        o_msg[d, states * 8 :, :] = turned[d * gate_rows : (d + 1) * gate_rows, :]
+    sent(o_gate, o_g)
+    s_ref, smem = ready(s_ref, bc)
 
     def one(i, later):
         t = count - 1 - i
@@ -323,6 +343,34 @@
         value = jnp.concatenate([leaving[n], leaving[n + 1]], axis=0).astype(BF)
         for d in range(seq_size):
             o_msg[d, 8 * n : 8 * n + 16, :] = value
+
+
+def states_kernel(
+    seq_size, start, a_ref, bc, s_ref, dx_ref, inner, conv_w, conv_b, seg, o_every, o_slope, ext
+):
+    start, a_ref, smem, s_ref, dx_ref = ready(start, a_ref, bc, s_ref, dx_ref)
+    count = smem.shape[0]
+    states = a_ref.shape[0] // 8
+    o_every[: states * 8, :] = start[...]
+
+    def again(t, state):
+        s, dx = block(s_ref, t), block(dx_ref, t)
+        state = tuple(
+            jnp.exp2(s * block(a_ref, n)) * state[n] + dx * smem[t, n] for n in range(states)
+        )
+        for n in range(states):
+            o_every[pl.ds(pl.multiple_of(((t + 1) * states + n) * 8, 8), 8), :] = state[n]
+        return state
+
+    lax.fori_loop(0, count, again, tuple(start[8 * n : 8 * n + 8, :] for n in range(states)), unroll=2)
+    sent(o_every)
+    inner, conv_w, conv_b, seg = ready(inner, conv_w, conv_b, seg)
+    ext[...] = inner[...].astype(F32)
+    offset = offsets_in_sequence(seg, seq_size)
+    for j in range(o_slope.shape[1] // LANES):
+        pre = conv_tile(ext, conv_w, conv_b, offset, j, count)
+        sig = jax.nn.sigmoid(pre)
+        o_slope[:, tile(j)] = sig * (1.0 + pre * (1.0 - sig))
 
 
 def fold8(values, sub):
@@ -340,49 +388,39 @@
 
 
 def adjoint_kernel(
-    seq_size, back, msg, start, s_ref, dx_ref, g_ref, bc, a_ref, mixed, low, step_pre, inner, conv_w, conv_b, seg,
-    w_dt, w_xp, d_skip, grad_gate, w_in, tok, halo, n1, grad_after, grad_n2,
-    o_msg, o_tok, o_halo,
-    held, gs_ref, ai_ref, sums, small, ext, gext, smem, sem,
+    seq_size, back, totals, a_ref, bc, s_ref, dx_ref, g_ref, mixed, step_pre, low, w_dt, w_xp, inner, slope, conv_w, d_skip,
+    seg, grad_n2, every,
+    o_msg, o_inner,
+    held, gs_ref, ai_ref, sums, small, ext, gext, arrived,
 ):
-    count, inner_width = mixed.shape
-    width = tok.shape[1]
-    tiles = inner_width // LANES
+    back, totals, a_ref = ready(back, totals, a_ref)
     states = a_ref.shape[0] // 8
-    rank = w_dt.shape[0]
-    taps = conv_w.shape[0]
-    copy = pltpu.make_async_copy(bc, smem, sem)
-    copy.start()
+    count = s_ref.shape[0] // 8
     zero = jnp.zeros((8, LANES), F32)
-    for n in range(states):
-        held[8 * n : 8 * n + 8, :] = start[8 * n : 8 * n + 8, :]
-    copy.wait()
-
-    def again(t, state):
-        s, dx = block(s_ref, t), block(dx_ref, t)
-        state = tuple(
-            jnp.exp2(s * block(a_ref, n)) * state[n] + dx * smem[t, n] for n in range(states)
-        )
-        for n in range(states):
-            held[pl.ds(pl.multiple_of(((t + 1) * states + n) * 8, 8), 8), :] = state[n]
-        return state
-
-    lax.fori_loop(0, count, again, tuple(start[8 * n : 8 * n + 8, :] for n in range(states)), unroll=2)
+    chunks = arrived.shape[0]
+    span = count // chunks
+    loads = []
+    for c in range(chunks):
+        first, last = c * span * states * 8, ((c + 1) * span + (c == chunks - 1)) * states * 8
+        loads.append(pltpu.make_async_copy(every.at[first:last], held.at[first:last], arrived.at[c]))
+    for load in reversed(loads):
+        load.start()
 
     def join(i, carry):
         d = seq_size - 1 - i
-        total = total_step(msg, d, states)
+        total = total_step(totals, d, 0)
         return tuple(
             jnp.exp2(block(a_ref, n) * total) * carry[n] + state_rows(back, d, n)
             for n in range(states)
         )
 
     leaving = lax.fori_loop(0, seq_size - 1 - lax.axis_index("seq"), join, (zero,) * states)
+    smem, s_ref, dx_ref, g_ref = ready(bc, s_ref, dx_ref, g_ref)
     sub = lax.broadcasted_iota(jnp.int32, (8, LANES), 0)
 
-    def one(i, carry):
+    def one(last, i, carry):
         later, grad_a = carry
-        t = count - 1 - i
+        t = last - i
         s, dx, g = block(s_ref, t), block(dx_ref, t), block(g_ref, t)
         new_later, new_grad_a, with_b, with_c = [], [], [], []
         grad_step, adjoint_in = zero, zero
@@ -406,7 +444,17 @@
             sums[pl.ds(pl.multiple_of(t * 32 + 8 * i, 8), 8), :] = fold8(part, sub)
         return tuple(new_later), tuple(new_grad_a)
 
-    _, grad_a = lax.fori_loop(0, count, one, (leaving, (zero,) * states))
+    carry = (leaving, (zero,) * states)
+    for c in reversed(range(chunks)):
+        loads[c].wait()
+        carry = lax.fori_loop(0, span, functools.partial(one, (c + 1) * span - 1), carry)
+    grad_a = carry[1]
+    mixed, step_pre, low, w_dt, w_xp, inner = ready(mixed, step_pre, low, w_dt, w_xp, inner)
+    slope, conv_w, d_skip, seg, grad_n2 = ready(slope, conv_w, d_skip, seg, grad_n2)
+    inner_width = mixed.shape[1]
+    tiles = inner_width // LANES
+    rank = w_dt.shape[0]
+    taps = conv_w.shape[0]
     small[...] = jnp.zeros_like(small)
     for n in range(states):
         small[(104 + n) * 8 : (105 + n) * 8, :] = grad_a[n] * (LN2 * block(a_ref, n))
@@ -431,20 +479,18 @@
     padded_dt = jnp.concatenate([w_dt[...], jnp.zeros((2 * states, inner_width), BF)], axis=0)
     grad_selector = (dot_nt(half, padded_dt) + grad_bc).astype(BF)
     grad_w_xp = dot_tn(grad_selector, mixed[...])
-    from_selector = dot_nt(grad_selector, w_xp[...])
+    from_selector = dot(grad_selector, w_xp[...])
     ext[...] = inner[...].astype(F32)
     gext[...] = jnp.zeros_like(gext)
     for j in range(tiles):
         to_rows(small.at[pl.ds(0, 64 * 8)], j, grad_w_xp[:, tile(j)])
         to_rows(small.at[pl.ds(64 * 8, 32 * 8)], j, grad_w_dt[:, tile(j)])
-        pre = conv_tile(ext, conv_w, conv_b, offset, j, count)
-        sig = jax.nn.sigmoid(pre)
         grad_mixed = (
             softplus(step_pre[:, tile(j)]) * from_rows(ai_ref, j, count)
             + from_rows(g_ref, j, count) * d_skip[:, tile(j)]
             + from_selector[:, tile(j)]
         )
-        grad_pre = grad_mixed * (sig * (1.0 + pre * (1.0 - sig)))
+        grad_pre = grad_mixed * slope[:, tile(j)]
         small[100 * 8 + j : 100 * 8 + j + 1, :] = jnp.sum(grad_pre, axis=0, keepdims=True)
         for k in range(taps):
             shifted = pl.ds(HALO - taps + 1 + k, count)
@@ -454,7 +500,8 @@
             gext[shifted, tile(j)] += conv_w[k : k + 1, tile(j)] * usable
     piece = inner_width // seq_size
     per = small.shape[0] // seq_size
-    grad_inner = gext[...].astype(BF)
+    o_inner[...] = gext[...].astype(BF)
+    sent(o_inner)
     for j in range(tiles):
         value = jnp.transpose(gext[HALO:, tile(j)]).astype(BF)
         for i in range(LANES // piece):
@@ -464,68 +511,275 @@
         if piece < LANES:
             rows = jnp.concatenate([rows, jnp.zeros((HALO, LANES - piece), F32)], axis=1)
         o_msg[d, piece : piece + HALO, :] = rows.astype(BF)
-    grad_normed = dot_nt(grad_inner, w_in[:, :inner_width])
+    width = grad_n2.shape[1]
+    for j in range(width // LANES):
+        small[103 * 8 + 4 + j : 103 * 8 + 5 + j, :] = grad_n2[:, tile(j)]
+    for d in range(seq_size):
+        o_msg[d, piece + HALO :, :] = small[d * per : (d + 1) * per, :].astype(BF)
+
+
+def tokens_kernel(grad_inner, w_in, grad_gate, tok, halo, n1, grad_after, o_tok, o_halo, o_n1):
+    grad_inner, w_in, grad_gate = ready(grad_inner, w_in, grad_gate)
+    inner_width = grad_inner.shape[1]
+    grad_normed = dot_nt(grad_inner[...], w_in[:, :inner_width])
     own = dot_nt(grad_gate[...], w_in[:, inner_width:])
     grad_normed = jnp.concatenate([grad_normed[:HALO], grad_normed[HALO:] + own], axis=0)
+    tok, halo, n1, grad_after = ready(tok, halo, n1, grad_after)
     x = jnp.concatenate([halo[...], tok[...]], axis=0).astype(F32)
     grad_x, grad_gain = rms_back(x, n1[...], grad_normed)
     o_tok[...] = grad_after[...] + grad_x[HALO:]
     o_halo[...] = grad_x[HALO - 8 : HALO]
     grad_gain = jnp.sum(grad_gain, axis=0, keepdims=True)
-    for j in range(width // LANES):
-        small[103 * 8 + j : 103 * 8 + j + 1, :] = grad_gain[:, tile(j)]
-        small[103 * 8 + 4 + j : 103 * 8 + 5 + j, :] = grad_n2[:, tile(j)]
+    tiles = grad_gain.shape[1] // LANES
+    rows = [grad_gain[:, tile(j)] for j in range(tiles)] + [jnp.zeros((16 - tiles, LANES), F32)]
+    o_n1[...] = jnp.concatenate(rows, axis=0).astype(BF)
+
+
+def head_products_kernel(width, back, cot, normed, *outs):
+    back, cot, normed = ready(back, cot, normed)
+    seq_size, count = back.shape[0], back.shape[1]
+    both = back[...].reshape(seq_size * count, 2 * LANES)
+    proj = dot_tn(both[:, LANES:], cot[...])[HD:]
+    if len(outs) == 1:
+        first = dot_tn(normed[:, width:], both[:, :LANES])
+        second = dot_tn(normed[:, width:], both[:, LANES:])
+        left = lax.broadcasted_iota(jnp.int32, (HD, LANES), 1) < HD
+        for g in range(width // LANES):
+            outs[0][g, :HD, :] = proj[:, tile(g)].astype(BF)
+            outs[0][g, HD : 3 * HD, :] = first[tile(g)].astype(BF)
+            low, high = second[g * LANES : g * LANES + HD], second[g * LANES + HD : (g + 1) * LANES]
+            outs[0][g, 3 * HD :, :] = jnp.where(left, low, pltpu.roll(high, HD, 1)).astype(BF)
+    else:
+        outs[0][...] = proj.astype(BF)
+        outs[1][: 2 * HD, :] = dot_tn(both[:, :LANES], normed[:, width:]).astype(BF)
+        outs[1][2 * HD :, :] = dot_tn(both[:, LANES:], normed[:, width:])[:HD].astype(BF)
+
+
+def gate_products_kernel(piece, normed, adj, *rest):
+    normed, adj = ready(normed, adj)
+    seq_size = adj.shape[0]
+    count = normed.shape[0] // seq_size
+    width = normed.shape[1]
+    gate = jnp.zeros((piece, width), F32)
     for d in range(seq_size):
-        o_msg[d, piece + HALO :, :] = small[d * per : (d + 1) * per, :].astype(BF)
-
-
-def early_products_kernel(width, back, nc, gn, adj, o_head, o_gate, o_out):
-    seq_size, count = back.shape[0], back.shape[1]
-    rows = seq_size * count
-    inner_width = gn.shape[1] - width
-    gate_rows, branch_rows = o_gate.shape[0], o_out.shape[0]
-    at = adj.shape[1] - gate_rows - branch_rows
-    both = back[...].reshape(rows, 2 * LANES)
-    first = dot_tn(both[:, :LANES], gn[:, inner_width:])
-    second = dot_tn(both[:, LANES:], gn[:, inner_width:])
-    third = dot_tn(both[:, LANES:], nc[:, width:])
-    o_head[:HD, :] = third[HD:].astype(BF)
-    o_head[HD : 3 * HD, :] = first.astype(BF)
-    o_head[3 * HD :, :] = second[:HD].astype(BF)
-    gate = jnp.zeros((gate_rows, width), F32)
-    out = jnp.zeros((branch_rows, inner_width), F32)
+        gate = gate + dot(adj[d], normed[d * count : (d + 1) * count, :])
+    if len(rest) == 2:
+        head, pieces = rest
+        head = ready(head)
+        own = head.shape[1]
+        for g in range(head.shape[0]):
+            pieces[g, :own, :] = head[g]
+            pieces[g, own:, :] = jnp.transpose(gate[:, tile(g)]).astype(BF)
+    else:
+        rest[0][...] = gate.astype(BF)
+
+
+def late_products_kernel(piece, gated, branch, normed, tail, *outs):
+    gated, branch = ready(gated, branch)
+    seq_size, count = gated.shape[0], gated.shape[1]
+    width = branch.shape[1]
+    out = jnp.zeros((piece, width), F32)
     for d in range(seq_size):
-        src = slice(d * count, (d + 1) * count)
-        gate = gate + dot(adj[d, at : at + gate_rows, :], nc[src, :width])
-        out = out + dot(adj[d, at + gate_rows :, :], gn[src, :inner_width])
-    o_gate[...] = gate.astype(BF)
-    o_out[...] = out.astype(BF)
-
-
-def late_products_kernel(width, tail, nc, o_in, o_small):
-    seq_size = tail.shape[0]
-    count = nc.shape[0] // seq_size
-    piece = o_in.shape[0]
+        out = out + dot_tn(gated[d, :, :piece], branch[d * count : (d + 1) * count, :])
+    normed, tail = ready(normed, tail)
     grad = jnp.zeros((piece, width), F32)
-    small = jnp.zeros(o_small.shape, F32)
+    small = jnp.zeros((tail.shape[1] - piece - HALO, LANES), F32)
     for d in range(seq_size):
-        grad = grad + dot(tail[d, :piece, :], nc[d * count : (d + 1) * count, :width])
+        grad = grad + dot(tail[d, :piece, :], normed[d * count : (d + 1) * count, :])
         small = small + tail[d, piece + HALO :, :].astype(F32)
         if d:
-            borrowed = dot_tn(tail[d, piece : piece + HALO, :], nc[d * count - HALO : d * count, :width])
+            borrowed = dot_tn(tail[d, piece : piece + HALO, :], normed[d * count - HALO : d * count, :])
             grad = grad + borrowed[:piece]
-    o_in[...] = grad.astype(BF)
-    o_small[...] = small.astype(BF)
-
-
-def call(kernel, outs, scratch, *args, name=None):
+    if len(outs) == 1:
+        groups = outs[0].shape[0]
+        rows = small.shape[0] // groups
+        for g in range(groups):
+            outs[0][g, :LANES, :] = jnp.transpose(grad[:, tile(g)]).astype(BF)
+            outs[0][g, LANES : 2 * LANES, :] = out[:, tile(g)].astype(BF)
+            outs[0][g, 2 * LANES :, :] = small[g * rows : (g + 1) * rows].astype(BF)
+    else:
+        outs[0][...] = grad.astype(BF)
+        outs[1][...] = out.astype(BF)
+        outs[2][...] = small.astype(BF)
+
+
+def sum_kernel(parts, o_sum):
+    parts = ready(parts)
+    total = parts[0].astype(F32)
+    for d in range(1, parts.shape[0]):
+        total = total + parts[d].astype(F32)
+    o_sum[...] = total.astype(BF)
+
+
+def sum_and_spread_kernel(parts, own, o_all):
+    parts, own = ready(parts, own)
+    total = parts[0].astype(F32)
+    for d in range(1, parts.shape[0]):
+        total = total + parts[d].astype(F32)
+    total = total.astype(BF)
+    rows = total.shape[0]
+    for d in range(o_all.shape[0]):
+        o_all[d, :rows, :] = total
+        o_all[d, rows:, :] = own[...]
+
+
+def early_assembly_kernel(groups, early, o_proj, o_qkv, o_in, gate, sem):
+    early = ready(early)
+    seq_size = early.shape[0] // groups
+    width = o_proj.shape[1]
+    inner_width = gate.shape[1]
+    left = lax.broadcasted_iota(jnp.int32, (LANES, LANES), 1) < HD
+
+    def pairs(a, b):
+        a, b = a.astype(F32), b.astype(F32)
+        mask = left[: a.shape[0]]
+        return jnp.where(mask, a, pltpu.roll(b, HD, 1)), jnp.where(mask, pltpu.roll(a, HD, 1), b)
+
+    for g in range(groups):
+        for s in range(seq_size):
+            gate[tile(g), tile(s)] = early[g * seq_size + s, 4 * HD :, :].astype(F32)
+    copy = pltpu.make_async_copy(gate, o_in.at[:, inner_width:], sem)
+    copy.start()
+    for g in range(groups):
+        rows = tile(g)
+        for s in range(seq_size):
+            o_proj[s * HD : (s + 1) * HD, tile(g)] = early[g * seq_size + s, :HD, :].astype(F32)
+        for p in range(seq_size // 2):
+            a, b = g * seq_size + 2 * p, g * seq_size + 2 * p + 1
+            q, k = pairs(early[a, HD : 3 * HD, :], early[b, HD : 3 * HD, :])
+            o_qkv[rows, p * LANES : (p + 1) * LANES] = q
+            o_qkv[rows, width + p * LANES : width + (p + 1) * LANES] = k
+            low, high = pairs(early[a, 3 * HD : 4 * HD, :], early[b, 3 * HD : 4 * HD, :])
+            o_qkv[g * LANES : g * LANES + HD, 2 * width + p * LANES : 2 * width + (p + 1) * LANES] = low
+            o_qkv[g * LANES + HD : (g + 1) * LANES, 2 * width + p * LANES : 2 * width + (p + 1) * LANES] = high
+    copy.wait()
+
+
+def late_assembly_kernel(
+    groups, mine, other, w_in, o_in, o_out, o_n1, o_conv_w, o_conv_b, o_xp, o_dt, o_dtb, o_a, o_skip, o_n2,
+    inner, small, sem,
+):
+    mine, other = ready(mine, other)
+    seq_size = mine.shape[0] * 2 // groups
+    core = lax.rem(lax.axis_index("dp"), 2)
+    width, inner_width = inner.shape
+    rows = mine.shape[1] - 2 * LANES - 16
+    for x in range(groups // 2):
+        for source, side in ((mine, core), (other, 1 - core)):
+            g = 2 * x + side
+            at = pl.ds(pl.multiple_of(g * LANES, LANES), LANES)
+            for s in range(seq_size):
+                inner[at, tile(s)] = source[x * seq_size + s, :LANES, :].astype(F32)
+                here = pl.ds(pl.multiple_of(s * LANES + g * rows, rows), rows)
+                small[here, :] = source[x * seq_size + s, 2 * LANES : 2 * LANES + rows, :].astype(F32)
+    copy = pltpu.make_async_copy(inner, o_in.at[:, :inner_width], sem)
+    copy.start()
+    for x in range(groups // 2):
+        for side in range(2):
+            for s in range(seq_size):
+                piece = [ref[x * seq_size + s, LANES : 2 * LANES, :] for ref in (mine, other)]
+                value = jnp.where(core == side, piece[0].astype(F32), piece[1].astype(F32))
+                o_out[tile(s), tile(2 * x + side)] = value
+    for j in range(inner_width // LANES):
+        value = from_rows(small, j, SMALL)
+        for ref, first, last in (
+            (o_xp, 0, 64), (o_dt, 64, 96), (o_conv_w, 96, 100), (o_conv_b, 100, 101), (o_dtb, 101, 102),
+            (o_skip, 102, 103), (o_a, 104, 120),
+        ):
+            ref[:, tile(j)] = value[first:last]
+        if j >= width // LANES:
+            o_n2[:, tile(j - width // LANES)] = value[103:104]
+    gain = jnp.zeros((16, LANES), F32)
+    for source in (mine, other):
+        for d in range(source.shape[0]):
+            gain = gain + source[d, 2 * LANES + rows :, :].astype(F32)
+    for j in range(width // LANES):
+        o_n1[:, tile(j)] = gain[j : j + 1]
+    copy.wait()
+
+
+class Held:
+    def __init__(self, buffer, copy):
+        self.ref, self.copy, self.shape = buffer, copy, buffer.shape
+        self.done = False
+
+    def __getitem__(self, at):
+        return self.ref[at]
+
+    def __setitem__(self, at, value):
+        self.ref[at] = value
+
+
+def ready(*held):
+    for one in held:
+        if not one.done:
+            one.copy.wait()
+            one.done = True
+    refs = tuple(one.ref for one in held)
+    return refs if len(refs) > 1 else refs[0]
+
+
+def sent(*held):
+    for one in held:
+        if not one.done:
+            one.copy.start()
+            one.done = True
+
+
+IN_HBM = pl.BlockSpec(memory_space=pltpu.HBM)
+
+
+def call(
+    kernel, outs, scratch, *args, name=None, us=1, raw=(), raw_out=(), scalars=(), views=None, aliases=None, after=(),
+    vmem=60,
+):
+    views = views or {}
+    count, first_out = len(args), len(args) + len(after)
+    first_scratch = first_out + len(outs)
+    buffers = []
+    for i, arg in enumerate(args):
+        shape = jax.eval_shape(lambda v, i=i: v[views[i]], arg).shape if i in views else arg.shape
+        kind = pltpu.SMEM if i in scalars else pltpu.VMEM
+        buffers.append(None if i in raw else kind(shape, arg.dtype))
+    for i, (shape, dtype) in enumerate(outs):
+        buffers.append(None if i in raw_out else pltpu.VMEM(shape, dtype))
+    used = [b for b in buffers if b is not None]
+
+    def run(*refs):
+        given = list(refs[:count]) + list(refs[first_out:first_scratch])
+        own = list(refs[first_scratch : first_scratch + len(used)])
+        sems = refs[first_scratch + len(used)]
+        passed = []
+        for i, (ref, buffer) in enumerate(zip(given, buffers)):
+            if buffer is None:
+                passed.append(ref)
+                continue
+            buffer = own.pop(0)
+            if i < count:
+                source = ref.at[views[i]] if i in views else ref
+                copy = pltpu.make_async_copy(source, buffer, sems.at[i])
+                copy.start()
+            else:
+                copy = pltpu.make_async_copy(buffer, ref, sems.at[i])
+            passed.append(Held(buffer, copy))
+        kernel(*passed, *refs[first_scratch + len(used) + 1 :])
+        ready(*[p for p in passed[:count] if isinstance(p, Held)])
+        results = [p for p in passed[count:] if isinstance(p, Held)]
+        sent(*results)
+        for result in results:
+            result.copy.wait()
+
     return pl.pallas_call(
-        kernel,
+        run,
         out_shape=[jax.ShapeDtypeStruct(s, d) for s, d in outs],
-        scratch_shapes=scratch,
-        compiler_params=pltpu.CompilerParams(vmem_limit_bytes=VMEM_LIMIT),
+        in_specs=[IN_HBM] * first_out,
+        out_specs=[IN_HBM] * len(outs),
+        scratch_shapes=used + [pltpu.SemaphoreType.DMA((len(buffers),))] + scratch,
+        compiler_params=pltpu.CompilerParams(vmem_limit_bytes=vmem * 1024 * 1024),
+        cost_estimate=pl.CostEstimate(flops=us * 1000, bytes_accessed=us * 1000, transcendentals=0),
+        input_output_aliases=aliases or {},
         name=name,
-    )(*args)
+    )(*args, *after)
 
 
 def exchange(value, axes):
@@ -536,6 +790,13 @@
     axes = ("dp", "seq")
     count = lax.axis_size(axes)
     return exchange(jnp.broadcast_to(value[None], (count,) + value.shape), axes)
+
+
+def own_core(value, groups, seq_size):
+    peers = [
+        [g * seq_size + s for g in range(core, groups, 2) for s in range(seq_size)] for core in range(2)
+    ]
+    return lax.all_to_all(value, ("dp", "seq"), 0, 0, tiled=True, axis_index_groups=peers)
 
 
 def body(
@@ -550,8 +811,8 @@
     rows = count * seq_size
     ext_rows = HALO + count
     piece = inner_width // seq_size
-    branch = width // seq_size
     copies = seq_size // H
+    tiled = piece == LANES and width == groups * LANES and copies == 1
     line = lambda v: v.reshape(1, -1)
     seg = line(seg_start)
     n1, n2, cb, dtb, skip = (line(v) for v in (norm_one, norm_two, conv_b, dt_bias, d_skip))
@@ -559,88 +820,151 @@
     sem = pltpu.SemaphoreType.DMA
     blocks = ((count * 8, LANES), F32)
     onward = [(i, i + 1) for i in range(seq_size - 1)]
+    cot_all = lax.all_gather(cotangent, "seq", axis=0, tiled=True)
+    ends_at = states * 8
     halo = lax.ppermute(tokens[count - HALO :], "seq", onward)
-    msg, nc, inner, gate, mixed, bc, low, step_pre, s, dx, a = call(
+    msg, normed, inner, gate, mixed, bc, low, step_pre, s, dx, a = call(
         functools.partial(forward_kernel, seq_size),
         [
-            ((seq_size, states * 8 + 32, LANES), BF), ((count, 2 * width), BF), ((ext_rows, inner_width), BF),
-            ((count, inner_width), BF), ((count, inner_width), BF), ((count, 2 * states), F32), ((count, rank), BF),
+            ((seq_size, states * 8 + 32, LANES), BF), ((count, width), BF),
+            ((ext_rows, inner_width), BF), ((count, inner_width), BF), ((count, inner_width), BF), ((count, 2 * states), F32), ((count, rank), BF),
             ((count, inner_width), F32), blocks, blocks, ((states * 8, LANES), F32),
         ],
         [vmem((ext_rows, inner_width), F32), smem, sem],
-        tokens, halo, cotangent, n1, w_in, conv_w, cb, w_xproj, w_dt, dtb, a_log.T, seg,
-        name="forward",
+        tokens, halo, n1, w_in, conv_w, cb, w_xproj.T, w_dt, dtb, a_log.T, seg,
+        name="forward", us=8,
     )
-    nc_all = lax.all_gather(nc, "seq", axis=0, tiled=True)
     msg = exchange(msg, "seq")
-    qkvg, start, ssm, gn, after = call(
+    qkvg, start, ssm, normed, after = call(
         middle_kernel,
         [
-            ((seq_size, count, 2 * LANES), BF), ((states * 8, LANES), F32), ((count, inner_width), F32),
-            ((count, inner_width + width), BF), ((count, width), F32),
+            ((seq_size, count, 3 * LANES), BF), ((states * 8, LANES), F32), ((count, inner_width), F32),
+            ((count, 2 * width), BF), ((count, width), F32),
         ],
-        [vmem(*blocks), smem, sem],
-        msg, s, dx, bc, a, mixed, gate, skip, tokens, w_out, n2, w_qkv, cotangent, w_proj,
-        name="middle",
+        [vmem((count, inner_width), BF), vmem(*blocks)],
+        msg, a, bc, s, dx, mixed, gate, skip, tokens, w_out, n2, w_qkv, cotangent, w_proj, normed,
+        name="middle", us=8, scalars=(2,), views={0: np.s_[:, : ends_at + 16, :]},
     )
-    gn_all = lax.all_gather(gn, "seq", axis=0, tiled=True)
+    normed_all = lax.all_gather(normed, "seq", axis=0, tiled=True)
     qkvg = exchange(qkvg, "seq")
     (back,) = call(
         attention_kernel,
         [((seq_size, count, 2 * LANES), BF)],
         [vmem((rows, LANES), BF)] * 4 + [vmem((rows, LANES), F32)] * 2,
-        qkvg, msg, name="attention",
+        qkvg, msg, name="attention", us=7,
+        views={0: np.s_[:, :, : 2 * LANES], 1: np.s_[:, ends_at + 16 :, :]},
     )
     back_own = exchange(back, "seq")
-    out, grad_after, grad_n2, grad_gate, g, adj = call(
+    out, grad_after, branch, grad_n2, grad_gate, g, adj = call(
         backward_kernel,
         [
-            ((count, width), BF), ((count, width), F32), ((1, width), F32), ((count, inner_width), BF), blocks,
-            ((seq_size, states * 8 + piece + branch, LANES), BF),
+            ((count, width), BF), ((count, width), F32), ((count, width), BF), ((1, width), F32),
+            ((count, inner_width), BF), blocks, ((seq_size, states * 8 + piece, LANES), BF),
         ],
-        [vmem((inner_width, LANES), BF), smem, sem],
-        back_own, after, cotangent, w_proj, w_qkv, n2, w_out, gate, ssm, s, bc, a,
-        name="backward",
+        [vmem((inner_width, LANES), BF)],
+        back_own, after, w_proj, w_qkv, n2, cotangent, w_out, gate, ssm, s, a, bc,
+        name="backward", us=7, scalars=(11,),
     )
     adj = exchange(adj, "seq")
-    head, gate_part, out_part = call(
-        functools.partial(early_products_kernel, width),
-        [((4 * HD, width), BF), ((piece, width), BF), ((branch, inner_width), BF)],
-        [],
-        back, nc_all, gn_all, adj, name="early_products",
+    branch_all = lax.all_gather(branch, "seq", axis=0, tiled=True)
+    every, slope = call(
+        functools.partial(states_kernel, seq_size),
+        [(((count + 1) * states * 8, LANES), F32), ((count, inner_width), F32)],
+        [vmem((ext_rows, inner_width), F32)],
+        start, a, bc, s, dx, inner, conv_w, cb, seg, name="states", us=6, scalars=(2,),
     )
-    if copies > 1:
-        own = 4 * HD // copies
-        head = lax.dynamic_slice_in_dim(head, lax.axis_index("seq") % copies * own, own, 0)
-    early = jnp.concatenate([v.reshape(groups, -1, LANES) for v in (head, gate_part, out_part)], axis=1)
-    early = jnp.sum(exchange(early, "dp").astype(F32), axis=0).astype(BF)
-    early = lax.all_gather(early, ("dp", "seq"))
-    tail, grad_tokens, grad_halo = call(
+    gate_views = {0: np.s_[:, :width], 1: np.s_[:, ends_at:, :]}
+    if tiled:
+        (head,) = call(
+            functools.partial(head_products_kernel, width), [((groups, 4 * HD, LANES), BF)], [],
+            back, cot_all, normed_all, name="head_products", us=3,
+        )
+        (early,) = call(
+            functools.partial(gate_products_kernel, piece), [((groups, 4 * HD + LANES, LANES), BF)], [],
+            normed_all, adj, head, name="gate_products", us=2, after=(every,), views=gate_views,
+        )
+    else:
+        proj_part, qkv_part = call(
+            functools.partial(head_products_kernel, width), [((HD, width), BF), ((3 * HD, width), BF)], [],
+            back, cot_all, normed_all, name="head_products", us=3,
+        )
+        (gate_part,) = call(
+            functools.partial(gate_products_kernel, piece), [((piece, width), BF)], [],
+            normed_all, adj, name="gate_products", us=2, views=gate_views,
+        )
+        head = jnp.concatenate([proj_part, qkv_part], axis=0)
+        if copies > 1:
+            own = 4 * HD // copies
+            head = lax.dynamic_slice_in_dim(head, lax.axis_index("seq") % copies * own, own, 0)
+        early = jnp.concatenate([v.reshape(groups, -1, LANES) for v in (head, gate_part)], axis=1)
+    adjoint_in = (adj, msg, a, bc, s, dx, g, mixed, step_pre, low, w_dt, w_xproj.T, inner, slope, conv_w, skip, seg,
+                  grad_n2, every)
+    tail, grad_inner = call(
         functools.partial(adjoint_kernel, seq_size),
-        [
-            ((seq_size, piece + HALO + SMALL * 8 // seq_size, LANES), BF), ((count, width), F32), ((8, width), F32),
-        ],
+        [((seq_size, piece + HALO + SMALL * 8 // seq_size, LANES), BF), ((ext_rows, inner_width), BF)],
         [
             vmem(((count + 1) * states * 8, LANES), F32), vmem(*blocks), vmem(*blocks),
             vmem((count * 2 * states, LANES), F32), vmem((SMALL * 8, LANES), F32),
-            vmem((ext_rows, inner_width), F32), vmem((ext_rows, inner_width), F32), smem, sem,
+            vmem((ext_rows, inner_width), F32), vmem((ext_rows, inner_width), F32), sem((8,)),
         ],
-        adj, msg, start, s, dx, g, bc, a, mixed, low, step_pre, inner, conv_w, cb, seg,
-        w_dt, w_xproj, skip, grad_gate, w_in, tokens, halo, n1, grad_after, grad_n2,
-        name="adjoint",
+        *adjoint_in, name="adjoint", us=15, raw=(len(adjoint_in) - 1,), scalars=(3,),
+        views={0: np.s_[:, :ends_at, :], 1: np.s_[:, ends_at : ends_at + 16, :]},
     )
+    early = exchange(early, "dp")
+    (early,) = call(
+        sum_kernel, [(early.shape[1:], BF)], [], early, name="early_sum", us=1, after=(grad_inner,)
+    )
+    early = lax.all_gather(early, ("dp", "seq"))
     tail = exchange(tail, "seq")
+    grad_tokens, grad_halo, grad_n1 = call(
+        tokens_kernel, [((count, width), F32), ((8, width), F32), ((16, LANES), BF)], [],
+        grad_inner, w_in, grad_gate, tokens, halo, n1, grad_after, name="tokens", us=4,
+    )
     returned = lax.ppermute(grad_halo, "seq", [(i + 1, i) for i in range(seq_size - 1)])
     grad_tokens = grad_tokens.at[count - 8 :].add(returned)
-    in_part, small = call(
-        functools.partial(late_products_kernel, width),
-        [((piece, width), BF), ((SMALL * 8 // seq_size, LANES), BF)],
-        [],
-        tail, nc_all, name="late_products",
+    per = SMALL * 8 // seq_size
+    late_views = {0: np.s_[:, :, 2 * LANES :], 2: np.s_[:, :width]}
+    if tiled:
+        (late,) = call(
+            functools.partial(late_products_kernel, piece), [((groups, 2 * LANES + per // groups, LANES), BF)], [],
+            qkvg, branch_all, normed_all, tail, name="late_products", us=2, views=late_views,
+        )
+    else:
+        in_part, out_part, small = call(
+            functools.partial(late_products_kernel, piece), [((piece, width), BF), ((piece, width), BF), ((per, LANES), BF)],
+            [], qkvg, branch_all, normed_all, tail, name="late_products", us=2, views=late_views,
+        )
+        late = jnp.concatenate([v.reshape(groups, -1, LANES) for v in (in_part, out_part, small)], axis=1)
+    late = exchange(late, "dp")
+    copies_out = groups // 2 * seq_size if tiled else 1
+    (late,) = call(
+        sum_and_spread_kernel, [((copies_out, late.shape[1] + 16, LANES), BF)], [], late, grad_n1, name="late_sum", us=1
     )
-    late = jnp.concatenate([v.reshape(groups, -1, LANES) for v in (in_part, small)], axis=1)
-    late = jnp.sum(exchange(late, "dp").astype(F32), axis=0).astype(BF)
-    late = everywhere(late)
+    if tiled:
+        grad_w_proj, grad_w_qkv, half = call(
+            functools.partial(early_assembly_kernel, groups),
+            [((width, width), F32), ((width, 3 * width), F32), ((width, 2 * inner_width), F32)],
+            [vmem((width, inner_width), F32), sem],
+            early, name="early_assembly", us=6, raw_out=(2,),
+        )
+        mine = own_core(late, groups, seq_size)
+        mine, half, grad_tokens = lax.optimization_barrier((mine, half, grad_tokens))
+        other = lax.ppermute(mine, "dp", [(g, g ^ 1) for g in range(groups)])
+        row = lambda n: ((n, inner_width), F32)
+        grad_w_in, grad_w_out, g_n1, g_conv_w, g_conv_b, g_xp, g_dt, g_dtb, g_a, g_skip, g_n2 = call(
+            functools.partial(late_assembly_kernel, groups),
+            [
+                ((width, 2 * inner_width), F32), ((inner_width, width), F32), ((1, width), F32), row(conv_w.shape[0]),
+                row(1), row(2 * states + rank), row(rank), row(1), row(states), row(1), ((1, width), F32),
+            ],
+            [vmem((width, inner_width), F32), vmem((SMALL * 8, LANES), F32), sem],
+            mine, other, half, name="late_assembly", us=4,
+            raw=(2,), raw_out=(0,), aliases={2: 0},
+        )
+        flat = lambda v: v.reshape(-1)
+        return (out, grad_tokens, flat(g_n1), grad_w_in, g_conv_w, flat(g_conv_b), g_xp.T, g_dt, flat(g_dtb), g_a.T,
+                flat(g_skip), grad_w_out, flat(g_n2), grad_w_qkv, grad_w_proj)
+    late = everywhere(late[0])
 
     def whole(gathered, first, last):
         part = gathered.reshape(groups, seq_size, -1, LANES)[:, :, first:last]
@@ -653,12 +977,12 @@
             total = ends[-1][1]
         return ends
 
-    at_head, at_gate, at_out = cut((4 * HD * width // copies, piece * width, branch * inner_width))
-    at_in, at_small = cut((piece * width, SMALL * 8 // seq_size * LANES))
+    at_head, at_gate = cut((4 * HD * width // copies, piece * width))
+    at_in, at_out, at_small = cut((piece * width, piece * width, per * LANES))
     heads = whole(early, *at_head).reshape(H, 4, HD, width)
     grad_w_proj = heads[:, 0].reshape(H * HD, width).astype(F32)
     grad_w_qkv = heads[:, 1:].transpose(3, 1, 0, 2).reshape(width, 3 * width).astype(F32)
-    grad_w_out = whole(early, *at_out).reshape(width, inner_width).T.astype(F32)
+    grad_w_out = whole(late, *at_out).reshape(inner_width, width).astype(F32)
     grad_w_in = jnp.concatenate(
         [whole(late, *at_in).reshape(inner_width, width), whole(early, *at_gate).reshape(inner_width, width)], axis=0
     ).T.astype(F32)
@@ -666,7 +990,7 @@
     return (
         out,
         grad_tokens,
-        small[103, :width],
+        jnp.sum(late[:, -16:].reshape(groups * seq_size, -1)[:, :width].astype(F32), axis=0),
         grad_w_in,
         small[96:100],
         small[100],

time: 346 us -> 264 us (0.76); the launches traced: 341 us -> 263 us
  blocking collectives: 154 us -> 64.5 us
  local copies, waits for them, and re-layouts: 72.4 us -> 5.44 us
  starting transfers between devices: 9.75 us -> 42.3 us
  Pallas kernels: 46.6 us -> 78 us
  waiting for transfers between devices: 30.3 us -> 57.7 us
  other arithmetic: 14 us -> 1.33 us
    all_to_all x7 -> x3, blocking collectives: 154 us -> 64.5 us  [exchange(): return lax.all_to_all(value, axes, 0, 0, tiled=True)]
    unnamed x142 -> x16, local copies, waits for them, and re-layouts: 47.1 us -> 4.71 us
    pallas_call x7 -> x14, Pallas kernels: 46.6 us -> 78 us  [call(): pl.pallas_call(run, out_shape=[jax.ShapeDtypeStruct(s, d) for s, d in out...]
    all_to_all x1 -> x4, starting transfers between devices: 4.33 us -> 27.5 us  [exchange(): return lax.all_to_all(value, axes, 0, 0, tiled=True)]
    all_to_all x1 -> x4, waiting for transfers between devices: 0.01 us -> 18.4 us  [exchange(): return lax.all_to_all(value, axes, 0, 0, tiled=True)]
    convert_element_type x5 -> x0, other arithmetic: 9.74 us -> none  [the longest x1 3.83 us: body(): grad_w_in = jnp.concatenate([whole(late, *at_in).reshape(inner_width, wid...]
    all_to_all x0 -> x1, starting transfers between devices: none -> 7.59 us  [own_core(): lax.all_to_all(value, ('dp', 'seq'), 0, 0, tiled=True, axis_index_groups=...]
    another operation x3 -> x0, local copies, waits for them, and re-layouts: 7.26 us -> none  [the longest x1 4.34 us: body(): heads = whole(early, *at_head).reshape(H, 4, HD, width)]
  transfers between devices with their start and end apart: 6 -> 12, of which waited for: 3 -> 5; matrix products, arithmetic and copies ran while one was open for 3% -> 1% of each run, Pallas kernels for 11% -> 28%
where the time goes in v1:
time: 264 us; the launch traced here: 263 us
  Pallas kernels  78 us (30%)
  blocking collectives  64.5 us (24%)
  waiting for transfers between devices  57.7 us (22%)
  starting transfers between devices  42.3 us (16%)
  between operations  14 us (5%)
  local copies, waits for them, and re-layouts  5.44 us (2%)
    pallas_call x14, Pallas kernels, call(): pl.pallas_call(run, out_shape=[jax.ShapeDtypeStruct(s, d) for s, d in out...  78 us
    all_to_all x3, blocking collectives, exchange(): return lax.all_to_all(value, axes, 0, 0, tiled=True)  64.5 us
    ppermute x1, waiting for transfers between devices, body(): lax.ppermute(grad_halo, 'seq', [(i + 1, i) for i in range(seq_size - 1)])  34.6 us
    all_to_all x4, starting transfers between devices, exchange(): return lax.all_to_all(value, axes, 0, 0, tiled=True)  27.5 us
    all_to_all x4, waiting for transfers between devices, exchange(): return lax.all_to_all(value, axes, 0, 0, tiled=True)  18.4 us
    all_to_all x1, starting transfers between devices, own_core(): lax.all_to_all(value, ('dp', 'seq'), 0, 0, tiled=True, axis_index_groups=...  7.59 us
  transfers between devices with their start and end apart: 12, of which 5 were waited for; matrix products, arithmetic and copies ran while one was open for 1% of the time, Pallas kernels for 28%

profile of v1, /device:TPU:13, one launch (start us, length us, event | category | flops | bytes accessed | tf_op | source)
XLA Modules:
  0.0 263.2 jit_solution(12661087735565351929)
XLA Ops:
  7.2 0.0 all-gather.10.cloned.1.call-start
  7.2 0.7 all-gather.10.cloned.1.call-update
  7.9 0.0 all-gather.8.cloned.1.call-start
  8.0 0.7 slice.22
  8.7 3.1 %collective-permute-start = (bf16[16,512]{1,0:T(8,128)(2,1)S(1)}, bf16[16,512]{1,0:T(8,128)(2,1)S(1)}, u32[]{:S(2)}, u32[]{:S(2)}) collective-permute-start(bf16[16,512]{1,0:T(8,128)(2,1)S(1)} %slice.22), channel_id=1, source_target_pairs={{0,1},{1,2},{2,3},{3,4},{4,5},{5,6},{6,7},{8,9},{9,10},{10,11},{11... | collective-permute-start | bytes 49160 | tf_op jit(solution)/shard_map/ppermute | solution.py:825
  11.8 1.3 collective-permute-done.refs_1_.refs_4_
  13.2 0.6 copy-done.6
  13.8 7.4 %forward.1 = (bf16[8,160,128]{2,1,0:T(8,128)(2,1)}, bf16[128,512]{1,0:T(8,128)(2,1)}, bf16[144,1024]{1,0:T(8,128)(2,1)}, bf16[128,1024]{1,0:T(8,128)(2,1)}, bf16...) custom-call(bf16[128,512]{1,0:T(8,128)(2,1)} %refs_3_.5, ...), custom_call_target="tpu_custom_call" | custom-call | flops 8000 | bytes 8000 | tf_op jit(solution)/shard_map/forward/pallas_call | solution.py:772
  21.2 13.4 %all_to_all.40.refs_0_.refs_1_ = bf16[8,160,128]{2,1,0:T(8,128)(2,1)} all-to-all(bf16[8,160,128]{2,1,0:T(8,128)(2,1)} %get-tuple-element.74), channel_id=1, replica_groups=mesh['dp'=4,'seq'=8] {'seq'}, dimensions={0} | all-to-all | bytes 655360 | tf_op jit(solution)/shard_map/all_to_all | solution.py:786
  34.6 6.8 %middle.1 = (bf16[8,128,384]{2,1,0:T(8,128)(2,1)}, f32[128,128]{1,0:T(8,128)}, f32[128,1024]{1,0:T(8,128)}, bf16[128,1024]{1,0:T(8,128)(2,1)}, f32[128,512]{1,0:T(8,128)}) custom-call(bf16[8,160,128]{2,1,0:T(8,128)(2,1)} %all_to_all.40.refs_0_.refs_1_, f32[128,128]{1,0:T(8,128)} %get-tuple-element.75.refs_1_.refs_10_.refs_2_, ...), custom_call_target="tpu_custom_call" | custom-call | flops 8000 | bytes 8000 | tf_op jit(solution)/shard_map/middle/pallas_call | solution.py:772
  41.3 0.0 all-gather.8.cloned.1.call-update
  41.4 0.0 all-gather.6.cloned.1.call-start
  41.4 23.8 %all_to_all.41.refs_0_ = bf16[8,128,384]{2,1,0:T(8,128)(2,1)} all-to-all(bf16[8,128,384]{2,1,0:T(8,128)(2,1)} %get-tuple-element.82), channel_id=1, replica_groups=mesh['dp'=4,'seq'=8] {'seq'}, dimensions={0} | all-to-all | bytes 1572864 | tf_op jit(solution)/shard_map/all_to_all | solution.py:786
  65.3 7.4 %attention.1.refs_0_ = bf16[8,128,256]{2,1,0:T(8,128)(2,1)} custom-call(bf16[8,128,384]{2,1,0:T(8,128)(2,1)} %all_to_all.41.refs_0_, bf16[8,160,128]{2,1,0:T(8,128)(2,1)} %all_to_all.40.refs_0_.refs_1_), custom_call_target="tpu_custom_call" | custom-call | flops 7000 | bytes 7000 | tf_op jit(solution)/shard_map/attention/pallas_call | solution.py:772
  72.7 27.2 %all_to_all.42.refs_0_ = bf16[8,128,256]{2,1,0:T(8,128)(2,1)} all-to-all(bf16[8,128,256]{2,1,0:T(8,128)(2,1)} %attention.1.refs_0_), channel_id=1, replica_groups=mesh['dp'=4,'seq'=8] {'seq'}, dimensions={0} | all-to-all | bytes 1048576 | tf_op jit(solution)/shard_map/all_to_all | solution.py:786
  99.9 6.1 %backward.1 = (bf16[128,512]{1,0:T(8,128)(2,1)}, f32[128,512]{1,0:T(8,128)}, bf16[128,512]{1,0:T(8,128)(2,1)}, f32[1,512]{1,0:T(1,128)}, bf16[128,1024]{1,0:T(8,...) custom-call(bf16[8,128,256]{2,1,0:T(8,128)(2,1)} %all_to_all.42.refs_0_, ...), custom_call_target="tpu_custom_call" | custom-call | flops 7000 | bytes 7000 | tf_op jit(solution)/shard_map/backward/pallas_call | solution.py:772
  106.0 0.0 all-gather.6.cloned.1.call-update
  106.1 7.2 %all-to-all-start.3 = ((bf16[8,256,128]{2,1,0:T(8,128)(2,1)}), bf16[8,256,128]{2,1,0:T(8,128)(2,1)S(1)}, u32[]{:S(2)}, u32[]{:S(2)}) async-start(bf16[8,256,128]{2,1,0:T(8,128)(2,1)} %get-tuple-element.88), calls=%async_computation.3 | async-start | bytes 1048576 | tf_op jit(solution)/shard_map/all_to_all | solution.py:786
  113.3 7.5 %states.1 = (f32[16512,128]{1,0:T(8,128)}, f32[128,1024]{1,0:T(8,128)}) custom-call(f32[128,128]{1,0:T(8,128)} %get-tuple-element.93.refs_0_, f32[128,128]{1,0:T(8,128)} %get-tuple-element.75.refs_1_.refs_10_.refs_2_, f32[128,32]{1,0:T(8,128)} %get-tuple-element.76.refs_2_.refs_11_.refs_3_, f32[1024,128]{1,0:T(8,128)} %get-tuple-element.77.refs_3_.refs_9_.refs_4_, ...), custom_call_target="tpu_custom_call" | custom-call | flops 6000 | bytes 6000 | tf_op jit(solution)/shard_map/states/pallas_call | solution.py:772
  120.8 0.0 all-gather.10.cloned.1.call-done.refs_1_
  120.9 0.0 all-gather.8.cloned.1.call-done.refs_2_.refs_0_
  120.9 3.8 %head_products.1.refs_2_ = bf16[4,256,128]{2,1,0:T(8,128)(2,1)} custom-call(bf16[8,128,256]{2,1,0:T(8,128)(2,1)} %attention.1.refs_0_, bf16[1024,512]{1,0:T(8,128)(2,1)} %all-gather.10.cloned.1.call-done.refs_1_, bf16[1024,1024]{1,0:T(8,128)(2,1)} %all-gather.8.cloned.1.call-done.refs_2_.refs_0_), custom_call_target="tpu_custom_call" | custom-call | flops 3000 | bytes 3000 | tf_op jit(solution)/shard_map/head_products/pallas_call | solution.py:772
  124.7 0.8 copy-done.1
  125.5 2.6 gate_products.1
  128.1 10.9 %all-to-all-start.7 = ((bf16[4,384,128]{2,1,0:T(8,128)(2,1)}), bf16[4,384,128]{2,1,0:T(8,128)(2,1)S(1)}, u32[]{:S(2)}, u32[]{:S(2)}) async-start(bf16[4,384,128]{2,1,0:T(8,128)(2,1)} %gate_products.1), calls=%async_computation.7 | async-start | bytes 786432 | tf_op jit(solution)/shard_map/all_to_all | solution.py:786
  139.0 14.8 %adjoint.1 = (bf16[8,272,128]{2,1,0:T(8,128)(2,1)}, bf16[144,1024]{1,0:T(8,128)(2,1)}) custom-call(bf16[8,256,128]{2,1,0:T(8,128)(2,1)} %copy-done.1, bf16[8,160,128]{2,1,0:T(8,128)(2,1)} %all_to_all.40.refs_0_.refs_1_, f32[128,128]{1,0:T(8,128)} %get-tuple-element.75.refs_1_.refs_10_.refs_2_, f32[128,32]{1,0:T(8,128)} %get-tuple-element.76.refs_2_.refs_11_.refs_3_, ...), custom_call_target="tpu_custom_call" | custom-call | flops 15000 | bytes 15000 | tf_op jit(solution)/shard_map/adjoint/pallas_call | solution.py:772
  153.8 0.0 copy-start.3
  153.8 0.7 copy-done.3
  154.6 1.7 early_sum.1
  156.3 0.0 all-gather.12.cloned.1.call-update
  156.3 5.5 %all-to-all-start.4 = ((bf16[8,272,128]{2,1,0:T(8,128)(2,1)}), bf16[8,272,128]{2,1,0:T(8,128)(2,1)S(1)}, u32[]{:S(2)}, u32[]{:S(2)}) async-start(bf16[8,272,128]{2,1,0:T(8,128)(2,1)} %get-tuple-element.97), calls=%async_computation.4 | async-start | bytes 1114112 | tf_op jit(solution)/shard_map/all_to_all | solution.py:786
  161.8 14.4 %all-to-all-done.4.refs_3_ = bf16[8,272,128]{2,1,0:T(8,128)(2,1)S(1)} async-done(((bf16[8,272,128]{2,1,0:T(8,128)(2,1)}), bf16[8,272,128]{2,1,0:T(8,128)(2,1)S(1)}, u32[]{:S(2)}, u32[]{:S(2)}) %all-to-all-start.4) | async-done | bytes 557088 | tf_op jit(solution)/shard_map/all_to_all | solution.py:786
  176.2 0.8 copy-done.2
  177.0 3.2 %late_products.1 = bf16[4,288,128]{2,1,0:T(8,128)(2,1)} custom-call(bf16[8,128,384]{2,1,0:T(8,128)(2,1)} %all_to_all.41.refs_0_, bf16[1024,512]{1,0:T(8,128)(2,1)} %all-gather.6.cloned.1.call-done.refs_1_, bf16[1024,1024]{1,0:T(8,128)(2,1)} %all-gather.8.cloned.1.call-done.refs_2_.refs_0_, bf16[8,272,128]{2,1,0:T(8,128)(2,1)} %copy-done.2), custom_call_target="tpu_custom_call" | custom-call | flops 2000 | bytes 2000 | tf_op jit(solution)/shard_map/late_products/pallas_call | solution.py:772
  180.3 3.9 %all-to-all-start.5 = ((bf16[4,288,128]{2,1,0:T(8,128)(2,1)}), bf16[4,288,128]{2,1,0:T(8,128)(2,1)S(1)}, u32[]{:S(2)}, u32[]{:S(2)}) async-start(bf16[4,288,128]{2,1,0:T(8,128)(2,1)} %late_products.1), calls=%async_computation.5 | async-start | bytes 589824 | tf_op jit(solution)/shard_map/all_to_all | solution.py:786
  184.1 3.5 %tokens.1 = (f32[128,512]{1,0:T(8,128)}, f32[8,512]{1,0:T(8,128)}, bf16[16,128]{1,0:T(8,128)(2,1)}) custom-call(bf16[144,1024]{1,0:T(8,128)(2,1)} %get-tuple-element.98.refs_0_.refs_1_, bf16[512,2048]{1,0:T(8,128)(2,1)} %refs_1_.1, bf16[128,1024]{1,0:T(8,128)(2,1)} %get-tuple-element.99.refs_2_, bf16[128,512]{1,0:T(8,128)(2,1)} %refs_3_.5, ...), custom_call_target="tpu_custom_call" | custom-call | flops 4000 | bytes 4000 | tf_op jit(solution)/shard_map/tokens/pallas_call | solution.py:772
  187.6 4.0 %all-to-all-done.5.refs_0_ = bf16[4,288,128]{2,1,0:T(8,128)(2,1)S(1)} async-done(((bf16[4,288,128]{2,1,0:T(8,128)(2,1)}), bf16[4,288,128]{2,1,0:T(8,128)(2,1)S(1)}, u32[]{:S(2)}, u32[]{:S(2)}) %all-to-all-start.5) | async-done | bytes 294944 | tf_op jit(solution)/shard_map/all_to_all | solution.py:786
  191.6 0.7 copy-done.5
  192.3 2.1 late_sum.1
  194.5 7.6 %all-to-all-start.6 = ((bf16[16,304,128]{2,1,0:T(8,128)(2,1)}), bf16[16,304,128]{2,1,0:T(8,128)(2,1)S(1)}, u32[]{:S(2)}, u32[]{:S(2)}) async-start(bf16[16,304,128]{2,1,0:T(8,128)(2,1)} %late_sum.1), calls=%async_computation.6 | async-start | bytes 2490368 | tf_op jit(solution)/shard_map/all_to_all | solution.py:799
  202.1 2.2 collective-permute-start.1
  204.3 34.6 %collective-permute-done.1 = f32[8,512]{1,0:T(8,128)S(1)} collective-permute-done((f32[8,512]{1,0:T(8,128)S(1)}, f32[8,512]{1,0:T(8,128)S(1)}, u32[]{:S(2)}, u32[]{:S(2)}) %collective-permute-start.1) | collective-permute-done | bytes 16416 | tf_op jit(solution)/shard_map/ppermute | solution.py:923
  238.9 1.3 add_dynamic-update-slice_fusion
  240.2 6.2 %early_assembly.1 = (f32[512,512]{1,0:T(8,128)}, f32[512,1536]{1,0:T(8,128)}, f32[512,2048]{1,0:T(8,128)}) custom-call(bf16[32,384,128]{2,1,0:T(8,128)(2,1)} %bitcast.16), custom_call_target="tpu_custom_call" | custom-call | flops 6000 | bytes 6000 | tf_op jit(solution)/shard_map/early_assembly/pallas_call | solution.py:772
  246.4 1.8 collective-permute-start.2
  248.2 2.6 collective-permute-done.2.refs_1_
  250.8 1.1 copy-done.4
  251.8 4.9 %late_assembly.1 = (f32[512,2048]{1,0:T(8,128)}, f32[1024,512]{1,0:T(8,128)}, f32[1,512]{1,0:T(1,128)}, f32[4,1024]{1,0:T(4,128)}, f32[1,1024]{1,0:T(1,128)}, /*...) custom-call(bf16[16,304,128]{2,1,0:T(8,128)(2,1)} %copy-done, ...), custom_call_target="tpu_custom_call", output_to_operand_aliasing={{0}: (2, {})} | custom-call | flops 4000 | bytes 4000 | tf_op jit(solution)/shard_map/late_assembly/pallas_call | solution.py:772
  (15 shorter events, 0.0 us)
Async XLA Ops:
  7.2 113.7 %all-gather.10.cloned.1.call-start = ((), (), s32[]{:S(2)}) async-start(), calls=%async_computation.10 | async-start | bytes 1179648 | tf_op jit(solution)/shard_map/all_gather | solution.py:823
  7.9 113.0 %all-gather.8.cloned.1.call-start = ((), (), s32[]{:S(2)}) async-start(), calls=%async_computation.9 | async-start | bytes 2359296 | tf_op jit(solution)/shard_map/all_gather | solution.py:848
  8.7 4.5 %collective-permute-start = (bf16[16,512]{1,0:T(8,128)(2,1)S(1)}, bf16[16,512]{1,0:T(8,128)(2,1)S(1)}, u32[]{:S(2)}, u32[]{:S(2)}) collective-permute-start(bf16[16,512]{1,0:T(8,128)(2,1)S(1)} %slice.22), channel_id=1, source_target_pairs={{0,1},{1,2},{2,3},{3,4},{4,5},{5,6},{6,7},{8,9},{9,10},{10,11},{11... | collective-permute-start | bytes 49160 | tf_op jit(solution)/shard_map/ppermute | solution.py:825
  13.2 0.6 copy-start.6
  41.4 120.4 %all-gather.6.cloned.1.call-start = ((), (), s32[]{:S(2)}) async-start(), calls=%async_computation.8 | async-start | bytes 1179648 | tf_op jit(solution)/shard_map/all_gather | solution.py:869
  106.1 18.7 %all-to-all-start.3 = ((bf16[8,256,128]{2,1,0:T(8,128)(2,1)}), bf16[8,256,128]{2,1,0:T(8,128)(2,1)S(1)}, u32[]{:S(2)}, u32[]{:S(2)}) async-start(bf16[8,256,128]{2,1,0:T(8,128)(2,1)} %get-tuple-element.88), calls=%async_computation.3 | async-start | bytes 1048576 | tf_op jit(solution)/shard_map/all_to_all | solution.py:786
  124.7 0.8 copy-start.1
  128.1 25.7 %all-to-all-start.7 = ((bf16[4,384,128]{2,1,0:T(8,128)(2,1)}), bf16[4,384,128]{2,1,0:T(8,128)(2,1)S(1)}, u32[]{:S(2)}, u32[]{:S(2)}) async-start(bf16[4,384,128]{2,1,0:T(8,128)(2,1)} %gate_products.1), calls=%async_computation.7 | async-start | bytes 786432 | tf_op jit(solution)/shard_map/all_to_all | solution.py:786
  139.0 101.2 %all-gather.12.cloned.1.call-start = ((), (), s32[]{:S(2)}) async-start(), calls=%async_computation.11 | async-start | bytes 3244032 | tf_op jit(solution)/shard_map/all_gather | solution.py:917
  153.8 0.7 copy-start.3
  156.3 19.9 %all-to-all-start.4 = ((bf16[8,272,128]{2,1,0:T(8,128)(2,1)}), bf16[8,272,128]{2,1,0:T(8,128)(2,1)S(1)}, u32[]{:S(2)}, u32[]{:S(2)}) async-start(bf16[8,272,128]{2,1,0:T(8,128)(2,1)} %get-tuple-element.97), calls=%async_computation.4 | async-start | bytes 1114112 | tf_op jit(solution)/shard_map/all_to_all | solution.py:786
  176.2 0.8 copy-start.2
  180.3 11.4 %all-to-all-start.5 = ((bf16[4,288,128]{2,1,0:T(8,128)(2,1)}), bf16[4,288,128]{2,1,0:T(8,128)(2,1)S(1)}, u32[]{:S(2)}, u32[]{:S(2)}) async-start(bf16[4,288,128]{2,1,0:T(8,128)(2,1)} %late_products.1), calls=%async_computation.5 | async-start | bytes 589824 | tf_op jit(solution)/shard_map/all_to_all | solution.py:786
  187.6 14.5 %copy-start.7 = (f32[8,512]{1,0:T(8,128)S(1)}, f32[8,512]{1,0:T(8,128)}, u32[]{:S(2)}) copy-start(f32[8,512]{1,0:T(8,128)} %get-tuple-element.104) | copy-start | bytes 49156
  191.6 0.7 copy-start.5
  194.5 51.9 %all-to-all-start.6 = ((bf16[16,304,128]{2,1,0:T(8,128)(2,1)}), bf16[16,304,128]{2,1,0:T(8,128)(2,1)S(1)}, u32[]{:S(2)}, u32[]{:S(2)}) async-start(bf16[16,304,128]{2,1,0:T(8,128)(2,1)} %late_sum.1), calls=%async_computation.6 | async-start | bytes 2490368 | tf_op jit(solution)/shard_map/all_to_all | solution.py:799
  202.1 36.8 %collective-permute-start.1 = (f32[8,512]{1,0:T(8,128)S(1)}, f32[8,512]{1,0:T(8,128)S(1)}, u32[]{:S(2)}, u32[]{:S(2)}) collective-permute-start(f32[8,512]{1,0:T(8,128)S(1)} %copy-done.7), channel_id=1, source_target_pairs={{1,0},{2,1},{3,2},{4,3},{5,4},{6,5},{7,6},{9,8},{10,9},{11,10},{12... | collective-permute-start | bytes 49160 | tf_op jit(solution)/shard_map/ppermute | solution.py:923
  246.4 4.4 %copy-start = (bf16[16,304,128]{2,1,0:T(8,128)(2,1)}, bf16[16,304,128]{2,1,0:T(8,128)(2,1)S(1)}, u32[]{:S(2)}) copy-start(bf16[16,304,128]{2,1,0:T(8,128)(2,1)S(1)} %all-to-all-done.6.refs_0_) | copy-start | bytes 3735556
  246.4 4.3 %collective-permute-start.2 = (bf16[16,304,128]{2,1,0:T(8,128)(2,1)S(1)}, bf16[16,304,128]{2,1,0:T(8,128)(2,1)S(1)}, u32[]{:S(2)}, u32[]{:S(2)}) collective-permute-start(bf16[16,304,128]{2,1,0:T(8,128)(2,1)S(1)} %all-to-all-done.6.refs_0_), channel_id=1, source_target_pairs={{0,8},{8,0},{16,24},{24,16},{1,9},{9,1},{17,25},{25,17},{2,10},{10... | collective-permute-start | bytes 3735560 | tf_op jit(solution)/shard_map/ppermute | solution.py:952
  250.8 1.1 copy-start.4
Sparse Core Ops, SparseCore 0:
  10.1 39.8 all-gather.9
  52.1 57.7 all-gather.7
  112.6 40.8 all-gather.5
  156.8 70.7 all-gather.11

commit v2 on v1

--- a/solution.py
+++ b/solution.py
@@ -96,7 +96,7 @@
     rank = w_dt.shape[0]
     x = jnp.concatenate([halo[...], tok[...]], axis=0).astype(F32)
     normed = (x * rms_parts(x) * n1[...]).astype(BF)
-    o_normed[...] = normed[HALO:]
+    o_normed[...] = normed
     sent(o_normed)
     w_in = ready(w_in)
     inner = dot(normed, w_in[:, :inner_width]).astype(BF)
@@ -160,9 +160,9 @@
 
 
 def middle_kernel(
-    msg, a_ref, bc, s_ref, dx_ref, mixed, gate, d_skip, tok, w_out, n2, w_qkv, cot, w_proj, normed_one,
-    o_qkvg, o_start, o_ssm, o_normed, o_after,
-    gated, y_ref,
+    msg, a_ref, bc, s_ref, dx_ref, mixed, gate, d_skip, tok, w_out, n2, w_qkv, grad_att,
+    o_qkvg, o_start, o_ssm, o_after, o_gated, o_normed,
+    y_ref,
 ):
     msg, a_ref = ready(msg, a_ref)
     states = a_ref.shape[0] // 8
@@ -201,26 +201,21 @@
         ssm = from_rows(y_ref, j, count) + d_skip[:, tile(j)] * mixed[:, tile(j)].astype(F32)
         o_ssm[:, tile(j)] = ssm
         v = gate[:, tile(j)].astype(F32)
-        gated[:, tile(j)] = (ssm * (v * jax.nn.sigmoid(v))).astype(BF)
-    sent(o_ssm)
-    piece = inner_width // o_qkvg.shape[0]
-    for d in range(o_qkvg.shape[0]):
-        o_qkvg[d, :, 2 * LANES : 2 * LANES + piece] = gated[:, d * piece : (d + 1) * piece]
-    after = tok[...].astype(F32) + dot(gated[...], w_out[...])
+        o_gated[:, tile(j)] = (ssm * (v * jax.nn.sigmoid(v))).astype(BF)
+    sent(o_ssm, o_gated)
+    after = tok[...].astype(F32) + dot(o_gated[...], w_out[...])
     o_after[...] = after
     sent(o_after)
     normed = (after * rms_parts(after) * n2[...]).astype(BF)
-    normed_one, w_qkv, cot, w_proj = ready(normed_one, w_qkv, cot, w_proj)
-    o_normed[:, :width] = normed_one[...]
-    o_normed[:, width:] = normed
+    o_normed[...] = normed
     sent(o_normed)
+    w_qkv, grad_att = ready(w_qkv, grad_att)
     qkv = dot(normed, w_qkv[...])
-    gatt = dot_nt(cot[...], w_proj[...])
     copies = o_qkvg.shape[0] // H
     left = lax.broadcasted_iota(jnp.int32, (count, LANES), 1) < HD
     for p in range(H // 2):
         q, k, v = (qkv[:, i * width + p * LANES : i * width + (p + 1) * LANES] for i in range(3))
-        g = gatt[:, tile(p)]
+        g = grad_att[:, tile(p)].astype(F32)
         first = (jnp.where(left, q, pltpu.roll(k, HD, 1)), jnp.where(left, v, pltpu.roll(g, HD, 1)))
         second = (jnp.where(left, pltpu.roll(q, HD, 1), k), jnp.where(left, pltpu.roll(v, HD, 1), g))
         for h, pair in ((2 * p, first), (2 * p + 1, second)):
@@ -230,6 +225,11 @@
                     o_qkvg[h * copies + r, :, tile(i)] = value
 
 
+def grad_att_kernel(cot, w_proj, o_grad):
+    cot, w_proj = ready(cot, w_proj)
+    o_grad[...] = dot_nt(cot[...], w_proj[...]).astype(BF)
+
+
 def attention_kernel(qkvg, ends, o_back, qz, kr, gz, vr, dk, dv):
     qkvg, ends = ready(qkvg, ends)
     seq_size, count = qkvg.shape[0], qkvg.shape[1]
@@ -237,7 +237,7 @@
     left = lax.broadcasted_iota(jnp.int32, (count, LANES), 1) < HD
     for d in range(seq_size):
         at = slice(d * count, (d + 1) * count)
-        a, b = qkvg[d, :, :LANES].astype(F32), qkvg[d, :, LANES : 2 * LANES].astype(F32)
+        a, b = qkvg[d, :, :LANES].astype(F32), qkvg[d, :, LANES:].astype(F32)
         qz[at, :] = jnp.where(left, a, 0.0).astype(BF)
         kr[at, :] = pltpu.roll(a, HD, 1).astype(BF)
         gz[at, :] = jnp.where(left, 0.0, b).astype(BF)
@@ -281,8 +281,7 @@
 
 def backward_kernel(
     back, after, w_proj, w_qkv, n2, cot, w_out, gate, ssm, s_ref, a_ref, bc,
-    o_out, o_after, o_branch, o_n2, o_gate, o_g, o_msg,
-    turned,
+    o_out, o_after, o_branch, o_n2, o_gate, o_g, o_msg, o_attended, *o_more
 ):
     back = ready(back)
     seq_size, count = back.shape[0], back.shape[1]
@@ -299,10 +298,13 @@
     attended = jnp.concatenate(att, axis=1).astype(BF)
     after, w_proj = ready(after, w_proj)
     width = after.shape[1]
+    o_attended[...] = attended
     o_out[...] = (after[...] + dot(attended, w_proj[...])).astype(BF)
-    sent(o_out)
+    sent(o_attended, o_out)
     w_qkv, n2, cot = ready(w_qkv, n2, cot)
     grad_qkv = jnp.concatenate(dq + dk + dv, axis=1).astype(BF)
+    if o_more:
+        o_more[0][...] = grad_qkv
     grad_x, grad_gain = rms_back(after[...], n2[...], dot_nt(grad_qkv, w_qkv[...]))
     o_n2[...] = jnp.sum(grad_gain, axis=0, keepdims=True)
     grad_after = cot[...].astype(F32) + grad_x
@@ -316,7 +318,6 @@
     a_ref = ready(a_ref)
     states = a_ref.shape[0] // 8
     grad_gated = dot_nt(branch, w_out[...])
-    gate_rows = inner_width // seq_size
     for j in range(tiles):
         v = gate[:, tile(j)].astype(F32)
         sig = jax.nn.sigmoid(v)
@@ -324,9 +325,6 @@
         to_rows(o_g, j, grad * (v * sig))
         grad_gate = grad * ssm[:, tile(j)] * (sig * (1.0 + v * (1.0 - sig)))
         o_gate[:, tile(j)] = grad_gate.astype(BF)
-        turned[tile(j), :] = jnp.transpose(grad_gate).astype(BF)
-    for d in range(seq_size):
-        o_msg[d, states * 8 :, :] = turned[d * gate_rows : (d + 1) * gate_rows, :]
     sent(o_gate, o_g)
     s_ref, smem = ready(s_ref, bc)
 
@@ -388,10 +386,7 @@
 
 
 def adjoint_kernel(
-    seq_size, back, totals, a_ref, bc, s_ref, dx_ref, g_ref, mixed, step_pre, low, w_dt, w_xp, inner, slope, conv_w, d_skip,
-    seg, grad_n2, every,
-    o_msg, o_inner,
-    held, gs_ref, ai_ref, sums, small, ext, gext, arrived,
+    seq_size, back, totals, a_ref, bc, s_ref, dx_ref, g_ref, every, gs_ref, ai_ref, o_bc, o_a, held, sums, arrived
 ):
     back, totals, a_ref = ready(back, totals, a_ref)
     states = a_ref.shape[0] // 8
@@ -447,22 +442,42 @@
     carry = (leaving, (zero,) * states)
     for c in reversed(range(chunks)):
         loads[c].wait()
-        carry = lax.fori_loop(0, span, functools.partial(one, (c + 1) * span - 1), carry)
+        carry = lax.fori_loop(0, span, functools.partial(one, (c + 1) * span - 1), carry, unroll=4)
     grad_a = carry[1]
+    sent(gs_ref, ai_ref)
+    for n in range(states):
+        o_a[8 * n : 8 * n + 8, :] = grad_a[n] * (LN2 * block(a_ref, n))
+    columns = o_bc.shape[1]
+    lane = lax.broadcasted_iota(jnp.int32, (LANES, columns), 1)
+    grad_bc = jnp.zeros(o_bc.shape, F32)
+    for q in range(2 * states):
+        rows = sums[pl.ds(q, count, stride=2 * states), :]
+        high = rows.astype(BF)
+        low = (rows - high.astype(F32)).astype(BF)
+        to_column = (lane == columns - 2 * states + q).astype(BF)
+        grad_bc = grad_bc + dot(high, to_column) + dot(low, to_column)
+    o_bc[...] = grad_bc
+
+
+def inner_kernel(
+    seq_size, gs_ref, ai_ref, g_ref, mixed, step_pre, low, w_dt, grad_bc, grad_a, w_xp, inner, slope, conv_w, d_skip,
+    seg, normed, grad_n2,
+    *rest,
+):
+    o_first, o_second, o_inner, *own_small, ext, gext, grad_w = rest
+    small = own_small[0] if own_small else o_second.ref
+    gs_ref, ai_ref, g_ref = ready(gs_ref, ai_ref, g_ref)
+    grad_bc, grad_a = ready(grad_bc, grad_a)
+    count = g_ref.shape[0] // 8
+    states = grad_a.shape[0] // 8
     mixed, step_pre, low, w_dt, w_xp, inner = ready(mixed, step_pre, low, w_dt, w_xp, inner)
-    slope, conv_w, d_skip, seg, grad_n2 = ready(slope, conv_w, d_skip, seg, grad_n2)
+    slope, conv_w, d_skip, seg, normed, grad_n2 = ready(slope, conv_w, d_skip, seg, normed, grad_n2)
     inner_width = mixed.shape[1]
     tiles = inner_width // LANES
     rank = w_dt.shape[0]
     taps = conv_w.shape[0]
     small[...] = jnp.zeros_like(small)
-    for n in range(states):
-        small[(104 + n) * 8 : (105 + n) * 8, :] = grad_a[n] * (LN2 * block(a_ref, n))
-    lane = lax.broadcasted_iota(jnp.int32, (count, rank + 2 * states), 1)
-    grad_bc = jnp.zeros((count, rank + 2 * states), F32)
-    for q in range(2 * states):
-        total = jnp.sum(sums[pl.ds(q, count, stride=2 * states), :], axis=1, keepdims=True)
-        grad_bc = jnp.where(lane == rank + q, total, grad_bc)
+    small[104 * 8 : (104 + states) * 8, :] = grad_a[...]
     offset = offsets_in_sequence(seg, seq_size)
     halves = []
     for j in range(tiles):
@@ -477,7 +492,7 @@
     half = jnp.concatenate(halves, axis=1)
     grad_w_dt = dot_tn(low[...], half)
     padded_dt = jnp.concatenate([w_dt[...], jnp.zeros((2 * states, inner_width), BF)], axis=0)
-    grad_selector = (dot_nt(half, padded_dt) + grad_bc).astype(BF)
+    grad_selector = (dot_nt(half, padded_dt) + grad_bc[...]).astype(BF)
     grad_w_xp = dot_tn(grad_selector, mixed[...])
     from_selector = dot(grad_selector, w_xp[...])
     ext[...] = inner[...].astype(F32)
@@ -498,24 +513,47 @@
             row = (96 + k) * 8 + j
             small[row : row + 1, :] = jnp.sum(usable * ext[shifted, tile(j)], axis=0, keepdims=True)
             gext[shifted, tile(j)] += conv_w[k : k + 1, tile(j)] * usable
-    piece = inner_width // seq_size
-    per = small.shape[0] // seq_size
     o_inner[...] = gext[...].astype(BF)
     sent(o_inner)
-    for j in range(tiles):
-        value = jnp.transpose(gext[HALO:, tile(j)]).astype(BF)
-        for i in range(LANES // piece):
-            o_msg[j * (LANES // piece) + i, :piece, :] = value[i * piece : (i + 1) * piece]
-    for d in range(seq_size):
-        rows = gext[:HALO, d * piece : (d + 1) * piece]
-        if piece < LANES:
-            rows = jnp.concatenate([rows, jnp.zeros((HALO, LANES - piece), F32)], axis=1)
-        o_msg[d, piece : piece + HALO, :] = rows.astype(BF)
     width = grad_n2.shape[1]
     for j in range(width // LANES):
         small[103 * 8 + 4 + j : 103 * 8 + 5 + j, :] = grad_n2[:, tile(j)]
-    for d in range(seq_size):
-        o_msg[d, piece + HALO :, :] = small[d * per : (d + 1) * per, :].astype(BF)
+    if not own_small:
+        o_first[...] = dot_tn(normed[...], o_inner[...])
+        return
+    grad_w[...] = dot_tn(normed[...], o_inner[...])
+    for to, x, s, at in receivers((o_first, o_second), seq_size):
+        to[x * seq_size + s, :LANES, :] = grad_w[pl.ds(pl.multiple_of(at * LANES, LANES), LANES), tile(s)].astype(BF)
+        rows = small.shape[0] // (width // LANES * seq_size)
+        here = pl.ds(pl.multiple_of((at * seq_size + s) * rows, rows), rows)
+        to[x * seq_size + s, LANES:, :] = small[here, :].astype(BF)
+
+
+def receivers(results, seq_size, mine=0):
+    core = lax.rem(lax.axis_index("dp"), 2)
+    for to, side in zip(results, (core, 1 - core)):
+        for x in range(to.shape[0] // seq_size):
+            for s in range(seq_size):
+                yield to, x, s, 2 * lax.bitwise_xor(x, mine) + side
+
+
+def partials_kernel(seq_size, gated, branch, normed, grad_gate, attended, cot, keep, send, out, gate, proj):
+    gated, branch = ready(gated, branch)
+    out[...] = dot_tn(gated[...], branch[...])
+    normed, grad_gate = ready(normed, grad_gate)
+    gate[...] = dot_tn(normed[...], grad_gate[...])
+    attended, cot = ready(attended, cot)
+    proj[...] = dot_tn(attended[...], cot[...])
+    across = out.shape[1] // LANES
+    down = seq_size // across
+    mine = lax.axis_index("dp") // 2
+    for to, x, s, at in receivers((keep, send), seq_size, mine):
+        rows = pl.ds(pl.multiple_of((at * down + s // across) * LANES, LANES), LANES)
+        to[x * seq_size + s, :LANES, :] = out[rows, tile(s % across)].astype(BF)
+        rows = pl.ds(pl.multiple_of(at * LANES, LANES), LANES)
+        to[x * seq_size + s, LANES : 2 * LANES, :] = gate[rows, tile(s)].astype(BF)
+        rows = pl.ds(pl.multiple_of((at * down + s // across) * HD, HD), HD)
+        to[x * seq_size + s, 2 * LANES :, :] = proj[rows, tile(s % across)].astype(BF)
 
 
 def tokens_kernel(grad_inner, w_in, grad_gate, tok, halo, n1, grad_after, o_tok, o_halo, o_n1):
@@ -535,80 +573,37 @@
     o_n1[...] = jnp.concatenate(rows, axis=0).astype(BF)
 
 
-def head_products_kernel(width, back, cot, normed, *outs):
-    back, cot, normed = ready(back, cot, normed)
-    seq_size, count = back.shape[0], back.shape[1]
-    both = back[...].reshape(seq_size * count, 2 * LANES)
-    proj = dot_tn(both[:, LANES:], cot[...])[HD:]
-    if len(outs) == 1:
-        first = dot_tn(normed[:, width:], both[:, :LANES])
-        second = dot_tn(normed[:, width:], both[:, LANES:])
-        left = lax.broadcasted_iota(jnp.int32, (HD, LANES), 1) < HD
-        for g in range(width // LANES):
-            outs[0][g, :HD, :] = proj[:, tile(g)].astype(BF)
-            outs[0][g, HD : 3 * HD, :] = first[tile(g)].astype(BF)
-            low, high = second[g * LANES : g * LANES + HD], second[g * LANES + HD : (g + 1) * LANES]
-            outs[0][g, 3 * HD :, :] = jnp.where(left, low, pltpu.roll(high, HD, 1)).astype(BF)
-    else:
-        outs[0][...] = proj.astype(BF)
-        outs[1][: 2 * HD, :] = dot_tn(both[:, :LANES], normed[:, width:]).astype(BF)
-        outs[1][2 * HD :, :] = dot_tn(both[:, LANES:], normed[:, width:])[:HD].astype(BF)
-
-
-def gate_products_kernel(piece, normed, adj, *rest):
-    normed, adj = ready(normed, adj)
-    seq_size = adj.shape[0]
-    count = normed.shape[0] // seq_size
-    width = normed.shape[1]
-    gate = jnp.zeros((piece, width), F32)
-    for d in range(seq_size):
-        gate = gate + dot(adj[d], normed[d * count : (d + 1) * count, :])
-    if len(rest) == 2:
-        head, pieces = rest
-        head = ready(head)
-        own = head.shape[1]
-        for g in range(head.shape[0]):
-            pieces[g, :own, :] = head[g]
-            pieces[g, own:, :] = jnp.transpose(gate[:, tile(g)]).astype(BF)
-    else:
-        rest[0][...] = gate.astype(BF)
-
-
-def late_products_kernel(piece, gated, branch, normed, tail, *outs):
-    gated, branch = ready(gated, branch)
-    seq_size, count = gated.shape[0], gated.shape[1]
-    width = branch.shape[1]
-    out = jnp.zeros((piece, width), F32)
-    for d in range(seq_size):
-        out = out + dot_tn(gated[d, :, :piece], branch[d * count : (d + 1) * count, :])
-    normed, tail = ready(normed, tail)
-    grad = jnp.zeros((piece, width), F32)
-    small = jnp.zeros((tail.shape[1] - piece - HALO, LANES), F32)
-    for d in range(seq_size):
-        grad = grad + dot(tail[d, :piece, :], normed[d * count : (d + 1) * count, :])
-        small = small + tail[d, piece + HALO :, :].astype(F32)
-        if d:
-            borrowed = dot_tn(tail[d, piece : piece + HALO, :], normed[d * count - HALO : d * count, :])
-            grad = grad + borrowed[:piece]
-    if len(outs) == 1:
-        groups = outs[0].shape[0]
-        rows = small.shape[0] // groups
-        for g in range(groups):
-            outs[0][g, :LANES, :] = jnp.transpose(grad[:, tile(g)]).astype(BF)
-            outs[0][g, LANES : 2 * LANES, :] = out[:, tile(g)].astype(BF)
-            outs[0][g, 2 * LANES :, :] = small[g * rows : (g + 1) * rows].astype(BF)
-    else:
-        outs[0][...] = grad.astype(BF)
-        outs[1][...] = out.astype(BF)
-        outs[2][...] = small.astype(BF)
-
-
-def sum_kernel(parts, o_sum):
-    parts = ready(parts)
+def head_products_kernel(normed, back, keep, send, grad, last):
+    normed, back = ready(normed, back)
+    both = back[...].reshape(back.shape[0] * back.shape[1], 2 * LANES)
+    grad[...] = dot_tn(normed[...], both[:, :LANES])
+    last[...] = dot_tn(normed[...], both[:, LANES:])
+    left = lax.broadcasted_iota(jnp.int32, (HD, LANES), 1) < HD
+    for to, x, _, at in receivers((keep, send), 1, lax.axis_index("dp") // 2):
+        to[x, : 2 * HD, :] = grad[pl.ds(pl.multiple_of(at * LANES, LANES), LANES), :].astype(BF)
+        low = last[pl.ds(pl.multiple_of(at * LANES, LANES), HD), :]
+        high = last[pl.ds(pl.multiple_of(at * LANES + HD, HD), HD), :]
+        to[x, 2 * HD :, :] = jnp.where(left, low, pltpu.roll(high, HD, 1)).astype(BF)
+
+
+def head_middle_kernel(keep, received, near, far):
+    keep, received = ready(keep, received)
+    near[...] = (keep[0].astype(F32) + received[0].astype(F32)).astype(BF)
+    far[...] = (keep[1].astype(F32) + received[1].astype(F32)).astype(BF)
+
+
+def early_sum_kernel(parts, *heads):
+    *heads, o_sum = heads
+    heads, parts = ready(*heads), ready(parts)
+    head = heads[0][...].astype(F32)
+    for part in heads[1:]:
+        head = head + part[...].astype(F32)
     total = parts[0].astype(F32)
     for d in range(1, parts.shape[0]):
         total = total + parts[d].astype(F32)
-    o_sum[...] = total.astype(BF)
+    rows = total.shape[0]
+    o_sum[:rows, :] = total.astype(BF)
+    o_sum[rows:, :] = head.astype(BF)
 
 
 def sum_and_spread_kernel(parts, own, o_all):
@@ -623,63 +618,66 @@
         o_all[d, rows:, :] = own[...]
 
 
-def early_assembly_kernel(groups, early, o_proj, o_qkv, o_in, gate, sem):
-    early = ready(early)
+def early_assembly_kernel(groups, early, w_in, o_out, o_proj, o_qkv, o_in, pieces, out, proj, qkv, gate, loads, stores):
     seq_size = early.shape[0] // groups
-    width = o_proj.shape[1]
-    inner_width = gate.shape[1]
+    inner_width, width = gate.shape[1], proj.shape[1]
+    across = width // LANES
     left = lax.broadcasted_iota(jnp.int32, (LANES, LANES), 1) < HD
+    at = 2 * LANES + HD
 
     def pairs(a, b):
         a, b = a.astype(F32), b.astype(F32)
         mask = left[: a.shape[0]]
         return jnp.where(mask, a, pltpu.roll(b, HD, 1)), jnp.where(mask, pltpu.roll(a, HD, 1), b)
 
+    own = [slice(g * seq_size, (g + 1) * seq_size) for g in range(groups)]
+    arrivals = [pltpu.make_async_copy(early.at[own[g]], pieces.at[own[g]], loads.at[g]) for g in range(groups)]
+    for copy in arrivals:
+        copy.start()
+    copies = []
     for g in range(groups):
+        arrivals[g].wait()
+        down = seq_size // across
         for s in range(seq_size):
-            gate[tile(g), tile(s)] = early[g * seq_size + s, 4 * HD :, :].astype(F32)
-    copy = pltpu.make_async_copy(gate, o_in.at[:, inner_width:], sem)
-    copy.start()
-    for g in range(groups):
-        rows = tile(g)
-        for s in range(seq_size):
-            o_proj[s * HD : (s + 1) * HD, tile(g)] = early[g * seq_size + s, :HD, :].astype(F32)
+            piece = pieces[g * seq_size + s]
+            row = g * down + s // across
+            out[tile(row), tile(s % across)] = piece[:LANES].astype(F32)
+            gate[tile(g), tile(s)] = piece[LANES : 2 * LANES].astype(F32)
+            proj[row * HD : (row + 1) * HD, tile(s % across)] = piece[2 * LANES : at].astype(F32)
         for p in range(seq_size // 2):
-            a, b = g * seq_size + 2 * p, g * seq_size + 2 * p + 1
-            q, k = pairs(early[a, HD : 3 * HD, :], early[b, HD : 3 * HD, :])
-            o_qkv[rows, p * LANES : (p + 1) * LANES] = q
-            o_qkv[rows, width + p * LANES : width + (p + 1) * LANES] = k
-            low, high = pairs(early[a, 3 * HD : 4 * HD, :], early[b, 3 * HD : 4 * HD, :])
-            o_qkv[g * LANES : g * LANES + HD, 2 * width + p * LANES : 2 * width + (p + 1) * LANES] = low
-            o_qkv[g * LANES + HD : (g + 1) * LANES, 2 * width + p * LANES : 2 * width + (p + 1) * LANES] = high
-    copy.wait()
+            a, b = pieces[g * seq_size + 2 * p], pieces[g * seq_size + 2 * p + 1]
+            first, second, third = (slice(i * width + p * LANES, i * width + (p + 1) * LANES) for i in range(3))
+            qkv[tile(g), first], qkv[tile(g), second] = pairs(a[at : at + LANES], b[at : at + LANES])
+            low, high = pairs(a[at + LANES :], b[at + LANES :])
+            qkv[g * LANES : g * LANES + HD, third] = low
+            qkv[g * LANES + HD : (g + 1) * LANES, third] = high
+        for i, (source, target, rows) in enumerate(
+            ((out, o_out, down * LANES), (proj, o_proj, down * HD), (qkv, o_qkv, LANES), (gate, o_in, LANES))
+        ):
+            here = slice(g * rows, (g + 1) * rows)
+            target = target.at[here, inner_width:] if i == 3 else target.at[here]
+            copies.append(pltpu.make_async_copy(source.at[here], target, stores.at[4 * g + i]))
+            copies[-1].start()
+    for copy in copies:
+        copy.wait()
 
 
 def late_assembly_kernel(
-    groups, mine, other, w_in, o_in, o_out, o_n1, o_conv_w, o_conv_b, o_xp, o_dt, o_dtb, o_a, o_skip, o_n2,
-    inner, small, sem,
+    groups, mine, other, o_in, o_n1, o_conv_w, o_conv_b, o_xp, o_dt, o_dtb, o_a, o_skip, o_n2, inner, small, sems
 ):
     mine, other = ready(mine, other)
     seq_size = mine.shape[0] * 2 // groups
-    core = lax.rem(lax.axis_index("dp"), 2)
     width, inner_width = inner.shape
-    rows = mine.shape[1] - 2 * LANES - 16
-    for x in range(groups // 2):
-        for source, side in ((mine, core), (other, 1 - core)):
-            g = 2 * x + side
-            at = pl.ds(pl.multiple_of(g * LANES, LANES), LANES)
-            for s in range(seq_size):
-                inner[at, tile(s)] = source[x * seq_size + s, :LANES, :].astype(F32)
-                here = pl.ds(pl.multiple_of(s * LANES + g * rows, rows), rows)
-                small[here, :] = source[x * seq_size + s, 2 * LANES : 2 * LANES + rows, :].astype(F32)
-    copy = pltpu.make_async_copy(inner, o_in.at[:, :inner_width], sem)
-    copy.start()
-    for x in range(groups // 2):
-        for side in range(2):
-            for s in range(seq_size):
-                piece = [ref[x * seq_size + s, LANES : 2 * LANES, :] for ref in (mine, other)]
-                value = jnp.where(core == side, piece[0].astype(F32), piece[1].astype(F32))
-                o_out[tile(s), tile(2 * x + side)] = value
+    rows = mine.shape[1] - LANES - 16
+    copies = []
+    for ref, x, s, g in receivers((mine, other), seq_size):
+        at = pl.ds(pl.multiple_of(g * LANES, LANES), LANES)
+        inner[at, tile(s)] = ref[x * seq_size + s, :LANES, :].astype(F32)
+        here = pl.ds(pl.multiple_of((g * seq_size + s) * rows, rows), rows)
+        small[here, :] = ref[x * seq_size + s, LANES : LANES + rows, :].astype(F32)
+        if s == seq_size - 1:
+            copies.append(pltpu.make_async_copy(inner.at[at], o_in.at[at, :inner_width], sems.at[len(copies)]))
+            copies[-1].start()
     for j in range(inner_width // LANES):
         value = from_rows(small, j, SMALL)
         for ref, first, last in (
@@ -689,13 +687,15 @@
             ref[:, tile(j)] = value[first:last]
         if j >= width // LANES:
             o_n2[:, tile(j - width // LANES)] = value[103:104]
+    sent(o_conv_w, o_conv_b, o_xp, o_dt, o_dtb, o_a, o_skip, o_n2)
     gain = jnp.zeros((16, LANES), F32)
     for source in (mine, other):
         for d in range(source.shape[0]):
-            gain = gain + source[d, 2 * LANES + rows :, :].astype(F32)
+            gain = gain + source[d, LANES + rows :, :].astype(F32)
     for j in range(width // LANES):
         o_n1[:, tile(j)] = gain[j : j + 1]
-    copy.wait()
+    for copy in copies:
+        copy.wait()
 
 
 class Held:
@@ -716,7 +716,7 @@
             one.copy.wait()
             one.done = True
     refs = tuple(one.ref for one in held)
-    return refs if len(refs) > 1 else refs[0]
+    return refs[0] if len(refs) == 1 else refs
 
 
 def sent(*held):
@@ -731,7 +731,7 @@
 
 def call(
     kernel, outs, scratch, *args, name=None, us=1, raw=(), raw_out=(), scalars=(), views=None, aliases=None, after=(),
-    vmem=60,
+    near=(), vmem=60,
 ):
     views = views or {}
     count, first_out = len(args), len(args) + len(after)
@@ -772,11 +772,11 @@
     return pl.pallas_call(
         run,
         out_shape=[jax.ShapeDtypeStruct(s, d) for s, d in outs],
-        in_specs=[IN_HBM] * first_out,
+        in_specs=[pl.BlockSpec(memory_space=pl.ANY) if i in near else IN_HBM for i in range(first_out)],
         out_specs=[IN_HBM] * len(outs),
         scratch_shapes=used + [pltpu.SemaphoreType.DMA((len(buffers),))] + scratch,
         compiler_params=pltpu.CompilerParams(vmem_limit_bytes=vmem * 1024 * 1024),
-        cost_estimate=pl.CostEstimate(flops=us * 1000, bytes_accessed=us * 1000, transcendentals=0),
+        cost_estimate=pl.CostEstimate(flops=us * 10**9 + 1000, bytes_accessed=1000, transcendentals=0),
         input_output_aliases=aliases or {},
         name=name,
     )(*args, *after)
@@ -784,12 +784,6 @@
 
 def exchange(value, axes):
     return lax.all_to_all(value, axes, 0, 0, tiled=True)
-
-
-def everywhere(value):
-    axes = ("dp", "seq")
-    count = lax.axis_size(axes)
-    return exchange(jnp.broadcast_to(value[None], (count,) + value.shape), axes)
 
 
 def own_core(value, groups, seq_size):
@@ -797,6 +791,10 @@
         [g * seq_size + s for g in range(core, groups, 2) for s in range(seq_size)] for core in range(2)
     ]
     return lax.all_to_all(value, ("dp", "seq"), 0, 0, tiled=True, axis_index_groups=peers)
+
+
+def other_core(value, groups):
+    return lax.ppermute(value, "dp", [(g, g ^ 1) for g in range(groups)])
 
 
 def body(
@@ -807,203 +805,163 @@
     inner_width = w_in.shape[1] // 2
     states = a_log.shape[1]
     rank = w_dt.shape[0]
+    taps = conv_w.shape[0]
     groups, seq_size = lax.axis_size("dp"), lax.axis_size("seq")
     rows = count * seq_size
     ext_rows = HALO + count
-    piece = inner_width // seq_size
-    copies = seq_size // H
-    tiled = piece == LANES and width == groups * LANES and copies == 1
+    tiled = inner_width == seq_size * LANES and width == groups * LANES and seq_size == H
+    peers = groups // 2 * seq_size
     line = lambda v: v.reshape(1, -1)
     seg = line(seg_start)
     n1, n2, cb, dtb, skip = (line(v) for v in (norm_one, norm_two, conv_b, dt_bias, d_skip))
     vmem, smem = pltpu.VMEM, pltpu.SMEM((count, 2 * states), F32)
     sem = pltpu.SemaphoreType.DMA
     blocks = ((count * 8, LANES), F32)
-    onward = [(i, i + 1) for i in range(seq_size - 1)]
-    cot_all = lax.all_gather(cotangent, "seq", axis=0, tiled=True)
     ends_at = states * 8
-    halo = lax.ppermute(tokens[count - HALO :], "seq", onward)
+    halo = lax.ppermute(tokens[count - HALO :], "seq", [(i, i + 1) for i in range(seq_size - 1)])
     msg, normed, inner, gate, mixed, bc, low, step_pre, s, dx, a = call(
         functools.partial(forward_kernel, seq_size),
         [
-            ((seq_size, states * 8 + 32, LANES), BF), ((count, width), BF),
-            ((ext_rows, inner_width), BF), ((count, inner_width), BF), ((count, inner_width), BF), ((count, 2 * states), F32), ((count, rank), BF),
-            ((count, inner_width), F32), blocks, blocks, ((states * 8, LANES), F32),
+            ((seq_size, states * 8 + 32, LANES), BF), ((ext_rows, width), BF),
+            ((ext_rows, inner_width), BF), ((count, inner_width), BF), ((count, inner_width), BF), ((count, 2 * states), F32),
+            ((count, rank), BF), ((count, inner_width), F32), blocks, blocks, ((states * 8, LANES), F32),
         ],
         [vmem((ext_rows, inner_width), F32), smem, sem],
         tokens, halo, n1, w_in, conv_w, cb, w_xproj.T, w_dt, dtb, a_log.T, seg,
-        name="forward", us=8,
+        name="forward", us=0, near=(1,),
     )
     msg = exchange(msg, "seq")
-    qkvg, start, ssm, normed, after = call(
+    (grad_att,) = call(
+        grad_att_kernel, [((count, width), BF)], [], cotangent, w_proj, name="grad_att", us=0
+    )
+    qkvg, start, ssm, after, gated, normed_two = call(
         middle_kernel,
         [
-            ((seq_size, count, 3 * LANES), BF), ((states * 8, LANES), F32), ((count, inner_width), F32),
-            ((count, 2 * width), BF), ((count, width), F32),
+            ((seq_size, count, 2 * LANES), BF), ((states * 8, LANES), F32), ((count, inner_width), F32),
+            ((count, width), F32), ((count, inner_width), BF), ((count, width), BF),
         ],
-        [vmem((count, inner_width), BF), vmem(*blocks)],
-        msg, a, bc, s, dx, mixed, gate, skip, tokens, w_out, n2, w_qkv, cotangent, w_proj, normed,
-        name="middle", us=8, scalars=(2,), views={0: np.s_[:, : ends_at + 16, :]},
+        [vmem(*blocks)],
+        msg, a, bc, s, dx, mixed, gate, skip, tokens, w_out, n2, w_qkv, grad_att,
+        name="middle", us=0, scalars=(2,), views={0: np.s_[:, : ends_at + 16, :]}, near=(0,),
     )
-    normed_all = lax.all_gather(normed, "seq", axis=0, tiled=True)
     qkvg = exchange(qkvg, "seq")
+    every, slope = call(
+        functools.partial(states_kernel, seq_size),
+        [(((count + 1) * states * 8, LANES), F32), ((count, inner_width), F32)],
+        [vmem((ext_rows, inner_width), F32)],
+        start, a, bc, s, dx, inner, conv_w, cb, seg, name="states", us=0, scalars=(2,),
+    )
     (back,) = call(
         attention_kernel,
         [((seq_size, count, 2 * LANES), BF)],
         [vmem((rows, LANES), BF)] * 4 + [vmem((rows, LANES), F32)] * 2,
-        qkvg, msg, name="attention", us=7,
-        views={0: np.s_[:, :, : 2 * LANES], 1: np.s_[:, ends_at + 16 :, :]},
+        qkvg, msg, name="attention", us=0, views={1: np.s_[:, ends_at + 16 :, :]}, after=(every,), near=(0,),
     )
     back_own = exchange(back, "seq")
-    out, grad_after, branch, grad_n2, grad_gate, g, adj = call(
+    out, grad_after, branch, grad_n2, grad_gate, g, adj, attended, *more = call(
         backward_kernel,
         [
             ((count, width), BF), ((count, width), F32), ((count, width), BF), ((1, width), F32),
-            ((count, inner_width), BF), blocks, ((seq_size, states * 8 + piece, LANES), BF),
-        ],
-        [vmem((inner_width, LANES), BF)],
+            ((count, inner_width), BF), blocks, ((seq_size, states * 8, LANES), BF),
+            ((count, width), BF),
+        ] + ([] if tiled else [((count, 3 * width), BF)]),
+        [],
         back_own, after, w_proj, w_qkv, n2, cotangent, w_out, gate, ssm, s, a, bc,
-        name="backward", us=7, scalars=(11,),
+        name="backward", us=0, scalars=(11,), near=(0,),
     )
     adj = exchange(adj, "seq")
-    branch_all = lax.all_gather(branch, "seq", axis=0, tiled=True)
-    every, slope = call(
-        functools.partial(states_kernel, seq_size),
-        [(((count + 1) * states * 8, LANES), F32), ((count, inner_width), F32)],
-        [vmem((ext_rows, inner_width), F32)],
-        start, a, bc, s, dx, inner, conv_w, cb, seg, name="states", us=6, scalars=(2,),
+    between = ()
+    if tiled:
+        normed_two_all = lax.all_gather(normed_two, "seq", axis=0, tiled=True)
+        keep, send = call(
+            functools.partial(partials_kernel, seq_size), [((peers, 2 * LANES + HD, LANES), BF)] * 2,
+            [vmem((inner_width, width), F32), vmem((width, inner_width), F32), vmem((width, width), F32)],
+            gated, branch, normed, grad_gate, attended, cotangent, name="partials", us=0, views={2: np.s_[HALO:, :]},
+        )
+        add = lambda *parts: sum(part.astype(F32) for part in parts).astype(BF)
+        received = other_core(send, groups)
+        across = add(keep[seq_size:], received[seq_size:])
+        across = lax.ppermute(across, "dp", [(g, g ^ 2) for g in range(groups)])
+        part = add(keep[:seq_size], received[:seq_size], across)
+        between = (part,)
+        part = exchange(part, "seq")
+    gs, ai, grad_bc, grad_a = call(
+        functools.partial(adjoint_kernel, seq_size),
+        [blocks, blocks, ((count, rank + 2 * states), F32), ((states * 8, LANES), F32)],
+        [vmem(((count + 1) * states * 8, LANES), F32), vmem((count * 2 * states, LANES), F32), sem((8,))],
+        adj, msg, a, bc, s, dx, g, every, name="adjoint", us=0, raw=(7,), scalars=(3,), near=(0,),
+        views={1: np.s_[:, ends_at : ends_at + 16, :]}, after=between,
     )
-    gate_views = {0: np.s_[:, :width], 1: np.s_[:, ends_at:, :]}
-    if tiled:
-        (head,) = call(
-            functools.partial(head_products_kernel, width), [((groups, 4 * HD, LANES), BF)], [],
-            back, cot_all, normed_all, name="head_products", us=3,
-        )
-        (early,) = call(
-            functools.partial(gate_products_kernel, piece), [((groups, 4 * HD + LANES, LANES), BF)], [],
-            normed_all, adj, head, name="gate_products", us=2, after=(every,), views=gate_views,
-        )
-    else:
-        proj_part, qkv_part = call(
-            functools.partial(head_products_kernel, width), [((HD, width), BF), ((3 * HD, width), BF)], [],
-            back, cot_all, normed_all, name="head_products", us=3,
-        )
-        (gate_part,) = call(
-            functools.partial(gate_products_kernel, piece), [((piece, width), BF)], [],
-            normed_all, adj, name="gate_products", us=2, views=gate_views,
-        )
-        head = jnp.concatenate([proj_part, qkv_part], axis=0)
-        if copies > 1:
-            own = 4 * HD // copies
-            head = lax.dynamic_slice_in_dim(head, lax.axis_index("seq") % copies * own, own, 0)
-        early = jnp.concatenate([v.reshape(groups, -1, LANES) for v in (head, gate_part)], axis=1)
-    adjoint_in = (adj, msg, a, bc, s, dx, g, mixed, step_pre, low, w_dt, w_xproj.T, inner, slope, conv_w, skip, seg,
-                  grad_n2, every)
-    tail, grad_inner = call(
-        functools.partial(adjoint_kernel, seq_size),
-        [((seq_size, piece + HALO + SMALL * 8 // seq_size, LANES), BF), ((ext_rows, inner_width), BF)],
-        [
-            vmem(((count + 1) * states * 8, LANES), F32), vmem(*blocks), vmem(*blocks),
-            vmem((count * 2 * states, LANES), F32), vmem((SMALL * 8, LANES), F32),
-            vmem((ext_rows, inner_width), F32), vmem((ext_rows, inner_width), F32), sem((8,)),
-        ],
-        *adjoint_in, name="adjoint", us=15, raw=(len(adjoint_in) - 1,), scalars=(3,),
-        views={0: np.s_[:, :ends_at, :], 1: np.s_[:, ends_at : ends_at + 16, :]},
+    small_rows = SMALL * 8 // (groups * seq_size)
+    *sums, small, grad_inner = call(
+        functools.partial(inner_kernel, seq_size),
+        ([((peers, LANES + small_rows, LANES), BF)] * 2 if tiled else [((width, inner_width), F32), ((SMALL * 8, LANES), F32)])
+        + [((ext_rows, inner_width), BF)],
+        ([vmem((SMALL * 8, LANES), F32)] if tiled else [])
+        + [vmem((ext_rows, inner_width), F32), vmem((ext_rows, inner_width), F32), vmem((width, inner_width), F32)],
+        gs, ai, g, mixed, step_pre, low, w_dt, grad_bc, grad_a, w_xproj.T, inner, slope, conv_w, skip, seg, normed, grad_n2,
+        name="inner", us=0,
     )
-    early = exchange(early, "dp")
-    (early,) = call(
-        sum_kernel, [(early.shape[1:], BF)], [], early, name="early_sum", us=1, after=(grad_inner,)
-    )
-    early = lax.all_gather(early, ("dp", "seq"))
-    tail = exchange(tail, "seq")
     grad_tokens, grad_halo, grad_n1 = call(
         tokens_kernel, [((count, width), F32), ((8, width), F32), ((16, LANES), BF)], [],
-        grad_inner, w_in, grad_gate, tokens, halo, n1, grad_after, name="tokens", us=4,
+        grad_inner, w_in, grad_gate, tokens, halo, n1, grad_after, name="tokens", us=0,
     )
     returned = lax.ppermute(grad_halo, "seq", [(i + 1, i) for i in range(seq_size - 1)])
     grad_tokens = grad_tokens.at[count - 8 :].add(returned)
-    per = SMALL * 8 // seq_size
-    late_views = {0: np.s_[:, :, 2 * LANES :], 2: np.s_[:, :width]}
+    flat = lambda v: v.reshape(-1)
     if tiled:
+        late = add(sums[0], other_core(small, groups))
+        late = own_core(late, groups, seq_size)
+        keep, send = call(
+            head_products_kernel, [((groups // 2, 3 * HD, LANES), BF)] * 2, [vmem((width, LANES), F32)] * 2,
+            normed_two_all, back, name="head_products", us=0, after=(grad_n1,),
+        )
+        head, far = call(
+            head_middle_kernel, [((3 * HD, LANES), BF)] * 2, [], keep, other_core(send, groups), name="head_middle", us=0,
+            near=(1,),
+        )
+        heads = [lax.ppermute(far, "dp", [(g, g ^ 2) for g in range(groups)])]
+        (early,) = call(
+            early_sum_kernel, [((part.shape[1] + head.shape[0], LANES), BF)], [], part, head, *heads,
+            name="early_sum", us=0, after=(grad_n1,), near=(0, 2),
+        )
+        early = lax.all_gather(early, ("dp", "seq"))
         (late,) = call(
-            functools.partial(late_products_kernel, piece), [((groups, 2 * LANES + per // groups, LANES), BF)], [],
-            qkvg, branch_all, normed_all, tail, name="late_products", us=2, views=late_views,
-        )
-    else:
-        in_part, out_part, small = call(
-            functools.partial(late_products_kernel, piece), [((piece, width), BF), ((piece, width), BF), ((per, LANES), BF)],
-            [], qkvg, branch_all, normed_all, tail, name="late_products", us=2, views=late_views,
-        )
-        late = jnp.concatenate([v.reshape(groups, -1, LANES) for v in (in_part, out_part, small)], axis=1)
-    late = exchange(late, "dp")
-    copies_out = groups // 2 * seq_size if tiled else 1
-    (late,) = call(
-        sum_and_spread_kernel, [((copies_out, late.shape[1] + 16, LANES), BF)], [], late, grad_n1, name="late_sum", us=1
-    )
-    if tiled:
-        grad_w_proj, grad_w_qkv, half = call(
-            functools.partial(early_assembly_kernel, groups),
-            [((width, width), F32), ((width, 3 * width), F32), ((width, 2 * inner_width), F32)],
-            [vmem((width, inner_width), F32), sem],
-            early, name="early_assembly", us=6, raw_out=(2,),
+            sum_and_spread_kernel, [((peers, late.shape[1] + 16, LANES), BF)], [], late, grad_n1, name="late_sum", us=0,
+            near=(0,),
         )
         mine = own_core(late, groups, seq_size)
-        mine, half, grad_tokens = lax.optimization_barrier((mine, half, grad_tokens))
-        other = lax.ppermute(mine, "dp", [(g, g ^ 1) for g in range(groups)])
+        mine, grad_tokens = lax.optimization_barrier((mine, grad_tokens))
         row = lambda n: ((n, inner_width), F32)
-        grad_w_in, grad_w_out, g_n1, g_conv_w, g_conv_b, g_xp, g_dt, g_dtb, g_a, g_skip, g_n2 = call(
+        half, g_n1, g_conv_w, g_conv_b, g_xp, g_dt, g_dtb, g_a, g_skip, g_n2 = call(
             functools.partial(late_assembly_kernel, groups),
             [
-                ((width, 2 * inner_width), F32), ((inner_width, width), F32), ((1, width), F32), row(conv_w.shape[0]),
-                row(1), row(2 * states + rank), row(rank), row(1), row(states), row(1), ((1, width), F32),
+                ((width, 2 * inner_width), F32), ((1, width), F32), row(taps), row(1), row(2 * states + rank), row(rank),
+                row(1), row(states), row(1), ((1, width), F32),
             ],
-            [vmem((width, inner_width), F32), vmem((SMALL * 8, LANES), F32), sem],
-            mine, other, half, name="late_assembly", us=4,
-            raw=(2,), raw_out=(0,), aliases={2: 0},
-        )
-        flat = lambda v: v.reshape(-1)
-        return (out, grad_tokens, flat(g_n1), grad_w_in, g_conv_w, flat(g_conv_b), g_xp.T, g_dt, flat(g_dtb), g_a.T,
-                flat(g_skip), grad_w_out, flat(g_n2), grad_w_qkv, grad_w_proj)
-    late = everywhere(late[0])
-
-    def whole(gathered, first, last):
-        part = gathered.reshape(groups, seq_size, -1, LANES)[:, :, first:last]
-        return part.swapaxes(0, 1).reshape(seq_size, -1)
-
-    def cut(sizes):
-        ends, total = [], 0
-        for n in sizes:
-            ends.append((total, total + n // LANES // groups))
-            total = ends[-1][1]
-        return ends
-
-    at_head, at_gate = cut((4 * HD * width // copies, piece * width))
-    at_in, at_out, at_small = cut((piece * width, piece * width, per * LANES))
-    heads = whole(early, *at_head).reshape(H, 4, HD, width)
-    grad_w_proj = heads[:, 0].reshape(H * HD, width).astype(F32)
-    grad_w_qkv = heads[:, 1:].transpose(3, 1, 0, 2).reshape(width, 3 * width).astype(F32)
-    grad_w_out = whole(late, *at_out).reshape(inner_width, width).astype(F32)
-    grad_w_in = jnp.concatenate(
-        [whole(late, *at_in).reshape(inner_width, width), whole(early, *at_gate).reshape(inner_width, width)], axis=0
-    ).T.astype(F32)
-    small = whole(late, *at_small).reshape(SMALL, inner_width).astype(F32)
-    return (
-        out,
-        grad_tokens,
-        jnp.sum(late[:, -16:].reshape(groups * seq_size, -1)[:, :width].astype(F32), axis=0),
-        grad_w_in,
-        small[96:100],
-        small[100],
-        small[:64].T,
-        small[64:96],
-        small[101],
-        small[104:120].T,
-        small[102],
-        grad_w_out,
-        small[103, width:],
-        grad_w_qkv,
-        grad_w_proj,
-    )
+            [vmem((width, inner_width), F32), vmem((SMALL * 8, LANES), F32), sem((4,))],
+            mine, other_core(mine, groups), name="late_assembly", us=0, raw_out=(0,), near=(0, 1),
+        )
+        whole = [((inner_width, width), F32), ((width, width), F32), ((width, 3 * width), F32)]
+        grad_w_out, grad_w_proj, grad_w_qkv, grad_w_in = call(
+            functools.partial(early_assembly_kernel, groups),
+            whole + [((width, 2 * inner_width), F32)],
+            [vmem(early.shape, BF)] + [vmem(*v) for v in whole] + [vmem((width, inner_width), F32), sem((4,)), sem((16,))],
+            early, half, name="early_assembly", us=0, raw=(0, 1), raw_out=(0, 1, 2, 3), aliases={1: 3},
+        )
+        g_xp, g_a, g_n1, g_n2 = g_xp.T, g_a.T, flat(g_n1), flat(g_n2)
+    else:
+        (grad_qkv,) = more
+        small = small.reshape(SMALL, inner_width)
+        g_n1 = flat(grad_n1[: width // LANES].astype(F32))
+        both = jnp.concatenate([sums[0], dot_tn(normed[HALO:], grad_gate)], axis=1)
+        grad_w_in, grad_w_out, grad_w_qkv, grad_w_proj, small, g_n1 = lax.psum(
+            (both, dot_tn(gated, branch), dot_tn(normed_two, grad_qkv), dot_tn(attended, cotangent), small, g_n1), ("dp", "seq")
+        )
+        g_xp, g_dt, g_conv_w, g_conv_b, g_dtb = small[:64].T, small[64:96], small[96:100], small[100], small[101]
+        g_skip, g_n2, g_a = small[102], small[103, width:], small[104:120].T
+    return (out, grad_tokens, g_n1, grad_w_in, g_conv_w, flat(g_conv_b), g_xp, g_dt, flat(g_dtb), g_a, flat(g_skip),
+            grad_w_out, g_n2, grad_w_qkv, grad_w_proj)
 
 
 def solution(mesh):

time: 264 us -> 246 us (0.932)
  blocking collectives: 64.5 us -> 42.9 us
  other arithmetic: 1.33 us -> 4.79 us
    all_to_all x3 -> x1, blocking collectives: 64.5 us -> 17.6 us  [exchange(): return lax.all_to_all(value, axes, 0, 0, tiled=True)]
    all_to_all x0 -> x1, blocking collectives: none -> 25.2 us  [own_core(): lax.all_to_all(value, ('dp', 'seq'), 0, 0, tiled=True, axis_index_groups=...]
    ppermute x2 -> x7, waiting for transfers between devices: 3.9 us -> 20.8 us  [the longest x1 9.83 us: body(): across = lax.ppermute(across, 'dp', [(g, g ^ 2) for g in range(groups)])]
    ppermute x1, waiting for transfers between devices: 34.6 us -> 24.8 us  [body(): lax.ppermute(grad_halo, 'seq', [(i + 1, i) for i in range(seq_size - 1)])]
    all_to_all x4, waiting for transfers between devices: 18.4 us -> 8.61 us  [exchange(): return lax.all_to_all(value, axes, 0, 0, tiled=True)]
    ppermute x2 -> x7, starting transfers between devices: 4.92 us -> 12.7 us  [the longest x4 7.06 us: other_core(): return lax.ppermute(value, 'dp', [(g, g ^ 1) for g in range(groups)])]
    all_to_all x4, starting transfers between devices: 27.5 us -> 22.5 us  [exchange(): return lax.all_to_all(value, axes, 0, 0, tiled=True)]
    convert_element_type x0 -> x3, other arithmetic: none -> 3.47 us  [body(): add = lambda *parts: sum((part.astype(F32) for part in parts)).astype(BF)]
  transfers between devices with their start and end apart: 12 -> 15, of which waited for: 5 -> 11; matrix products, arithmetic and copies ran while one was open for 1% -> 1% of each run, Pallas kernels for 28% -> 17%
where the time goes in v2:
time: 246 us; the launch traced here: 245 us
  Pallas kernels  78.7 us (32%)
  waiting for transfers between devices  56.1 us (23%)
  blocking collectives  42.9 us (17%)
  starting transfers between devices  42.8 us (17%)
  between operations  14.2 us (6%)
  local copies, waits for them, and re-layouts  5.22 us (2%)
  other arithmetic  4.79 us (2%)
    pallas_call x16, Pallas kernels, call(): pl.pallas_call(run, out_shape=[jax.ShapeDtypeStruct(s, d) for s, d in out...  78.7 us
    all_to_all x1, blocking collectives, own_core(): lax.all_to_all(value, ('dp', 'seq'), 0, 0, tiled=True, axis_index_groups=...  25.2 us
    ppermute x1, waiting for transfers between devices, body(): lax.ppermute(grad_halo, 'seq', [(i + 1, i) for i in range(seq_size - 1)])  24.8 us
    all_to_all x4, starting transfers between devices, exchange(): return lax.all_to_all(value, axes, 0, 0, tiled=True)  22.5 us
    all_to_all x1, blocking collectives, exchange(): return lax.all_to_all(value, axes, 0, 0, tiled=True)  17.6 us
    ppermute x1, waiting for transfers between devices, body(): across = lax.ppermute(across, 'dp', [(g, g ^ 2) for g in range(groups)])  9.83 us
    all_to_all x4, waiting for transfers between devices, exchange(): return lax.all_to_all(value, axes, 0, 0, tiled=True)  8.61 us
    ppermute x4, waiting for transfers between devices, other_core(): return lax.ppermute(value, 'dp', [(g, g ^ 1) for g in range(groups)])  7.74 us
  transfers between devices with their start and end apart: 15, of which 11 were waited for; matrix products, arithmetic and copies ran while one was open for 1% of the time, Pallas kernels for 17%

profile of v2, /device:TPU:13, one launch (start us, length us, event | category | flops | bytes accessed | tf_op | source)
XLA Modules:
  0.0 244.7 jit_solution(12233084608024444584)
XLA Ops:
  7.9 3.1 %collective-permute-start = (bf16[16,512]{1,0:T(8,128)(2,1)S(1)}, bf16[16,512]{1,0:T(8,128)(2,1)S(1)}, u32[]{:S(2)}, u32[]{:S(2)}) collective-permute-start(bf16[16,512]{1,0:T(8,128)(2,1)S(1)} %slice.34), channel_id=1, source_target_pairs={{0,1},{1,2},{2,3},{3,4},{4,5},{5,6},{6,7},{8,9},{9,10},{10,11},{11... | collective-permute-start | bytes 49160 | tf_op jit(solution)/shard_map/ppermute | solution.py:821
  11.0 1.3 collective-permute-done.refs_1_.refs_4_
  13.0 7.4 %forward.1 = (bf16[8,160,128]{2,1,0:T(8,128)(2,1)}, bf16[144,512]{1,0:T(8,128)(2,1)}, bf16[144,1024]{1,0:T(8,128)(2,1)}, bf16[128,1024]{1,0:T(8,128)(2,1)}, bf16...) custom-call(bf16[128,512]{1,0:T(8,128)(2,1)} %refs_3_.5, ...), custom_call_target="tpu_custom_call" | custom-call | flops 1000 | bytes 1000 | tf_op jit(solution)/shard_map/forward/pallas_call | solution.py:772
  20.4 5.7 %all-to-all-start = ((bf16[8,160,128]{2,1,0:T(8,128)(2,1)}), bf16[8,160,128]{2,1,0:T(8,128)(2,1)S(1)}, u32[]{:S(2)}, u32[]{:S(2)}) async-start(bf16[8,160,128]{2,1,0:T(8,128)(2,1)} %get-tuple-element.86), calls=%async_computation | async-start | bytes 655360 | tf_op jit(solution)/shard_map/all_to_all | solution.py:786
  26.1 2.1 grad_att.1.refs_12_
  28.2 4.8 %all-to-all-done.refs_0_.refs_1_ = bf16[8,160,128]{2,1,0:T(8,128)(2,1)S(1)} async-done(((bf16[8,160,128]{2,1,0:T(8,128)(2,1)}), bf16[8,160,128]{2,1,0:T(8,128)(2,1)S(1)}, u32[]{:S(2)}, u32[]{:S(2)}) %all-to-all-start) | async-done | bytes 327712 | tf_op jit(solution)/shard_map/all_to_all | solution.py:786
  33.0 0.7 copy-done
  33.7 6.4 %middle.1 = (bf16[8,128,256]{2,1,0:T(8,128)(2,1)}, f32[128,128]{1,0:T(8,128)}, f32[128,1024]{1,0:T(8,128)}, f32[128,512]{1,0:T(8,128)}, bf16[128,1024]{1,0:T(8,128)(2,1)}, /*index=5*/bf16[128,512]{1,0:T(8,128)(2,1)}) custom-call(bf16[8,160,128]{2,1,0:T(8,128)(2,1)} %copy-done, f32[128,128]{1,0:T(8,128)} %get-tuple-element.87.refs_1_.refs_10_.refs_2_, ...), custom_call_target="tpu_custom_call" | custom-call | flops 1000 | bytes 1000 | tf_op jit(solution)/shard_map/middle/pallas_call | solution.py:772
  40.1 6.4 %all-to-all-start.1 = ((bf16[8,128,256]{2,1,0:T(8,128)(2,1)}), bf16[8,128,256]{2,1,0:T(8,128)(2,1)S(1)}, u32[]{:S(2)}, u32[]{:S(2)}) async-start(bf16[8,128,256]{2,1,0:T(8,128)(2,1)} %get-tuple-element.93), calls=%async_computation.1 | async-start | bytes 1048576 | tf_op jit(solution)/shard_map/all_to_all | solution.py:786
  46.5 7.6 %states.1 = (f32[16512,128]{1,0:T(8,128)}, f32[128,1024]{1,0:T(8,128)}) custom-call(f32[128,128]{1,0:T(8,128)} %get-tuple-element.94.refs_0_, f32[128,128]{1,0:T(8,128)} %get-tuple-element.87.refs_1_.refs_10_.refs_2_, f32[128,32]{1,0:T(8,128)} %get-tuple-element.88.refs_2_.refs_11_.refs_3_, f32[1024,128]{1,0:T(8,128)} %get-tuple-element.89.refs_3_.refs_9_.refs_4_, ...), custom_call_target="tpu_custom_call" | custom-call | flops 1000 | bytes 1000 | tf_op jit(solution)/shard_map/states/pallas_call | solution.py:772
  54.1 3.8 %all-to-all-done.1.refs_0_ = bf16[8,128,256]{2,1,0:T(8,128)(2,1)S(1)} async-done(((bf16[8,128,256]{2,1,0:T(8,128)(2,1)}), bf16[8,128,256]{2,1,0:T(8,128)(2,1)S(1)}, u32[]{:S(2)}, u32[]{:S(2)}) %all-to-all-start.1) | async-done | bytes 524320 | tf_op jit(solution)/shard_map/all_to_all | solution.py:786
  57.9 0.8 copy-done.3
  58.7 7.4 %attention.1.refs_1_ = bf16[8,128,256]{2,1,0:T(8,128)(2,1)} custom-call(bf16[8,128,256]{2,1,0:T(8,128)(2,1)} %copy-done.3, bf16[8,160,128]{2,1,0:T(8,128)(2,1)} %copy-done, f32[16512,128]{1,0:T(8,128)} %get-tuple-element.96.refs_2_.refs_7_), custom_call_target="tpu_custom_call" | custom-call | flops 1000 | bytes 1000 | tf_op jit(solution)/shard_map/attention/pallas_call | solution.py:772
  66.1 17.6 %all_to_all.35.refs_0_ = bf16[8,128,256]{2,1,0:T(8,128)(2,1)} all-to-all(bf16[8,128,256]{2,1,0:T(8,128)(2,1)} %attention.1.refs_1_), channel_id=1, replica_groups=mesh['dp'=4,'seq'=8] {'seq'}, dimensions={0} | all-to-all | bytes 1048576 | tf_op jit(solution)/shard_map/all_to_all | solution.py:786
  83.8 6.0 %backward.1 = (bf16[128,512]{1,0:T(8,128)(2,1)}, f32[128,512]{1,0:T(8,128)}, bf16[128,512]{1,0:T(8,128)(2,1)}, f32[1,512]{1,0:T(1,128)}, bf16[128,1024]{1,0:T(8,...) custom-call(bf16[8,128,256]{2,1,0:T(8,128)(2,1)} %all_to_all.35.refs_0_, ...), custom_call_target="tpu_custom_call" | custom-call | flops 1000 | bytes 1000 | tf_op jit(solution)/shard_map/backward/pallas_call | solution.py:772
  89.7 3.8 %partials.1 = (bf16[16,320,128]{2,1,0:T(8,128)(2,1)}, bf16[16,320,128]{2,1,0:T(8,128)(2,1)}) custom-call(bf16[128,1024]{1,0:T(8,128)(2,1)} %get-tuple-element.102.refs_0_, bf16[128,512]{1,0:T(8,128)(2,1)} %get-tuple-element.103.refs_1_, bf16[144,512]{1,0:T(8,128)(2,1)} %get-tuple-element.104.refs_2_.refs_15_, ...), custom_call_target="tpu_custom_call" | custom-call | flops 1000 | bytes 1000 | tf_op jit(solution)/shard_map/partials/pallas_call | solution.py:772
  93.6 2.5 %collective-permute-start.1 = (bf16[16,320,128]{2,1,0:T(8,128)(2,1)}, bf16[16,320,128]{2,1,0:T(8,128)(2,1)S(1)}, u32[]{:S(2)}, u32[]{:S(2)}) collective-permute-start(bf16[16,320,128]{2,1,0:T(8,128)(2,1)} %get-tuple-element.108), channel_id=1, source_target_pairs={{0,8},{8,0},{16,24},{24,16},{1,9},{9,1},{17,25},{25,17},{2,10},{10... | collective-permute-start | bytes 3932168 | tf_op jit(solution)/shard_map/ppermute | solution.py:797
  96.1 2.9 %collective-permute-done.1 = bf16[16,320,128]{2,1,0:T(8,128)(2,1)S(1)} collective-permute-done((bf16[16,320,128]{2,1,0:T(8,128)(2,1)}, bf16[16,320,128]{2,1,0:T(8,128)(2,1)S(1)}, u32[]{:S(2)}, u32[]{:S(2)}) %collective-permute-start.1) | collective-permute-done | bytes 1310752 | tf_op jit(solution)/shard_map/ppermute | solution.py:797
  99.0 2.2 add_convert_fusion.2
  101.2 1.2 collective-permute-start.2
  102.4 5.2 %all-to-all-start.3 = ((bf16[8,128,128]{2,1,0:T(8,128)(2,1)}), bf16[8,128,128]{2,1,0:T(8,128)(2,1)S(1)}, u32[]{:S(2)}, u32[]{:S(2)}) async-start(bf16[8,128,128]{2,1,0:T(8,128)(2,1)} %get-tuple-element.100), calls=%async_computation.3 | async-start | bytes 524288 | tf_op jit(solution)/shard_map/all_to_all | solution.py:786
  107.6 9.8 %collective-permute-done.2 = bf16[8,320,128]{2,1,0:T(8,128)(2,1)S(1)} collective-permute-done((bf16[8,320,128]{2,1,0:T(8,128)(2,1)}, bf16[8,320,128]{2,1,0:T(8,128)(2,1)S(1)}, u32[]{:S(2)}, u32[]{:S(2)}) %collective-permute-start.2) | collective-permute-done | bytes 655392 | tf_op jit(solution)/shard_map/ppermute | solution.py:884
  117.4 1.1 add_convert_fusion.1.refs_8_
  118.5 5.3 %all-to-all-start.6 = ((bf16[8,320,128]{2,1,0:T(8,128)(2,1)}), bf16[8,320,128]{2,1,0:T(8,128)(2,1)S(1)}, u32[]{:S(2)}, u32[]{:S(2)}) async-start(bf16[8,320,128]{2,1,0:T(8,128)(2,1)} %add_convert_fusion.1.refs_8_), calls=%async_computation.6 | async-start | bytes 1310720 | tf_op jit(solution)/shard_map/all_to_all | solution.py:786
  123.8 11.4 %adjoint.1 = (f32[1024,128]{1,0:T(8,128)}, f32[1024,128]{1,0:T(8,128)}, f32[128,64]{1,0:T(8,128)}, f32[128,128]{1,0:T(8,128)}) custom-call(bf16[8,128,128]{2,1,0:T(8,128)(2,1)} %copy-done.5, bf16[8,160,128]{2,1,0:T(8,128)(2,1)} %copy-done, f32[128,128]{1,0:T(8,128)} %get-tuple-element.87.refs_1_.refs_10_.refs_2_, ...), custom_call_target="tpu_custom_call" | custom-call | flops 1000 | bytes 1000 | tf_op jit(solution)/shard_map/adjoint/pallas_call | solution.py:772
  135.3 6.0 %inner.1 = (bf16[16,160,128]{2,1,0:T(8,128)(2,1)}, bf16[16,160,128]{2,1,0:T(8,128)(2,1)}, bf16[144,1024]{1,0:T(8,128)(2,1)}) custom-call(f32[1024,128]{1,0:T(8,128)} %get-tuple-element.109.refs_0_, f32[1024,128]{1,0:T(8,128)} %get-tuple-element.110.refs_1_, f32[1024,128]{1,0:T(8,128)} %get-tuple-element.101.refs_6_.refs_2_, ...), custom_call_target="tpu_custom_call" | custom-call | flops 1000 | bytes 1000 | tf_op jit(solution)/shard_map/inner/pallas_call | solution.py:772
  141.2 3.5 %tokens.1 = (f32[128,512]{1,0:T(8,128)}, f32[8,512]{1,0:T(8,128)}, bf16[16,128]{1,0:T(8,128)(2,1)}) custom-call(bf16[144,1024]{1,0:T(8,128)(2,1)} %get-tuple-element.119.refs_0_, bf16[512,2048]{1,0:T(8,128)(2,1)} %refs_1_.3, bf16[128,1024]{1,0:T(8,128)(2,1)} %get-tuple-element.105.refs_3_.refs_2_, bf16[128,512]{1,0:T(8,128)(2,1)} %refs_3_.5, ...), custom_call_target="tpu_custom_call" | custom-call | flops 1000 | bytes 1000 | tf_op jit(solution)/shard_map/tokens/pallas_call | solution.py:772
  144.7 1.8 all-gather.4.cloned.1.call-done.refs_0_
  146.5 3.0 %head_products.1 = (bf16[2,192,128]{2,1,0:T(8,128)(2,1)}, bf16[2,192,128]{2,1,0:T(8,128)(2,1)}) custom-call(bf16[1024,512]{1,0:T(8,128)(2,1)} %all-gather.4.cloned.1.call-done.refs_0_, bf16[8,128,256]{2,1,0:T(8,128)(2,1)} %attention.1.refs_1_, bf16[16,128]{1,0:T(8,128)(2,1)} %get-tuple-element.121.refs_1_.refs_2_.refs_3_), custom_call_target="tpu_custom_call" | custom-call | flops 1000 | bytes 1000 | tf_op jit(solution)/shard_map/head_products/pallas_call | solution.py:772
  149.5 1.3 collective-permute-start.6
  150.8 1.2 collective-permute-done.6.refs_1_
  152.6 1.6 head_middle.1
  154.2 1.3 collective-permute-start.7
  155.5 1.9 collective-permute-done.7.refs_2_
  158.3 1.9 early_sum.1
  160.2 1.6 collective-permute-start.3
  161.7 1.7 collective-permute-done.3
  163.6 25.2 %all_to_all.36.refs_0_ = bf16[16,160,128]{2,1,0:T(8,128)(2,1)} all-to-all(bf16[16,160,128]{2,1,0:T(8,128)(2,1)S(1)} %add_convert_fusion), channel_id=1, replica_groups={{0,1,2,3,4,5,6,7,16,17,18,19,20,21,22,23},{8,9,10,11,12,13,14,15,24,25,..., dimensions={0} | all-to-all | bytes 1310720 | tf_op jit(solution)/shard_map/all_to_all | solution.py:793
  188.9 2.1 late_sum.1
  191.0 5.4 %all-to-all-start.5 = ((bf16[16,176,128]{2,1,0:T(8,128)(2,1)}), bf16[16,176,128]{2,1,0:T(8,128)(2,1)S(1)}, u32[]{:S(2)}, u32[]{:S(2)}) async-start(bf16[16,176,128]{2,1,0:T(8,128)(2,1)} %late_sum.1), calls=%async_computation.5 | async-start | bytes 1441792 | tf_op jit(solution)/shard_map/all_to_all | solution.py:793
  196.3 2.2 collective-permute-start.4
  198.5 24.8 %collective-permute-done.4 = f32[8,512]{1,0:T(8,128)S(1)} collective-permute-done((f32[8,512]{1,0:T(8,128)S(1)}, f32[8,512]{1,0:T(8,128)S(1)}, u32[]{:S(2)}, u32[]{:S(2)}) %collective-permute-start.4) | collective-permute-done | bytes 16416 | tf_op jit(solution)/shard_map/ppermute | solution.py:909
  223.3 1.3 add_dynamic-update-slice_fusion
  224.7 1.7 collective-permute-start.5
  226.4 2.0 collective-permute-done.5.refs_1_
  228.4 0.9 copy-done.6
  229.2 3.6 %late_assembly.1 = (f32[512,2048]{1,0:T(8,128)}, f32[1,512]{1,0:T(1,128)}, f32[4,1024]{1,0:T(4,128)}, f32[1,1024]{1,0:T(1,128)}, f32[64,1024]{1,0:T(8,128)}, /*i...) custom-call(bf16[16,176,128]{2,1,0:T(8,128)(2,1)} %copy-done.1, ...), custom_call_target="tpu_custom_call" | custom-call | flops 1000 | bytes 1000 | tf_op jit(solution)/shard_map/late_assembly/pallas_call | solution.py:772
  232.9 4.9 %early_assembly.1 = (f32[1024,512]{1,0:T(8,128)}, f32[512,512]{1,0:T(8,128)}, f32[512,1536]{1,0:T(8,128)}, f32[512,2048]{1,0:T(8,128)}) custom-call(bf16[32,512,128]{2,1,0:T(8,128)(2,1)} %bitcast.16, f32[512,2048]{1,0:T(8,128)} %get-tuple-element.132.refs_1_), custom_call_target="tpu_custom_call", output_to_operand_aliasing={{3}: (1, {})} | custom-call | flops 1000 | bytes 1000 | tf_op jit(solution)/shard_map/early_assembly/pallas_call | solution.py:772
  (33 shorter events, 3.1 us)
Async XLA Ops:
  7.9 4.5 %collective-permute-start = (bf16[16,512]{1,0:T(8,128)(2,1)S(1)}, bf16[16,512]{1,0:T(8,128)(2,1)S(1)}, u32[]{:S(2)}, u32[]{:S(2)}) collective-permute-start(bf16[16,512]{1,0:T(8,128)(2,1)S(1)} %slice.34), channel_id=1, source_target_pairs={{0,1},{1,2},{2,3},{3,4},{4,5},{5,6},{6,7},{8,9},{9,10},{10,11},{11... | collective-permute-start | bytes 49160 | tf_op jit(solution)/shard_map/ppermute | solution.py:821
  12.4 0.6 copy-start.9
  20.4 12.6 %all-to-all-start = ((bf16[8,160,128]{2,1,0:T(8,128)(2,1)}), bf16[8,160,128]{2,1,0:T(8,128)(2,1)S(1)}, u32[]{:S(2)}, u32[]{:S(2)}) async-start(bf16[8,160,128]{2,1,0:T(8,128)(2,1)} %get-tuple-element.86), calls=%async_computation | async-start | bytes 655360 | tf_op jit(solution)/shard_map/all_to_all | solution.py:786
  33.0 0.7 copy-start
  40.1 17.8 %all-to-all-start.1 = ((bf16[8,128,256]{2,1,0:T(8,128)(2,1)}), bf16[8,128,256]{2,1,0:T(8,128)(2,1)S(1)}, u32[]{:S(2)}, u32[]{:S(2)}) async-start(bf16[8,128,256]{2,1,0:T(8,128)(2,1)} %get-tuple-element.93), calls=%async_computation.1 | async-start | bytes 1048576 | tf_op jit(solution)/shard_map/all_to_all | solution.py:786
  46.5 100.0 %all-gather.4.cloned.1.call-start = ((), (), s32[]{:S(2)}) async-start(), calls=%async_computation.7 | async-start | bytes 1179648 | tf_op jit(solution)/shard_map/all_gather | solution.py:875
  57.9 0.8 copy-start.3
  93.6 5.4 %collective-permute-start.1 = (bf16[16,320,128]{2,1,0:T(8,128)(2,1)}, bf16[16,320,128]{2,1,0:T(8,128)(2,1)S(1)}, u32[]{:S(2)}, u32[]{:S(2)}) collective-permute-start(bf16[16,320,128]{2,1,0:T(8,128)(2,1)} %get-tuple-element.108), channel_id=1, source_target_pairs={{0,8},{8,0},{16,24},{24,16},{1,9},{9,1},{17,25},{25,17},{2,10},{10... | collective-permute-start | bytes 3932168 | tf_op jit(solution)/shard_map/ppermute | solution.py:797
  99.0 18.5 %copy-start.4 = (bf16[16,320,128]{2,1,0:T(8,128)(2,1)S(1)}, bf16[16,320,128]{2,1,0:T(8,128)(2,1)}, u32[]{:S(2)}) copy-start(bf16[16,320,128]{2,1,0:T(8,128)(2,1)} %get-tuple-element.107) | copy-start | bytes 3932164
  101.2 16.3 %collective-permute-start.2 = (bf16[8,320,128]{2,1,0:T(8,128)(2,1)}, bf16[8,320,128]{2,1,0:T(8,128)(2,1)S(1)}, u32[]{:S(2)}, u32[]{:S(2)}) collective-permute-start(bf16[8,320,128]{2,1,0:T(8,128)(2,1)} %add_convert_fusion.2), channel_id=1, source_target_pairs={{0,16},{8,24},{16,0},{24,8},{1,17},{9,25},{17,1},{25,9},{2,18},{10... | collective-permute-start | bytes 1966088 | tf_op jit(solution)/shard_map/ppermute | solution.py:884
  102.4 16.1 %all-to-all-start.3 = ((bf16[8,128,128]{2,1,0:T(8,128)(2,1)}), bf16[8,128,128]{2,1,0:T(8,128)(2,1)S(1)}, u32[]{:S(2)}, u32[]{:S(2)}) async-start(bf16[8,128,128]{2,1,0:T(8,128)(2,1)} %get-tuple-element.100), calls=%async_computation.3 | async-start | bytes 524288 | tf_op jit(solution)/shard_map/all_to_all | solution.py:786
  118.5 5.3 %copy-start.5 = (bf16[8,128,128]{2,1,0:T(8,128)(2,1)}, bf16[8,128,128]{2,1,0:T(8,128)(2,1)S(1)}, u32[]{:S(2)}) copy-start(bf16[8,128,128]{2,1,0:T(8,128)(2,1)S(1)} %all-to-all-done.3.refs_0_) | copy-start | bytes 786436
  118.5 38.9 %all-to-all-start.6 = ((bf16[8,320,128]{2,1,0:T(8,128)(2,1)}), bf16[8,320,128]{2,1,0:T(8,128)(2,1)S(1)}, u32[]{:S(2)}, u32[]{:S(2)}) async-start(bf16[8,320,128]{2,1,0:T(8,128)(2,1)} %add_convert_fusion.1.refs_8_), calls=%async_computation.6 | async-start | bytes 1310720 | tf_op jit(solution)/shard_map/all_to_all | solution.py:786
  123.8 109.1 %all-gather.6.cloned.1.call-start = ((), (), s32[]{:S(2)}) async-start(), calls=%async_computation.8 | async-start | bytes 4325376 | tf_op jit(solution)/shard_map/all_gather | solution.py:928
  146.5 13.7 %copy-start.11 = (bf16[16,160,128]{2,1,0:T(8,128)(2,1)S(1)}, bf16[16,160,128]{2,1,0:T(8,128)(2,1)}, u32[]{:S(2)}) copy-start(bf16[16,160,128]{2,1,0:T(8,128)(2,1)} %get-tuple-element.118) | copy-start | bytes 1966084
  146.5 17.0 %copy-start.7 = (bf16[16,160,128]{2,1,0:T(8,128)(2,1)S(1)}, bf16[16,160,128]{2,1,0:T(8,128)(2,1)}, u32[]{:S(2)}) copy-start(bf16[16,160,128]{2,1,0:T(8,128)(2,1)} %get-tuple-element.117) | copy-start | bytes 1966084
  149.5 2.4 collective-permute-start.6
  151.9 0.6 copy-start.8
  154.2 3.2 %collective-permute-start.7 = (bf16[192,128]{1,0:T(8,128)(2,1)}, bf16[192,128]{1,0:T(8,128)(2,1)S(1)}, u32[]{:S(2)}, u32[]{:S(2)}) collective-permute-start(bf16[192,128]{1,0:T(8,128)(2,1)} %get-tuple-element.131), channel_id=1, source_target_pairs={{0,16},{8,24},{16,0},{24,8},{1,17},{9,25},{17,1},{25,9},{2,18},{10... | collective-permute-start | bytes 147464 | tf_op jit(solution)/shard_map/ppermute | solution.py:923
  157.4 0.6 copy-start.10
  157.4 0.8 copy-start.2
  160.2 3.3 %collective-permute-start.3 = (bf16[16,160,128]{2,1,0:T(8,128)(2,1)S(1)}, bf16[16,160,128]{2,1,0:T(8,128)(2,1)S(1)}, u32[]{:S(2)}, u32[]{:S(2)}) collective-permute-start(bf16[16,160,128]{2,1,0:T(8,128)(2,1)S(1)} %copy-done.11), channel_id=1, source_target_pairs={{0,8},{8,0},{16,24},{24,16},{1,9},{9,1},{17,25},{25,17},{2,10},{10... | collective-permute-start | bytes 1966088 | tf_op jit(solution)/shard_map/ppermute | solution.py:797
  188.9 7.5 %copy-start.12 = (f32[8,512]{1,0:T(8,128)S(1)}, f32[8,512]{1,0:T(8,128)}, u32[]{:S(2)}) copy-start(f32[8,512]{1,0:T(8,128)} %get-tuple-element.123) | copy-start | bytes 49156
  191.0 33.7 %all-to-all-start.5 = ((bf16[16,176,128]{2,1,0:T(8,128)(2,1)}), bf16[16,176,128]{2,1,0:T(8,128)(2,1)S(1)}, u32[]{:S(2)}, u32[]{:S(2)}) async-start(bf16[16,176,128]{2,1,0:T(8,128)(2,1)} %late_sum.1), calls=%async_computation.5 | async-start | bytes 1441792 | tf_op jit(solution)/shard_map/all_to_all | solution.py:793
  196.3 27.0 %collective-permute-start.4 = (f32[8,512]{1,0:T(8,128)S(1)}, f32[8,512]{1,0:T(8,128)S(1)}, u32[]{:S(2)}, u32[]{:S(2)}) collective-permute-start(f32[8,512]{1,0:T(8,128)S(1)} %copy-done.12), channel_id=1, source_target_pairs={{1,0},{2,1},{3,2},{4,3},{5,4},{6,5},{7,6},{9,8},{10,9},{11,10},{12... | collective-permute-start | bytes 49160 | tf_op jit(solution)/shard_map/ppermute | solution.py:909
  224.7 3.7 %copy-start.1 = (bf16[16,176,128]{2,1,0:T(8,128)(2,1)}, bf16[16,176,128]{2,1,0:T(8,128)(2,1)S(1)}, u32[]{:S(2)}) copy-start(bf16[16,176,128]{2,1,0:T(8,128)(2,1)S(1)} %all-to-all-done.5.refs_0_) | copy-start | bytes 2162692
  224.7 3.7 %collective-permute-start.5 = (bf16[16,176,128]{2,1,0:T(8,128)(2,1)S(1)}, bf16[16,176,128]{2,1,0:T(8,128)(2,1)S(1)}, u32[]{:S(2)}, u32[]{:S(2)}) collective-permute-start(bf16[16,176,128]{2,1,0:T(8,128)(2,1)S(1)} %all-to-all-done.5.refs_0_), channel_id=1, source_target_pairs={{0,8},{8,0},{16,24},{24,16},{1,9},{9,1},{17,25},{25,17},{2,10},{10... | collective-permute-start | bytes 2162696 | tf_op jit(solution)/shard_map/ppermute | solution.py:797
  228.4 0.9 copy-start.6
Sparse Core Ops, SparseCore 0:
  102.5 43.9 all-gather.3
  160.3 69.8 all-gather.5

commit v3 on v2

--- a/solution.py
+++ b/solution.py
@@ -280,8 +280,8 @@
 
 
 def backward_kernel(
-    back, after, w_proj, w_qkv, n2, cot, w_out, gate, ssm, s_ref, a_ref, bc,
-    o_out, o_after, o_branch, o_n2, o_gate, o_g, o_msg, o_attended, *o_more
+    tiled, back, after, w_proj, w_qkv, n2, cot, w_out, gate, ssm, gated, normed, s_ref, a_ref, bc,
+    o_out, o_after, o_n2, o_gate, o_g, o_msg, *o_more
 ):
     back = ready(back)
     seq_size, count = back.shape[0], back.shape[1]
@@ -298,20 +298,21 @@
     attended = jnp.concatenate(att, axis=1).astype(BF)
     after, w_proj = ready(after, w_proj)
     width = after.shape[1]
-    o_attended[...] = attended
     o_out[...] = (after[...] + dot(attended, w_proj[...])).astype(BF)
-    sent(o_attended, o_out)
+    sent(o_out)
     w_qkv, n2, cot = ready(w_qkv, n2, cot)
     grad_qkv = jnp.concatenate(dq + dk + dv, axis=1).astype(BF)
-    if o_more:
-        o_more[0][...] = grad_qkv
+    if not tiled:
+        o_more[0][...] = attended
+        o_more[1][...] = grad_qkv
     grad_x, grad_gain = rms_back(after[...], n2[...], dot_nt(grad_qkv, w_qkv[...]))
     o_n2[...] = jnp.sum(grad_gain, axis=0, keepdims=True)
     grad_after = cot[...].astype(F32) + grad_x
     o_after[...] = grad_after
     branch = grad_after.astype(BF)
-    o_branch[...] = branch
-    sent(o_n2, o_after, o_branch)
+    if not tiled:
+        o_more[2][...] = branch
+    sent(o_n2, o_after)
     w_out, gate, ssm = ready(w_out, gate, ssm)
     inner_width = gate.shape[1]
     tiles = inner_width // LANES
@@ -326,6 +327,10 @@
         grad_gate = grad * ssm[:, tile(j)] * (sig * (1.0 + v * (1.0 - sig)))
         o_gate[:, tile(j)] = grad_gate.astype(BF)
     sent(o_gate, o_g)
+    gated, normed = ready(gated, normed)
+    if tiled:
+        partials(seq_size, gated, branch, normed, o_gate, attended, cot, *o_more)
+        sent(*o_more[:2])
     s_ref, smem = ready(s_ref, bc)
 
     def one(i, later):
@@ -537,13 +542,10 @@
                 yield to, x, s, 2 * lax.bitwise_xor(x, mine) + side
 
 
-def partials_kernel(seq_size, gated, branch, normed, grad_gate, attended, cot, keep, send, out, gate, proj):
-    gated, branch = ready(gated, branch)
-    out[...] = dot_tn(gated[...], branch[...])
-    normed, grad_gate = ready(normed, grad_gate)
+def partials(seq_size, gated, branch, normed, grad_gate, attended, cot, keep, send, out, gate, proj):
+    out[...] = dot_tn(gated[...], branch)
     gate[...] = dot_tn(normed[...], grad_gate[...])
-    attended, cot = ready(attended, cot)
-    proj[...] = dot_tn(attended[...], cot[...])
+    proj[...] = dot_tn(attended, cot[...])
     across = out.shape[1] // LANES
     down = seq_size // across
     mine = lax.axis_index("dp") // 2
@@ -573,23 +575,19 @@
     o_n1[...] = jnp.concatenate(rows, axis=0).astype(BF)
 
 
-def head_products_kernel(normed, back, keep, send, grad, last):
+def head_products_kernel(normed, back, *rest):
+    *outs, grad, last = rest
     normed, back = ready(normed, back)
     both = back[...].reshape(back.shape[0] * back.shape[1], 2 * LANES)
     grad[...] = dot_tn(normed[...], both[:, :LANES])
     last[...] = dot_tn(normed[...], both[:, LANES:])
     left = lax.broadcasted_iota(jnp.int32, (HD, LANES), 1) < HD
-    for to, x, _, at in receivers((keep, send), 1, lax.axis_index("dp") // 2):
-        to[x, : 2 * HD, :] = grad[pl.ds(pl.multiple_of(at * LANES, LANES), LANES), :].astype(BF)
-        low = last[pl.ds(pl.multiple_of(at * LANES, LANES), HD), :]
-        high = last[pl.ds(pl.multiple_of(at * LANES + HD, HD), HD), :]
-        to[x, 2 * HD :, :] = jnp.where(left, low, pltpu.roll(high, HD, 1)).astype(BF)
-
-
-def head_middle_kernel(keep, received, near, far):
-    keep, received = ready(keep, received)
-    near[...] = (keep[0].astype(F32) + received[0].astype(F32)).astype(BF)
-    far[...] = (keep[1].astype(F32) + received[1].astype(F32)).astype(BF)
+    for distance, to in enumerate(outs):
+        g = lax.bitwise_xor(lax.axis_index("dp"), distance)
+        to[: 2 * HD, :] = grad[pl.ds(pl.multiple_of(g * LANES, LANES), LANES), :].astype(BF)
+        low = last[pl.ds(pl.multiple_of(g * LANES, LANES), HD), :]
+        high = last[pl.ds(pl.multiple_of(g * LANES + HD, HD), HD), :]
+        to[2 * HD :, :] = jnp.where(left, low, pltpu.roll(high, HD, 1)).astype(BF)
 
 
 def early_sum_kernel(parts, *heads):
@@ -858,26 +856,23 @@
         qkvg, msg, name="attention", us=0, views={1: np.s_[:, ends_at + 16 :, :]}, after=(every,), near=(0,),
     )
     back_own = exchange(back, "seq")
-    out, grad_after, branch, grad_n2, grad_gate, g, adj, attended, *more = call(
-        backward_kernel,
+    pieces = [((peers, 2 * LANES + HD, LANES), BF)] * 2
+    rest = [((count, width), BF), ((count, 3 * width), BF), ((count, width), BF)]
+    out, grad_after, grad_n2, grad_gate, g, adj, *more = call(
+        functools.partial(backward_kernel, tiled),
         [
-            ((count, width), BF), ((count, width), F32), ((count, width), BF), ((1, width), F32),
-            ((count, inner_width), BF), blocks, ((seq_size, states * 8, LANES), BF),
-            ((count, width), BF),
-        ] + ([] if tiled else [((count, 3 * width), BF)]),
-        [],
-        back_own, after, w_proj, w_qkv, n2, cotangent, w_out, gate, ssm, s, a, bc,
-        name="backward", us=0, scalars=(11,), near=(0,),
+            ((count, width), BF), ((count, width), F32), ((1, width), F32), ((count, inner_width), BF), blocks,
+            ((seq_size, states * 8, LANES), BF),
+        ] + (pieces if tiled else rest),
+        [vmem((inner_width, width), F32), vmem((width, inner_width), F32), vmem((width, width), F32)] if tiled else [],
+        back_own, after, w_proj, w_qkv, n2, cotangent, w_out, gate, ssm, gated, normed, s, a, bc,
+        name="backward", us=0, scalars=(13,), views={10: np.s_[HALO:, :]}, near=(0,),
     )
     adj = exchange(adj, "seq")
     between = ()
     if tiled:
         normed_two_all = lax.all_gather(normed_two, "seq", axis=0, tiled=True)
-        keep, send = call(
-            functools.partial(partials_kernel, seq_size), [((peers, 2 * LANES + HD, LANES), BF)] * 2,
-            [vmem((inner_width, width), F32), vmem((width, inner_width), F32), vmem((width, width), F32)],
-            gated, branch, normed, grad_gate, attended, cotangent, name="partials", us=0, views={2: np.s_[HALO:, :]},
-        )
+        keep, send = more
         add = lambda *parts: sum(part.astype(F32) for part in parts).astype(BF)
         received = other_core(send, groups)
         across = add(keep[seq_size:], received[seq_size:])
@@ -910,21 +905,21 @@
     grad_tokens = grad_tokens.at[count - 8 :].add(returned)
     flat = lambda v: v.reshape(-1)
     if tiled:
-        late = add(sums[0], other_core(small, groups))
-        late = own_core(late, groups, seq_size)
-        keep, send = call(
-            head_products_kernel, [((groups // 2, 3 * HD, LANES), BF)] * 2, [vmem((width, LANES), F32)] * 2,
+        head, *heads = call(
+            head_products_kernel, [((3 * HD, LANES), BF)] * groups, [vmem((width, LANES), F32)] * 2,
             normed_two_all, back, name="head_products", us=0, after=(grad_n1,),
         )
-        head, far = call(
-            head_middle_kernel, [((3 * HD, LANES), BF)] * 2, [], keep, other_core(send, groups), name="head_middle", us=0,
-            near=(1,),
-        )
-        heads = [lax.ppermute(far, "dp", [(g, g ^ 2) for g in range(groups)])]
+        heads = [
+            lax.ppermute(piece, "dp", [(g, g ^ distance) for g in range(groups)])
+            for distance, piece in enumerate(heads, 1)
+        ]
         (early,) = call(
             early_sum_kernel, [((part.shape[1] + head.shape[0], LANES), BF)], [], part, head, *heads,
-            name="early_sum", us=0, after=(grad_n1,), near=(0, 2),
-        )
+            name="early_sum", us=0, after=(grad_n1,), near=(0, 2, 3, 4),
+        )
+        late = add(sums[0], other_core(small, groups))
+        late, early = lax.optimization_barrier((late, early))
+        late = own_core(late, groups, seq_size)
         early = lax.all_gather(early, ("dp", "seq"))
         (late,) = call(
             sum_and_spread_kernel, [((peers, late.shape[1] + 16, LANES), BF)], [], late, grad_n1, name="late_sum", us=0,
@@ -951,7 +946,7 @@
         )
         g_xp, g_a, g_n1, g_n2 = g_xp.T, g_a.T, flat(g_n1), flat(g_n2)
     else:
-        (grad_qkv,) = more
+        attended, grad_qkv, branch = more
         small = small.reshape(SMALL, inner_width)
         g_n1 = flat(grad_n1[: width // LANES].astype(F32))
         both = jnp.concatenate([sums[0], dot_tn(normed[HALO:], grad_gate)], axis=1)

time: 246 us -> 238 us (0.967)
  Pallas kernels: 78.7 us -> 74.2 us
  waiting for transfers between devices: 56.1 us -> 52.2 us
    pallas_call x16 -> x14, Pallas kernels: 78.7 us -> 74.2 us  [call(): pl.pallas_call(run, out_shape=[jax.ShapeDtypeStruct(s, d) for s, d in out...]
    ppermute x4 -> x3, waiting for transfers between devices: 7.74 us -> 4.67 us  [other_core(): return lax.ppermute(value, 'dp', [(g, g ^ 1) for g in range(groups)])]
    ppermute x1, waiting for transfers between devices: 24.8 us -> 21.8 us  [body(): lax.ppermute(grad_halo, 'seq', [(i + 1, i) for i in range(seq_size - 1)])]
    ppermute x4 -> x3, starting transfers between devices: 7.06 us -> 6.5 us  [other_core(): return lax.ppermute(value, 'dp', [(g, g ^ 1) for g in range(groups)])]
  transfers between devices with their start and end apart: 15 -> 16, of which waited for: 11 -> 10; matrix products, arithmetic and copies ran while one was open for 1% -> 2% of each run, Pallas kernels for 17% -> 17%
where the time goes in v3:
time: 238 us; the launch traced here: 235 us
  Pallas kernels  74.2 us (31%)
  waiting for transfers between devices  52.2 us (22%)
  starting transfers between devices  43.2 us (18%)
  blocking collectives  42 us (18%)
  between operations  14.3 us (6%)
  other arithmetic  4.69 us (2%)
  local copies, waits for them, and re-layouts  4.56 us (2%)
    pallas_call x14, Pallas kernels, call(): pl.pallas_call(run, out_shape=[jax.ShapeDtypeStruct(s, d) for s, d in out...  74.2 us
    all_to_all x1, blocking collectives, own_core(): lax.all_to_all(value, ('dp', 'seq'), 0, 0, tiled=True, axis_index_groups=...  24.4 us
    all_to_all x4, starting transfers between devices, exchange(): return lax.all_to_all(value, axes, 0, 0, tiled=True)  22.5 us
    ppermute x1, waiting for transfers between devices, body(): lax.ppermute(grad_halo, 'seq', [(i + 1, i) for i in range(seq_size - 1)])  21.8 us
    all_to_all x1, blocking collectives, exchange(): return lax.all_to_all(value, axes, 0, 0, tiled=True)  17.6 us
    ppermute x1, waiting for transfers between devices, body(): across = lax.ppermute(across, 'dp', [(g, g ^ 2) for g in range(groups)])  9.86 us
    all_to_all x4, waiting for transfers between devices, exchange(): return lax.all_to_all(value, axes, 0, 0, tiled=True)  8.62 us
    ppermute x3, starting transfers between devices, other_core(): return lax.ppermute(value, 'dp', [(g, g ^ 1) for g in range(groups)])  6.5 us
  transfers between devices with their start and end apart: 16, of which 10 were waited for; matrix products, arithmetic and copies ran while one was open for 2% of the time, Pallas kernels for 17%

profile of v3, /device:TPU:13, one launch (start us, length us, event | category | flops | bytes accessed | tf_op | source)
XLA Modules:
  0.0 235.1 jit_solution(14826391591685334963)
XLA Ops:
  7.2 0.7 slice.34
  7.9 3.1 %collective-permute-start = (bf16[16,512]{1,0:T(8,128)(2,1)S(1)}, bf16[16,512]{1,0:T(8,128)(2,1)S(1)}, u32[]{:S(2)}, u32[]{:S(2)}) collective-permute-start(bf16[16,512]{1,0:T(8,128)(2,1)S(1)} %slice.34), channel_id=1, source_target_pairs={{0,1},{1,2},{2,3},{3,4},{4,5},{5,6},{6,7},{8,9},{9,10},{10,11},{11... | collective-permute-start | bytes 49160 | tf_op jit(solution)/shard_map/ppermute | solution.py:819
  11.0 1.3 collective-permute-done.refs_1_.refs_4_
  12.4 0.6 copy-done.8
  13.0 7.4 %forward.1 = (bf16[8,160,128]{2,1,0:T(8,128)(2,1)}, bf16[144,512]{1,0:T(8,128)(2,1)}, bf16[144,1024]{1,0:T(8,128)(2,1)}, bf16[128,1024]{1,0:T(8,128)(2,1)}, bf16...) custom-call(bf16[128,512]{1,0:T(8,128)(2,1)} %refs_3_.5, ...), custom_call_target="tpu_custom_call" | custom-call | flops 1000 | bytes 1000 | tf_op jit(solution)/shard_map/forward/pallas_call | solution.py:770
  20.4 5.7 %all-to-all-start = ((bf16[8,160,128]{2,1,0:T(8,128)(2,1)}), bf16[8,160,128]{2,1,0:T(8,128)(2,1)S(1)}, u32[]{:S(2)}, u32[]{:S(2)}) async-start(bf16[8,160,128]{2,1,0:T(8,128)(2,1)} %get-tuple-element.86), calls=%async_computation | async-start | bytes 655360 | tf_op jit(solution)/shard_map/all_to_all | solution.py:784
  26.1 2.1 grad_att.1.refs_12_
  28.2 4.8 %all-to-all-done.refs_0_.refs_1_ = bf16[8,160,128]{2,1,0:T(8,128)(2,1)S(1)} async-done(((bf16[8,160,128]{2,1,0:T(8,128)(2,1)}), bf16[8,160,128]{2,1,0:T(8,128)(2,1)S(1)}, u32[]{:S(2)}, u32[]{:S(2)}) %all-to-all-start) | async-done | bytes 327712 | tf_op jit(solution)/shard_map/all_to_all | solution.py:784
  33.0 0.7 copy-done
  33.7 6.4 %middle.1 = (bf16[8,128,256]{2,1,0:T(8,128)(2,1)}, f32[128,128]{1,0:T(8,128)}, f32[128,1024]{1,0:T(8,128)}, f32[128,512]{1,0:T(8,128)}, bf16[128,1024]{1,0:T(8,128)(2,1)}, /*index=5*/bf16[128,512]{1,0:T(8,128)(2,1)}) custom-call(bf16[8,160,128]{2,1,0:T(8,128)(2,1)} %copy-done, f32[128,128]{1,0:T(8,128)} %get-tuple-element.87.refs_1_.refs_12_.refs_2_, ...), custom_call_target="tpu_custom_call" | custom-call | flops 1000 | bytes 1000 | tf_op jit(solution)/shard_map/middle/pallas_call | solution.py:770
  40.1 6.4 %all-to-all-start.1 = ((bf16[8,128,256]{2,1,0:T(8,128)(2,1)}), bf16[8,128,256]{2,1,0:T(8,128)(2,1)S(1)}, u32[]{:S(2)}, u32[]{:S(2)}) async-start(bf16[8,128,256]{2,1,0:T(8,128)(2,1)} %get-tuple-element.93), calls=%async_computation.1 | async-start | bytes 1048576 | tf_op jit(solution)/shard_map/all_to_all | solution.py:784
  46.5 7.6 %states.1 = (f32[16512,128]{1,0:T(8,128)}, f32[128,1024]{1,0:T(8,128)}) custom-call(f32[128,128]{1,0:T(8,128)} %get-tuple-element.94.refs_0_, f32[128,128]{1,0:T(8,128)} %get-tuple-element.87.refs_1_.refs_12_.refs_2_, f32[128,32]{1,0:T(8,128)} %get-tuple-element.88.refs_2_.refs_13_.refs_3_, f32[1024,128]{1,0:T(8,128)} %get-tuple-element.89.refs_3_.refs_11_.refs_4_, ...), custom_call_target="tpu_custom_call" | custom-call | flops 1000 | bytes 1000 | tf_op jit(solution)/shard_map/states/pallas_call | solution.py:770
  54.1 3.8 %all-to-all-done.1.refs_0_ = bf16[8,128,256]{2,1,0:T(8,128)(2,1)S(1)} async-done(((bf16[8,128,256]{2,1,0:T(8,128)(2,1)}), bf16[8,128,256]{2,1,0:T(8,128)(2,1)S(1)}, u32[]{:S(2)}, u32[]{:S(2)}) %all-to-all-start.1) | async-done | bytes 524320 | tf_op jit(solution)/shard_map/all_to_all | solution.py:784
  57.9 0.8 copy-done.3
  58.7 7.4 %attention.1.refs_1_ = bf16[8,128,256]{2,1,0:T(8,128)(2,1)} custom-call(bf16[8,128,256]{2,1,0:T(8,128)(2,1)} %copy-done.3, bf16[8,160,128]{2,1,0:T(8,128)(2,1)} %copy-done, f32[16512,128]{1,0:T(8,128)} %get-tuple-element.96.refs_2_.refs_7_), custom_call_target="tpu_custom_call" | custom-call | flops 1000 | bytes 1000 | tf_op jit(solution)/shard_map/attention/pallas_call | solution.py:770
  66.1 17.6 %all_to_all.35.refs_0_ = bf16[8,128,256]{2,1,0:T(8,128)(2,1)} all-to-all(bf16[8,128,256]{2,1,0:T(8,128)(2,1)} %attention.1.refs_1_), channel_id=1, replica_groups=mesh['dp'=4,'seq'=8] {'seq'}, dimensions={0} | all-to-all | bytes 1048576 | tf_op jit(solution)/shard_map/all_to_all | solution.py:784
  83.8 7.0 %backward.1 = (bf16[128,512]{1,0:T(8,128)(2,1)}, f32[128,512]{1,0:T(8,128)}, f32[1,512]{1,0:T(1,128)}, bf16[128,1024]{1,0:T(8,128)(2,1)}, f32[1024,128]{1,0:T(8,...) custom-call(bf16[8,128,256]{2,1,0:T(8,128)(2,1)} %all_to_all.35.refs_0_, ...), custom_call_target="tpu_custom_call" | custom-call | flops 1000 | bytes 1000 | tf_op jit(solution)/shard_map/backward/pallas_call | solution.py:770
  90.7 2.5 %collective-permute-start.1 = (bf16[16,320,128]{2,1,0:T(8,128)(2,1)}, bf16[16,320,128]{2,1,0:T(8,128)(2,1)S(1)}, u32[]{:S(2)}, u32[]{:S(2)}) collective-permute-start(bf16[16,320,128]{2,1,0:T(8,128)(2,1)} %get-tuple-element.105), channel_id=1, source_target_pairs={{0,8},{8,0},{16,24},{24,16},{1,9},{9,1},{17,25},{25,17},{2,10},{10... | collective-permute-start | bytes 3932168 | tf_op jit(solution)/shard_map/ppermute | solution.py:795
  93.3 2.8 %collective-permute-done.1 = bf16[16,320,128]{2,1,0:T(8,128)(2,1)S(1)} collective-permute-done((bf16[16,320,128]{2,1,0:T(8,128)(2,1)}, bf16[16,320,128]{2,1,0:T(8,128)(2,1)S(1)}, u32[]{:S(2)}, u32[]{:S(2)}) %collective-permute-start.1) | collective-permute-done | bytes 1310752 | tf_op jit(solution)/shard_map/ppermute | solution.py:795
  96.1 2.1 add_convert_fusion.2
  98.2 1.2 collective-permute-start.2
  99.4 5.2 %all-to-all-start.3 = ((bf16[8,128,128]{2,1,0:T(8,128)(2,1)}), bf16[8,128,128]{2,1,0:T(8,128)(2,1)S(1)}, u32[]{:S(2)}, u32[]{:S(2)}) async-start(bf16[8,128,128]{2,1,0:T(8,128)(2,1)} %get-tuple-element.102), calls=%async_computation.3 | async-start | bytes 524288 | tf_op jit(solution)/shard_map/all_to_all | solution.py:784
  104.6 9.9 %collective-permute-done.2 = bf16[8,320,128]{2,1,0:T(8,128)(2,1)S(1)} collective-permute-done((bf16[8,320,128]{2,1,0:T(8,128)(2,1)}, bf16[8,320,128]{2,1,0:T(8,128)(2,1)S(1)}, u32[]{:S(2)}, u32[]{:S(2)}) %collective-permute-start.2) | collective-permute-done | bytes 655392 | tf_op jit(solution)/shard_map/ppermute | solution.py:879
  114.5 1.1 add_convert_fusion.1.refs_8_
  115.6 5.3 %all-to-all-start.4 = ((bf16[8,320,128]{2,1,0:T(8,128)(2,1)}), bf16[8,320,128]{2,1,0:T(8,128)(2,1)S(1)}, u32[]{:S(2)}, u32[]{:S(2)}) async-start(bf16[8,320,128]{2,1,0:T(8,128)(2,1)} %add_convert_fusion.1.refs_8_), calls=%async_computation.4 | async-start | bytes 1310720 | tf_op jit(solution)/shard_map/all_to_all | solution.py:784
  120.9 11.4 %adjoint.1 = (f32[1024,128]{1,0:T(8,128)}, f32[1024,128]{1,0:T(8,128)}, f32[128,64]{1,0:T(8,128)}, f32[128,128]{1,0:T(8,128)}) custom-call(bf16[8,128,128]{2,1,0:T(8,128)(2,1)} %copy-done.5, bf16[8,160,128]{2,1,0:T(8,128)(2,1)} %copy-done, f32[128,128]{1,0:T(8,128)} %get-tuple-element.87.refs_1_.refs_12_.refs_2_, ...), custom_call_target="tpu_custom_call" | custom-call | flops 1000 | bytes 1000 | tf_op jit(solution)/shard_map/adjoint/pallas_call | solution.py:770
  132.3 6.0 %inner.1 = (bf16[16,160,128]{2,1,0:T(8,128)(2,1)}, bf16[16,160,128]{2,1,0:T(8,128)(2,1)}, bf16[144,1024]{1,0:T(8,128)(2,1)}) custom-call(f32[1024,128]{1,0:T(8,128)} %get-tuple-element.106.refs_0_, f32[1024,128]{1,0:T(8,128)} %get-tuple-element.107.refs_1_, f32[1024,128]{1,0:T(8,128)} %get-tuple-element.103.refs_6_.refs_2_, ...), custom_call_target="tpu_custom_call" | custom-call | flops 1000 | bytes 1000 | tf_op jit(solution)/shard_map/inner/pallas_call | solution.py:770
  138.3 1.6 collective-permute-start.3
  139.9 3.5 %tokens.1 = (f32[128,512]{1,0:T(8,128)}, f32[8,512]{1,0:T(8,128)}, bf16[16,128]{1,0:T(8,128)(2,1)}) custom-call(bf16[144,1024]{1,0:T(8,128)(2,1)} %get-tuple-element.117.refs_0_, bf16[512,2048]{1,0:T(8,128)(2,1)} %refs_1_.3, bf16[128,1024]{1,0:T(8,128)(2,1)} %get-tuple-element.118.refs_2_, bf16[128,512]{1,0:T(8,128)(2,1)} %refs_3_.5, ...), custom_call_target="tpu_custom_call" | custom-call | flops 1000 | bytes 1000 | tf_op jit(solution)/shard_map/tokens/pallas_call | solution.py:770
  143.4 2.9 %head_products.1 = (bf16[192,128]{1,0:T(8,128)(2,1)}, bf16[192,128]{1,0:T(8,128)(2,1)}, bf16[192,128]{1,0:T(8,128)(2,1)}, bf16[192,128]{1,0:T(8,128)(2,1)}) custom-call(bf16[1024,512]{1,0:T(8,128)(2,1)} %all-gather.4.cloned.1.call-done.refs_0_, bf16[8,128,256]{2,1,0:T(8,128)(2,1)} %attention.1.refs_1_, bf16[16,128]{1,0:T(8,128)(2,1)} %get-tuple-element.120.refs_2_.refs_5_.refs_1_), custom_call_target="tpu_custom_call" | custom-call | flops 1000 | bytes 1000 | tf_op jit(solution)/shard_map/head_products/pallas_call | solution.py:770
  146.4 1.3 collective-permute-start.5
  147.7 0.9 collective-permute-start.6
  148.8 0.9 collective-permute-done.5.refs_3_
  149.6 2.6 %collective-permute-done.6.refs_4_ = bf16[192,128]{1,0:T(8,128)(2,1)S(1)} collective-permute-done((bf16[192,128]{1,0:T(8,128)(2,1)}, bf16[192,128]{1,0:T(8,128)(2,1)S(1)}, u32[]{:S(2)}, u32[]{:S(2)}) %collective-permute-start.6) | collective-permute-done | bytes 49184 | tf_op jit(solution)/shard_map/ppermute | solution.py:913
  152.2 0.6 copy-done.11
  153.1 1.9 early_sum.1
  155.0 24.4 %all_to_all.36.refs_0_ = bf16[16,160,128]{2,1,0:T(8,128)(2,1)} all-to-all(bf16[16,160,128]{2,1,0:T(8,128)(2,1)S(1)} %add_convert_fusion), channel_id=1, replica_groups={{0,1,2,3,4,5,6,7,16,17,18,19,20,21,22,23},{8,9,10,11,12,13,14,15,24,25,..., dimensions={0} | all-to-all | bytes 1310720 | tf_op jit(solution)/shard_map/all_to_all | solution.py:791
  179.4 2.1 late_sum.1
  181.5 5.4 %all-to-all-start.6 = ((bf16[16,176,128]{2,1,0:T(8,128)(2,1)}), bf16[16,176,128]{2,1,0:T(8,128)(2,1)S(1)}, u32[]{:S(2)}, u32[]{:S(2)}) async-start(bf16[16,176,128]{2,1,0:T(8,128)(2,1)} %late_sum.1), calls=%async_computation.6 | async-start | bytes 1441792 | tf_op jit(solution)/shard_map/all_to_all | solution.py:791
  186.9 2.2 collective-permute-start.7
  189.1 21.8 %collective-permute-done.7 = f32[8,512]{1,0:T(8,128)S(1)} collective-permute-done((f32[8,512]{1,0:T(8,128)S(1)}, f32[8,512]{1,0:T(8,128)S(1)}, u32[]{:S(2)}, u32[]{:S(2)}) %collective-permute-start.7) | collective-permute-done | bytes 16416 | tf_op jit(solution)/shard_map/ppermute | solution.py:904
  210.9 1.3 add_dynamic-update-slice_fusion
  212.2 2.4 %collective-permute-start.8 = (bf16[16,176,128]{2,1,0:T(8,128)(2,1)S(1)}, bf16[16,176,128]{2,1,0:T(8,128)(2,1)S(1)}, u32[]{:S(2)}, u32[]{:S(2)}) collective-permute-start(bf16[16,176,128]{2,1,0:T(8,128)(2,1)S(1)} %all-to-all-done.6.refs_0_), channel_id=1, source_target_pairs={{0,8},{8,0},{16,24},{24,16},{1,9},{9,1},{17,25},{25,17},{2,10},{10... | collective-permute-start | bytes 2162696 | tf_op jit(solution)/shard_map/ppermute | solution.py:795
  214.6 1.8 collective-permute-done.8.refs_1_
  216.4 0.9 copy-done.6
  217.3 3.6 %late_assembly.1 = (f32[512,2048]{1,0:T(8,128)}, f32[1,512]{1,0:T(1,128)}, f32[4,1024]{1,0:T(4,128)}, f32[1,1024]{1,0:T(1,128)}, f32[64,1024]{1,0:T(8,128)}, /*i...) custom-call(bf16[16,176,128]{2,1,0:T(8,128)(2,1)} %copy-done.1, ...), custom_call_target="tpu_custom_call" | custom-call | flops 1000 | bytes 1000 | tf_op jit(solution)/shard_map/late_assembly/pallas_call | solution.py:770
  220.9 2.4 %all-gather.6.cloned.1.call-done = bf16[16384,128]{1,0:T(8,128)(2,1)} async-done(((bf16[512,128]{1,0:T(8,128)(2,1)}), bf16[16384,128]{1,0:T(8,128)(2,1)}) %all-gather.6.cloned.1.call-update) | async-done | bytes 4194320 | tf_op jit(solution)/shard_map/all_gather | solution.py:923
  223.3 4.9 %early_assembly.1 = (f32[1024,512]{1,0:T(8,128)}, f32[512,512]{1,0:T(8,128)}, f32[512,1536]{1,0:T(8,128)}, f32[512,2048]{1,0:T(8,128)}) custom-call(bf16[32,512,128]{2,1,0:T(8,128)(2,1)} %bitcast.16, f32[512,2048]{1,0:T(8,128)} %get-tuple-element.132.refs_1_), custom_call_target="tpu_custom_call", output_to_operand_aliasing={{3}: (1, {})} | custom-call | flops 1000 | bytes 1000 | tf_op jit(solution)/shard_map/early_assembly/pallas_call | solution.py:770
  (33 shorter events, 0.6 us)
Async XLA Ops:
  7.9 4.5 %collective-permute-start = (bf16[16,512]{1,0:T(8,128)(2,1)S(1)}, bf16[16,512]{1,0:T(8,128)(2,1)S(1)}, u32[]{:S(2)}, u32[]{:S(2)}) collective-permute-start(bf16[16,512]{1,0:T(8,128)(2,1)S(1)} %slice.34), channel_id=1, source_target_pairs={{0,1},{1,2},{2,3},{3,4},{4,5},{5,6},{6,7},{8,9},{9,10},{10,11},{11... | collective-permute-start | bytes 49160 | tf_op jit(solution)/shard_map/ppermute | solution.py:819
  12.4 0.6 copy-start.8
  20.4 12.6 %all-to-all-start = ((bf16[8,160,128]{2,1,0:T(8,128)(2,1)}), bf16[8,160,128]{2,1,0:T(8,128)(2,1)S(1)}, u32[]{:S(2)}, u32[]{:S(2)}) async-start(bf16[8,160,128]{2,1,0:T(8,128)(2,1)} %get-tuple-element.86), calls=%async_computation | async-start | bytes 655360 | tf_op jit(solution)/shard_map/all_to_all | solution.py:784
  33.0 0.7 copy-start
  40.1 17.8 %all-to-all-start.1 = ((bf16[8,128,256]{2,1,0:T(8,128)(2,1)}), bf16[8,128,256]{2,1,0:T(8,128)(2,1)S(1)}, u32[]{:S(2)}, u32[]{:S(2)}) async-start(bf16[8,128,256]{2,1,0:T(8,128)(2,1)} %get-tuple-element.93), calls=%async_computation.1 | async-start | bytes 1048576 | tf_op jit(solution)/shard_map/all_to_all | solution.py:784
  46.5 96.9 %all-gather.4.cloned.1.call-start = ((), (), s32[]{:S(2)}) async-start(), calls=%async_computation.7 | async-start | bytes 1179648 | tf_op jit(solution)/shard_map/all_gather | solution.py:874
  57.9 0.8 copy-start.3
  90.7 5.4 %collective-permute-start.1 = (bf16[16,320,128]{2,1,0:T(8,128)(2,1)}, bf16[16,320,128]{2,1,0:T(8,128)(2,1)S(1)}, u32[]{:S(2)}, u32[]{:S(2)}) collective-permute-start(bf16[16,320,128]{2,1,0:T(8,128)(2,1)} %get-tuple-element.105), channel_id=1, source_target_pairs={{0,8},{8,0},{16,24},{24,16},{1,9},{9,1},{17,25},{25,17},{2,10},{10... | collective-permute-start | bytes 3932168 | tf_op jit(solution)/shard_map/ppermute | solution.py:795
  93.2 21.2 %copy-start.4 = (bf16[16,320,128]{2,1,0:T(8,128)(2,1)S(1)}, bf16[16,320,128]{2,1,0:T(8,128)(2,1)}, u32[]{:S(2)}) copy-start(bf16[16,320,128]{2,1,0:T(8,128)(2,1)} %get-tuple-element.104) | copy-start | bytes 3932164
  98.2 16.3 %collective-permute-start.2 = (bf16[8,320,128]{2,1,0:T(8,128)(2,1)}, bf16[8,320,128]{2,1,0:T(8,128)(2,1)S(1)}, u32[]{:S(2)}, u32[]{:S(2)}) collective-permute-start(bf16[8,320,128]{2,1,0:T(8,128)(2,1)} %add_convert_fusion.2), channel_id=1, source_target_pairs={{0,16},{8,24},{16,0},{24,8},{1,17},{9,25},{17,1},{25,9},{2,18},{10... | collective-permute-start | bytes 1966088 | tf_op jit(solution)/shard_map/ppermute | solution.py:879
  99.4 16.2 %all-to-all-start.3 = ((bf16[8,128,128]{2,1,0:T(8,128)(2,1)}), bf16[8,128,128]{2,1,0:T(8,128)(2,1)S(1)}, u32[]{:S(2)}, u32[]{:S(2)}) async-start(bf16[8,128,128]{2,1,0:T(8,128)(2,1)} %get-tuple-element.102), calls=%async_computation.3 | async-start | bytes 524288 | tf_op jit(solution)/shard_map/all_to_all | solution.py:784
  115.6 5.3 %copy-start.5 = (bf16[8,128,128]{2,1,0:T(8,128)(2,1)}, bf16[8,128,128]{2,1,0:T(8,128)(2,1)S(1)}, u32[]{:S(2)}) copy-start(bf16[8,128,128]{2,1,0:T(8,128)(2,1)S(1)} %all-to-all-done.3.refs_0_) | copy-start | bytes 786436
  115.6 36.7 %all-to-all-start.4 = ((bf16[8,320,128]{2,1,0:T(8,128)(2,1)}), bf16[8,320,128]{2,1,0:T(8,128)(2,1)S(1)}, u32[]{:S(2)}, u32[]{:S(2)}) async-start(bf16[8,320,128]{2,1,0:T(8,128)(2,1)} %add_convert_fusion.1.refs_8_), calls=%async_computation.4 | async-start | bytes 1310720 | tf_op jit(solution)/shard_map/all_to_all | solution.py:784
  120.9 102.5 %all-gather.6.cloned.1.call-start = ((), (), s32[]{:S(2)}) async-start(), calls=%async_computation.8 | async-start | bytes 4325376 | tf_op jit(solution)/shard_map/all_gather | solution.py:923
  138.3 10.3 %collective-permute-start.3 = (bf16[16,160,128]{2,1,0:T(8,128)(2,1)}, bf16[16,160,128]{2,1,0:T(8,128)(2,1)S(1)}, u32[]{:S(2)}, u32[]{:S(2)}) collective-permute-start(bf16[16,160,128]{2,1,0:T(8,128)(2,1)} %get-tuple-element.115), channel_id=1, source_target_pairs={{0,8},{8,0},{16,24},{24,16},{1,9},{9,1},{17,25},{25,17},{2,10},{10... | collective-permute-start | bytes 1966088 | tf_op jit(solution)/shard_map/ppermute | solution.py:795
  143.4 5.2 %copy-start.7 = (bf16[16,160,128]{2,1,0:T(8,128)(2,1)S(1)}, bf16[16,160,128]{2,1,0:T(8,128)(2,1)}, u32[]{:S(2)}) copy-start(bf16[16,160,128]{2,1,0:T(8,128)(2,1)} %get-tuple-element.114) | copy-start | bytes 1966084
  146.3 2.4 %collective-permute-start.4 = (bf16[192,128]{1,0:T(8,128)(2,1)}, bf16[192,128]{1,0:T(8,128)(2,1)S(1)}, u32[]{:S(2)}, u32[]{:S(2)}) collective-permute-start(bf16[192,128]{1,0:T(8,128)(2,1)} %get-tuple-element.122), channel_id=1, source_target_pairs={{0,8},{8,0},{16,24},{24,16},{1,9},{9,1},{17,25},{25,17},{2,10},{10... | collective-permute-start | bytes 147464 | tf_op jit(solution)/shard_map/ppermute | solution.py:913
  146.4 3.2 %collective-permute-start.5 = (bf16[192,128]{1,0:T(8,128)(2,1)}, bf16[192,128]{1,0:T(8,128)(2,1)S(1)}, u32[]{:S(2)}, u32[]{:S(2)}) collective-permute-start(bf16[192,128]{1,0:T(8,128)(2,1)} %get-tuple-element.123), channel_id=1, source_target_pairs={{0,16},{8,24},{16,0},{24,8},{1,17},{9,25},{17,1},{25,9},{2,18},{10... | collective-permute-start | bytes 147464 | tf_op jit(solution)/shard_map/ppermute | solution.py:913
  147.7 4.5 %collective-permute-start.6 = (bf16[192,128]{1,0:T(8,128)(2,1)}, bf16[192,128]{1,0:T(8,128)(2,1)S(1)}, u32[]{:S(2)}, u32[]{:S(2)}) collective-permute-start(bf16[192,128]{1,0:T(8,128)(2,1)} %get-tuple-element.124), channel_id=1, source_target_pairs={{0,24},{8,16},{16,8},{24,0},{1,25},{9,17},{17,9},{25,1},{2,26},{10... | collective-permute-start | bytes 147464 | tf_op jit(solution)/shard_map/ppermute | solution.py:913
  148.7 3.5 %copy-start.9 = (bf16[192,128]{1,0:T(8,128)(2,1)}, bf16[192,128]{1,0:T(8,128)(2,1)S(1)}, u32[]{:S(2)}) copy-start(bf16[192,128]{1,0:T(8,128)(2,1)S(1)} %collective-permute-done.4.refs_2_) | copy-start | bytes 147460
  149.6 2.6 %copy-start.10 = (bf16[192,128]{1,0:T(8,128)(2,1)}, bf16[192,128]{1,0:T(8,128)(2,1)S(1)}, u32[]{:S(2)}) copy-start(bf16[192,128]{1,0:T(8,128)(2,1)S(1)} %collective-permute-done.5.refs_3_) | copy-start | bytes 147460
  152.2 0.6 copy-start.11
  152.2 0.8 copy-start.2
  179.4 7.5 %copy-start.12 = (f32[8,512]{1,0:T(8,128)S(1)}, f32[8,512]{1,0:T(8,128)}, u32[]{:S(2)}) copy-start(f32[8,512]{1,0:T(8,128)} %get-tuple-element.127) | copy-start | bytes 49156
  181.5 30.7 %all-to-all-start.6 = ((bf16[16,176,128]{2,1,0:T(8,128)(2,1)}), bf16[16,176,128]{2,1,0:T(8,128)(2,1)S(1)}, u32[]{:S(2)}, u32[]{:S(2)}) async-start(bf16[16,176,128]{2,1,0:T(8,128)(2,1)} %late_sum.1), calls=%async_computation.6 | async-start | bytes 1441792 | tf_op jit(solution)/shard_map/all_to_all | solution.py:791
  186.9 24.0 %collective-permute-start.7 = (f32[8,512]{1,0:T(8,128)S(1)}, f32[8,512]{1,0:T(8,128)S(1)}, u32[]{:S(2)}, u32[]{:S(2)}) collective-permute-start(f32[8,512]{1,0:T(8,128)S(1)} %copy-done.12), channel_id=1, source_target_pairs={{1,0},{2,1},{3,2},{4,3},{5,4},{6,5},{7,6},{9,8},{10,9},{11,10},{12... | collective-permute-start | bytes 49160 | tf_op jit(solution)/shard_map/ppermute | solution.py:904
  212.2 4.2 %copy-start.1 = (bf16[16,176,128]{2,1,0:T(8,128)(2,1)}, bf16[16,176,128]{2,1,0:T(8,128)(2,1)S(1)}, u32[]{:S(2)}) copy-start(bf16[16,176,128]{2,1,0:T(8,128)(2,1)S(1)} %all-to-all-done.6.refs_0_) | copy-start | bytes 2162692
  212.2 4.2 %collective-permute-start.8 = (bf16[16,176,128]{2,1,0:T(8,128)(2,1)S(1)}, bf16[16,176,128]{2,1,0:T(8,128)(2,1)S(1)}, u32[]{:S(2)}, u32[]{:S(2)}) collective-permute-start(bf16[16,176,128]{2,1,0:T(8,128)(2,1)S(1)} %all-to-all-done.6.refs_0_), channel_id=1, source_target_pairs={{0,8},{8,0},{16,24},{24,16},{1,9},{9,1},{17,25},{25,17},{2,10},{10... | collective-permute-start | bytes 2162696 | tf_op jit(solution)/shard_map/ppermute | solution.py:795
  216.4 0.9 copy-start.6
Sparse Core Ops, SparseCore 0:
  93.4 47.0 all-gather.3
  155.1 68.1 all-gather.5

commit v4 on v3

--- a/solution.py
+++ b/solution.py
@@ -103,8 +103,6 @@
     o_inner[...] = inner
     sent(o_inner)
     ext[...] = inner.astype(F32)
-    o_gate[...] = dot(normed[HALO:], w_in[:, inner_width:]).astype(BF)
-    sent(o_gate)
     conv_w, conv_b, w_xp, w_dt, dtb, a_log = ready(conv_w, conv_b, w_xp, w_dt, dtb, a_log)
     offset = offsets_in_sequence(seg, seq_size)
     for j in range(tiles):
@@ -120,6 +118,8 @@
     copy.start()
     o_pre[...] = dot(low, w_dt[...]) + dtb[...]
     sent(o_pre)
+    o_gate[...] = dot(normed[HALO:], w_in[:, inner_width:]).astype(BF)
+    sent(o_gate)
     for j in range(tiles):
         step = softplus(o_pre[:, tile(j)])
         to_rows(o_s, j, jnp.where(offset == 0.0, RESET, step))
@@ -246,13 +246,17 @@
     dv[...] = jnp.zeros_like(dv)
     scale = HD**-0.5
 
-    def queries(b, length):
-        at = pl.ds(b * count if isinstance(b, int) else pl.multiple_of(b * count, count), count)
-        tail = ends[b].astype(F32)
-        starts = jnp.broadcast_to(tail[0:1] * 64.0 + tail[1:2], (LANES, LANES))
-        first = jnp.transpose(starts)[:, :1].astype(jnp.int32)
-        column = lax.broadcasted_iota(jnp.int32, (count, length), 1)
-        row = b * count + lax.broadcasted_iota(jnp.int32, (count, 1), 0)
+    def queries(b, length, blocks):
+        tall = blocks * count
+        at = pl.ds(b * count if isinstance(b, int) else pl.multiple_of(b * count, count), tall)
+        firsts = []
+        for i in range(blocks):
+            tail = ends[b + i].astype(F32)
+            starts = jnp.broadcast_to(tail[0:1] * 64.0 + tail[1:2], (LANES, LANES))
+            firsts.append(jnp.transpose(starts)[:, :1])
+        first = jnp.concatenate(firsts, axis=0).astype(jnp.int32)
+        column = lax.broadcasted_iota(jnp.int32, (tall, length), 1)
+        row = b * count + lax.broadcasted_iota(jnp.int32, (tall, 1), 0)
         visible = (column <= row) & (column >= first)
         scores = jnp.where(visible, dot_nt(qz[at, :], kr[:length, :]) * scale, -1e30)
         weight = jnp.exp(scores - jnp.max(scores, axis=1, keepdims=True))
@@ -263,16 +267,17 @@
         grad_scores = (probs * (grad_probs - delta)).astype(BF)
         dk[:length, :] += dot_tn(grad_scores, kr[at, :])
         dv[:length, :] += dot_tn(low, vr[at, :])
-        dq = dot(grad_scores, kr[:length, :])
-        attended = dot(low, vr[:length, :])
-        o_back[b, :, :LANES] = (dq * scale).astype(BF)
-        o_back[b, :, LANES:] = attended.astype(BF)
+        dq = (dot(grad_scores, kr[:length, :]) * scale).astype(BF)
+        attended = dot(low, vr[:length, :]).astype(BF)
+        for i in range(blocks):
+            o_back[b + i, :, :LANES] = dq[i * count : (i + 1) * count]
+            o_back[b + i, :, LANES:] = attended[i * count : (i + 1) * count]
 
     if seq_size <= 8:
-        for b in range(seq_size):
-            queries(b, (b + 1) * count)
+        for b in range(0, seq_size, 2):
+            queries(b, (b + 2) * count, 2)
     else:
-        lax.fori_loop(0, seq_size, lambda b, _: (queries(b, rows), 0)[1], 0)
+        lax.fori_loop(0, seq_size, lambda b, _: (queries(b, rows, 1), 0)[1], 0)
     for d in range(seq_size):
         at = slice(d * count, (d + 1) * count)
         o_back[d, :, :LANES] = jnp.where(left, o_back[d, :, :LANES].astype(F32), dk[at, :] * scale).astype(BF)
@@ -915,14 +920,14 @@
         ]
         (early,) = call(
             early_sum_kernel, [((part.shape[1] + head.shape[0], LANES), BF)], [], part, head, *heads,
-            name="early_sum", us=0, after=(grad_n1,), near=(0, 2, 3, 4),
+            name="early_sum", us=0, vmem=40, after=(grad_n1,), near=(0, 2, 3, 4),
         )
         late = add(sums[0], other_core(small, groups))
         late, early = lax.optimization_barrier((late, early))
         late = own_core(late, groups, seq_size)
         early = lax.all_gather(early, ("dp", "seq"))
         (late,) = call(
-            sum_and_spread_kernel, [((peers, late.shape[1] + 16, LANES), BF)], [], late, grad_n1, name="late_sum", us=0,
+            sum_and_spread_kernel, [((peers, late.shape[1] + 16, LANES), BF)], [], late, grad_n1, name="late_sum", us=0, vmem=40,
             near=(0,),
         )
         mine = own_core(late, groups, seq_size)
@@ -935,7 +940,7 @@
                 row(1), row(states), row(1), ((1, width), F32),
             ],
             [vmem((width, inner_width), F32), vmem((SMALL * 8, LANES), F32), sem((4,))],
-            mine, other_core(mine, groups), name="late_assembly", us=0, raw_out=(0,), near=(0, 1),
+            mine, other_core(mine, groups), name="late_assembly", us=0, vmem=40, raw_out=(0,), near=(0, 1),
         )
         whole = [((inner_width, width), F32), ((width, width), F32), ((width, 3 * width), F32)]
         grad_w_out, grad_w_proj, grad_w_qkv, grad_w_in = call(

time: 238 us -> 234 us (0.983)
  Pallas kernels: 74.2 us -> 70.5 us
    pallas_call x14, Pallas kernels: 74.2 us -> 70.5 us  [call(): pl.pallas_call(run, out_shape=[jax.ShapeDtypeStruct(s, d) for s, d in out...]
  transfers between devices with their start and end apart: 16 -> 16, of which waited for: 10 -> 10; matrix products, arithmetic and copies ran while one was open for 2% -> 2% of each run, Pallas kernels for 17% -> 16%
where the time goes in v4:
time: 234 us; the launch traced here: 232 us
  Pallas kernels  70.5 us (30%)
  waiting for transfers between devices  53.1 us (23%)
  starting transfers between devices  44.5 us (19%)
  blocking collectives  42 us (18%)
  between operations  14.2 us (6%)
  other arithmetic  4.69 us (2%)
  local copies, waits for them, and re-layouts  2.87 us (1%)
    pallas_call x14, Pallas kernels, call(): pl.pallas_call(run, out_shape=[jax.ShapeDtypeStruct(s, d) for s, d in out...  70.5 us
    all_to_all x1, blocking collectives, own_core(): lax.all_to_all(value, ('dp', 'seq'), 0, 0, tiled=True, axis_index_groups=...  24.3 us
    all_to_all x4, starting transfers between devices, exchange(): return lax.all_to_all(value, axes, 0, 0, tiled=True)  22.5 us
    ppermute x1, waiting for transfers between devices, body(): lax.ppermute(grad_halo, 'seq', [(i + 1, i) for i in range(seq_size - 1)])  20.7 us
    all_to_all x1, blocking collectives, exchange(): return lax.all_to_all(value, axes, 0, 0, tiled=True)  17.7 us
    ppermute x1, waiting for transfers between devices, body(): across = lax.ppermute(across, 'dp', [(g, g ^ 2) for g in range(groups)])  9.87 us
    all_to_all x4, waiting for transfers between devices, exchange(): return lax.all_to_all(value, axes, 0, 0, tiled=True)  8.64 us
    ppermute x3, starting transfers between devices, other_core(): return lax.ppermute(value, 'dp', [(g, g ^ 1) for g in range(groups)])  7.81 us
  transfers between devices with their start and end apart: 16, of which 10 were waited for; matrix products, arithmetic and copies ran while one was open for 2% of the time, Pallas kernels for 16%

profile of v4, /device:TPU:13, one launch (start us, length us, event | category | flops | bytes accessed | tf_op | source)
XLA Modules:
  0.0 231.8 jit_solution(12036508262197141926)
XLA Ops:
  7.2 0.7 slice.34
  7.9 3.1 %collective-permute-start = (bf16[16,512]{1,0:T(8,128)(2,1)S(1)}, bf16[16,512]{1,0:T(8,128)(2,1)S(1)}, u32[]{:S(2)}, u32[]{:S(2)}) collective-permute-start(bf16[16,512]{1,0:T(8,128)(2,1)S(1)} %slice.34), channel_id=1, source_target_pairs={{0,1},{1,2},{2,3},{3,4},{4,5},{5,6},{6,7},{8,9},{9,10},{10,11},{11... | collective-permute-start | bytes 49160 | tf_op jit(solution)/shard_map/ppermute | solution.py:824
  11.0 1.3 collective-permute-done.refs_1_.refs_4_
  12.4 0.6 copy-done.7
  13.0 7.3 %forward.1 = (bf16[8,160,128]{2,1,0:T(8,128)(2,1)}, bf16[144,512]{1,0:T(8,128)(2,1)}, bf16[144,1024]{1,0:T(8,128)(2,1)}, bf16[128,1024]{1,0:T(8,128)(2,1)}, bf16...) custom-call(bf16[128,512]{1,0:T(8,128)(2,1)} %refs_3_.5, ...), custom_call_target="tpu_custom_call" | custom-call | flops 1000 | bytes 1000 | tf_op jit(solution)/shard_map/forward/pallas_call | solution.py:775
  20.3 5.7 %all-to-all-start = ((bf16[8,160,128]{2,1,0:T(8,128)(2,1)}), bf16[8,160,128]{2,1,0:T(8,128)(2,1)S(1)}, u32[]{:S(2)}, u32[]{:S(2)}) async-start(bf16[8,160,128]{2,1,0:T(8,128)(2,1)} %get-tuple-element.86), calls=%async_computation | async-start | bytes 655360 | tf_op jit(solution)/shard_map/all_to_all | solution.py:789
  25.9 2.1 grad_att.1.refs_12_
  28.0 4.8 %all-to-all-done.refs_0_.refs_1_ = bf16[8,160,128]{2,1,0:T(8,128)(2,1)S(1)} async-done(((bf16[8,160,128]{2,1,0:T(8,128)(2,1)}), bf16[8,160,128]{2,1,0:T(8,128)(2,1)S(1)}, u32[]{:S(2)}, u32[]{:S(2)}) %all-to-all-start) | async-done | bytes 327712 | tf_op jit(solution)/shard_map/all_to_all | solution.py:789
  32.8 0.7 copy-done.2
  33.6 6.4 %middle.1 = (bf16[8,128,256]{2,1,0:T(8,128)(2,1)}, f32[128,128]{1,0:T(8,128)}, f32[128,1024]{1,0:T(8,128)}, f32[128,512]{1,0:T(8,128)}, bf16[128,1024]{1,0:T(8,128)(2,1)}, /*index=5*/bf16[128,512]{1,0:T(8,128)(2,1)}) custom-call(bf16[8,160,128]{2,1,0:T(8,128)(2,1)} %copy-done.2, f32[128,128]{1,0:T(8,128)} %get-tuple-element.87.refs_1_.refs_12_.refs_2_, ...), custom_call_target="tpu_custom_call" | custom-call | flops 1000 | bytes 1000 | tf_op jit(solution)/shard_map/middle/pallas_call | solution.py:775
  40.0 6.4 %all-to-all-start.1 = ((bf16[8,128,256]{2,1,0:T(8,128)(2,1)}), bf16[8,128,256]{2,1,0:T(8,128)(2,1)S(1)}, u32[]{:S(2)}, u32[]{:S(2)}) async-start(bf16[8,128,256]{2,1,0:T(8,128)(2,1)} %get-tuple-element.93), calls=%async_computation.1 | async-start | bytes 1048576 | tf_op jit(solution)/shard_map/all_to_all | solution.py:789
  46.4 7.6 %states.1 = (f32[16512,128]{1,0:T(8,128)}, f32[128,1024]{1,0:T(8,128)}) custom-call(f32[128,128]{1,0:T(8,128)} %get-tuple-element.94.refs_0_, f32[128,128]{1,0:T(8,128)} %get-tuple-element.87.refs_1_.refs_12_.refs_2_, f32[128,32]{1,0:T(8,128)} %get-tuple-element.88.refs_2_.refs_13_.refs_3_, f32[1024,128]{1,0:T(8,128)} %get-tuple-element.89.refs_3_.refs_11_.refs_4_, ...), custom_call_target="tpu_custom_call" | custom-call | flops 1000 | bytes 1000 | tf_op jit(solution)/shard_map/states/pallas_call | solution.py:775
  53.9 3.8 %all-to-all-done.1.refs_0_ = bf16[8,128,256]{2,1,0:T(8,128)(2,1)S(1)} async-done(((bf16[8,128,256]{2,1,0:T(8,128)(2,1)}), bf16[8,128,256]{2,1,0:T(8,128)(2,1)S(1)}, u32[]{:S(2)}, u32[]{:S(2)}) %all-to-all-start.1) | async-done | bytes 524320 | tf_op jit(solution)/shard_map/all_to_all | solution.py:789
  57.8 0.8 copy-done.3
  58.6 6.1 %attention.1.refs_1_ = bf16[8,128,256]{2,1,0:T(8,128)(2,1)} custom-call(bf16[8,128,256]{2,1,0:T(8,128)(2,1)} %copy-done.3, bf16[8,160,128]{2,1,0:T(8,128)(2,1)} %copy-done.2, f32[16512,128]{1,0:T(8,128)} %get-tuple-element.96.refs_2_.refs_7_), custom_call_target="tpu_custom_call" | custom-call | flops 1000 | bytes 1000 | tf_op jit(solution)/shard_map/attention/pallas_call | solution.py:775
  64.6 17.7 %all_to_all.35.refs_0_ = bf16[8,128,256]{2,1,0:T(8,128)(2,1)} all-to-all(bf16[8,128,256]{2,1,0:T(8,128)(2,1)} %attention.1.refs_1_), channel_id=1, replica_groups=mesh['dp'=4,'seq'=8] {'seq'}, dimensions={0} | all-to-all | bytes 1048576 | tf_op jit(solution)/shard_map/all_to_all | solution.py:789
  82.3 7.0 %backward.1 = (bf16[128,512]{1,0:T(8,128)(2,1)}, f32[128,512]{1,0:T(8,128)}, f32[1,512]{1,0:T(1,128)}, bf16[128,1024]{1,0:T(8,128)(2,1)}, f32[1024,128]{1,0:T(8,...) custom-call(bf16[8,128,256]{2,1,0:T(8,128)(2,1)} %all_to_all.35.refs_0_, ...), custom_call_target="tpu_custom_call" | custom-call | flops 1000 | bytes 1000 | tf_op jit(solution)/shard_map/backward/pallas_call | solution.py:775
  89.3 2.5 %collective-permute-start.1 = (bf16[16,320,128]{2,1,0:T(8,128)(2,1)}, bf16[16,320,128]{2,1,0:T(8,128)(2,1)S(1)}, u32[]{:S(2)}, u32[]{:S(2)}) collective-permute-start(bf16[16,320,128]{2,1,0:T(8,128)(2,1)} %get-tuple-element.105), channel_id=1, source_target_pairs={{0,8},{8,0},{16,24},{24,16},{1,9},{9,1},{17,25},{25,17},{2,10},{10... | collective-permute-start | bytes 3932168 | tf_op jit(solution)/shard_map/ppermute | solution.py:800
  91.8 2.8 %collective-permute-done.1 = bf16[16,320,128]{2,1,0:T(8,128)(2,1)S(1)} collective-permute-done((bf16[16,320,128]{2,1,0:T(8,128)(2,1)}, bf16[16,320,128]{2,1,0:T(8,128)(2,1)S(1)}, u32[]{:S(2)}, u32[]{:S(2)}) %collective-permute-start.1) | collective-permute-done | bytes 1310752 | tf_op jit(solution)/shard_map/ppermute | solution.py:800
  94.6 2.1 add_convert_fusion.2
  96.7 1.2 collective-permute-start.2
  97.9 5.2 %all-to-all-start.3 = ((bf16[8,128,128]{2,1,0:T(8,128)(2,1)}), bf16[8,128,128]{2,1,0:T(8,128)(2,1)S(1)}, u32[]{:S(2)}, u32[]{:S(2)}) async-start(bf16[8,128,128]{2,1,0:T(8,128)(2,1)} %get-tuple-element.102), calls=%async_computation.3 | async-start | bytes 524288 | tf_op jit(solution)/shard_map/all_to_all | solution.py:789
  103.1 9.9 %collective-permute-done.2 = bf16[8,320,128]{2,1,0:T(8,128)(2,1)S(1)} collective-permute-done((bf16[8,320,128]{2,1,0:T(8,128)(2,1)}, bf16[8,320,128]{2,1,0:T(8,128)(2,1)S(1)}, u32[]{:S(2)}, u32[]{:S(2)}) %collective-permute-start.2) | collective-permute-done | bytes 655392 | tf_op jit(solution)/shard_map/ppermute | solution.py:884
  113.0 1.1 add_convert_fusion.1.refs_8_
  114.1 5.3 %all-to-all-start.4 = ((bf16[8,320,128]{2,1,0:T(8,128)(2,1)}), bf16[8,320,128]{2,1,0:T(8,128)(2,1)S(1)}, u32[]{:S(2)}, u32[]{:S(2)}) async-start(bf16[8,320,128]{2,1,0:T(8,128)(2,1)} %add_convert_fusion.1.refs_8_), calls=%async_computation.4 | async-start | bytes 1310720 | tf_op jit(solution)/shard_map/all_to_all | solution.py:789
  119.4 11.4 %adjoint.1 = (f32[1024,128]{1,0:T(8,128)}, f32[1024,128]{1,0:T(8,128)}, f32[128,64]{1,0:T(8,128)}, f32[128,128]{1,0:T(8,128)}) custom-call(bf16[8,128,128]{2,1,0:T(8,128)(2,1)} %copy-done.5, bf16[8,160,128]{2,1,0:T(8,128)(2,1)} %copy-done.2, f32[128,128]{1,0:T(8,128)} %get-tuple-element.87.refs_1_.refs_12_.refs_2_, ...), custom_call_target="tpu_custom_call" | custom-call | flops 1000 | bytes 1000 | tf_op jit(solution)/shard_map/adjoint/pallas_call | solution.py:775
  130.8 6.0 %inner.1 = (bf16[16,160,128]{2,1,0:T(8,128)(2,1)}, bf16[16,160,128]{2,1,0:T(8,128)(2,1)}, bf16[144,1024]{1,0:T(8,128)(2,1)}) custom-call(f32[1024,128]{1,0:T(8,128)} %get-tuple-element.106.refs_0_, f32[1024,128]{1,0:T(8,128)} %get-tuple-element.107.refs_1_, f32[1024,128]{1,0:T(8,128)} %get-tuple-element.103.refs_6_.refs_2_, ...), custom_call_target="tpu_custom_call" | custom-call | flops 1000 | bytes 1000 | tf_op jit(solution)/shard_map/inner/pallas_call | solution.py:775
  136.8 1.6 collective-permute-start.3
  138.4 3.5 %tokens.1 = (f32[128,512]{1,0:T(8,128)}, f32[8,512]{1,0:T(8,128)}, bf16[16,128]{1,0:T(8,128)(2,1)}) custom-call(bf16[144,1024]{1,0:T(8,128)(2,1)} %get-tuple-element.117.refs_0_, bf16[512,2048]{1,0:T(8,128)(2,1)} %refs_1_.3, bf16[128,1024]{1,0:T(8,128)(2,1)} %get-tuple-element.118.refs_2_, bf16[128,512]{1,0:T(8,128)(2,1)} %refs_3_.5, ...), custom_call_target="tpu_custom_call" | custom-call | flops 1000 | bytes 1000 | tf_op jit(solution)/shard_map/tokens/pallas_call | solution.py:775
  141.9 2.9 %head_products.1 = (bf16[192,128]{1,0:T(8,128)(2,1)}, bf16[192,128]{1,0:T(8,128)(2,1)}, bf16[192,128]{1,0:T(8,128)(2,1)}, bf16[192,128]{1,0:T(8,128)(2,1)}) custom-call(bf16[1024,512]{1,0:T(8,128)(2,1)} %all-gather.4.cloned.1.call-done.refs_0_, bf16[8,128,256]{2,1,0:T(8,128)(2,1)} %attention.1.refs_1_, bf16[16,128]{1,0:T(8,128)(2,1)} %get-tuple-element.120.refs_2_.refs_5_.refs_1_), custom_call_target="tpu_custom_call" | custom-call | flops 1000 | bytes 1000 | tf_op jit(solution)/shard_map/head_products/pallas_call | solution.py:775
  144.9 0.1 collective-permute-start.4
  145.0 1.3 collective-permute-start.5
  146.3 0.9 collective-permute-start.6
  147.1 0.2 add_convert_fusion
  147.3 0.9 collective-permute-done.5.refs_3_
  148.2 2.6 %collective-permute-done.6.refs_4_ = bf16[192,128]{1,0:T(8,128)(2,1)S(1)} collective-permute-done((bf16[192,128]{1,0:T(8,128)(2,1)}, bf16[192,128]{1,0:T(8,128)(2,1)S(1)}, u32[]{:S(2)}, u32[]{:S(2)}) %collective-permute-start.6) | collective-permute-done | bytes 49184 | tf_op jit(solution)/shard_map/ppermute | solution.py:918
  150.8 1.3 early_sum.1
  152.1 24.3 %all_to_all.36.refs_0_ = bf16[16,160,128]{2,1,0:T(8,128)(2,1)S(1)} all-to-all(bf16[16,160,128]{2,1,0:T(8,128)(2,1)S(1)} %add_convert_fusion), channel_id=1, replica_groups={{0,1,2,3,4,5,6,7,16,17,18,19,20,21,22,23},{8,9,10,11,12,13,14,15,24,25,..., dimensions={0} | all-to-all | bytes 1310720 | tf_op jit(solution)/shard_map/all_to_all | solution.py:796
  176.4 1.2 late_sum.1
  177.6 5.4 %all-to-all-start.6 = ((bf16[16,176,128]{2,1,0:T(8,128)(2,1)}), bf16[16,176,128]{2,1,0:T(8,128)(2,1)S(1)}, u32[]{:S(2)}, u32[]{:S(2)}) async-start(bf16[16,176,128]{2,1,0:T(8,128)(2,1)} %late_sum.1), calls=%async_computation.6 | async-start | bytes 1441792 | tf_op jit(solution)/shard_map/all_to_all | solution.py:796
  183.0 2.2 collective-permute-start.7
  185.2 20.7 %collective-permute-done.7 = f32[8,512]{1,0:T(8,128)S(1)} collective-permute-done((f32[8,512]{1,0:T(8,128)S(1)}, f32[8,512]{1,0:T(8,128)S(1)}, u32[]{:S(2)}, u32[]{:S(2)}) %collective-permute-start.7) | collective-permute-done | bytes 16416 | tf_op jit(solution)/shard_map/ppermute | solution.py:909
  205.9 1.3 add_dynamic-update-slice_fusion
  207.3 3.7 %collective-permute-start.8 = (bf16[16,176,128]{2,1,0:T(8,128)(2,1)S(1)}, bf16[16,176,128]{2,1,0:T(8,128)(2,1)S(1)}, u32[]{:S(2)}, u32[]{:S(2)}) collective-permute-start(bf16[16,176,128]{2,1,0:T(8,128)(2,1)S(1)} %all-to-all-done.6.refs_0_), channel_id=1, source_target_pairs={{0,8},{8,0},{16,24},{24,16},{1,9},{9,1},{17,25},{25,17},{2,10},{10... | collective-permute-start | bytes 2162696 | tf_op jit(solution)/shard_map/ppermute | solution.py:800
  211.0 1.8 collective-permute-done.8.refs_1_
  212.8 2.9 %late_assembly.1 = (f32[512,2048]{1,0:T(8,128)}, f32[1,512]{1,0:T(1,128)}, f32[4,1024]{1,0:T(4,128)}, f32[1,1024]{1,0:T(1,128)}, f32[64,1024]{1,0:T(8,128)}, /*i...) custom-call(bf16[16,176,128]{2,1,0:T(8,128)(2,1)S(1)} %all-to-all-done.6., ...), custom_call_target="tpu_custom_call" | custom-call | flops 1000 | bytes 1000 | tf_op jit(solution)/shard_map/late_assembly/pallas_call | solution.py:775
  215.7 4.4 %all-gather.6.cloned.1.call-done = bf16[16384,128]{1,0:T(8,128)(2,1)} async-done(((bf16[512,128]{1,0:T(8,128)(2,1)}), bf16[16384,128]{1,0:T(8,128)(2,1)}) %all-gather.6.cloned.1.call-update) | async-done | bytes 4194320 | tf_op jit(solution)/shard_map/all_gather | solution.py:928
  220.0 4.9 %early_assembly.1 = (f32[1024,512]{1,0:T(8,128)}, f32[512,512]{1,0:T(8,128)}, f32[512,1536]{1,0:T(8,128)}, f32[512,2048]{1,0:T(8,128)}) custom-call(bf16[32,512,128]{2,1,0:T(8,128)(2,1)} %bitcast.16, f32[512,2048]{1,0:T(8,128)} %get-tuple-element.132.refs_1_), custom_call_target="tpu_custom_call", output_to_operand_aliasing={{3}: (1, {})} | custom-call | flops 1000 | bytes 1000 | tf_op jit(solution)/shard_map/early_assembly/pallas_call | solution.py:775
  (25 shorter events, 0.1 us)
Async XLA Ops:
  7.9 4.5 %collective-permute-start = (bf16[16,512]{1,0:T(8,128)(2,1)S(1)}, bf16[16,512]{1,0:T(8,128)(2,1)S(1)}, u32[]{:S(2)}, u32[]{:S(2)}) collective-permute-start(bf16[16,512]{1,0:T(8,128)(2,1)S(1)} %slice.34), channel_id=1, source_target_pairs={{0,1},{1,2},{2,3},{3,4},{4,5},{5,6},{6,7},{8,9},{9,10},{10,11},{11... | collective-permute-start | bytes 49160 | tf_op jit(solution)/shard_map/ppermute | solution.py:824
  12.4 0.6 copy-start.7
  20.3 12.6 %all-to-all-start = ((bf16[8,160,128]{2,1,0:T(8,128)(2,1)}), bf16[8,160,128]{2,1,0:T(8,128)(2,1)S(1)}, u32[]{:S(2)}, u32[]{:S(2)}) async-start(bf16[8,160,128]{2,1,0:T(8,128)(2,1)} %get-tuple-element.86), calls=%async_computation | async-start | bytes 655360 | tf_op jit(solution)/shard_map/all_to_all | solution.py:789
  32.8 0.7 copy-start.2
  40.0 17.8 %all-to-all-start.1 = ((bf16[8,128,256]{2,1,0:T(8,128)(2,1)}), bf16[8,128,256]{2,1,0:T(8,128)(2,1)S(1)}, u32[]{:S(2)}, u32[]{:S(2)}) async-start(bf16[8,128,256]{2,1,0:T(8,128)(2,1)} %get-tuple-element.93), calls=%async_computation.1 | async-start | bytes 1048576 | tf_op jit(solution)/shard_map/all_to_all | solution.py:789
  46.4 95.6 %all-gather.4.cloned.1.call-start = ((), (), s32[]{:S(2)}) async-start(), calls=%async_computation.7 | async-start | bytes 1179648 | tf_op jit(solution)/shard_map/all_gather | solution.py:879
  57.8 0.8 copy-start.3
  89.3 5.4 %collective-permute-start.1 = (bf16[16,320,128]{2,1,0:T(8,128)(2,1)}, bf16[16,320,128]{2,1,0:T(8,128)(2,1)S(1)}, u32[]{:S(2)}, u32[]{:S(2)}) collective-permute-start(bf16[16,320,128]{2,1,0:T(8,128)(2,1)} %get-tuple-element.105), channel_id=1, source_target_pairs={{0,8},{8,0},{16,24},{24,16},{1,9},{9,1},{17,25},{25,17},{2,10},{10... | collective-permute-start | bytes 3932168 | tf_op jit(solution)/shard_map/ppermute | solution.py:800
  91.8 21.2 %copy-start.4 = (bf16[16,320,128]{2,1,0:T(8,128)(2,1)S(1)}, bf16[16,320,128]{2,1,0:T(8,128)(2,1)}, u32[]{:S(2)}) copy-start(bf16[16,320,128]{2,1,0:T(8,128)(2,1)} %get-tuple-element.104) | copy-start | bytes 3932164
  96.7 16.3 %collective-permute-start.2 = (bf16[8,320,128]{2,1,0:T(8,128)(2,1)}, bf16[8,320,128]{2,1,0:T(8,128)(2,1)S(1)}, u32[]{:S(2)}, u32[]{:S(2)}) collective-permute-start(bf16[8,320,128]{2,1,0:T(8,128)(2,1)} %add_convert_fusion.2), channel_id=1, source_target_pairs={{0,16},{8,24},{16,0},{24,8},{1,17},{9,25},{17,1},{25,9},{2,18},{10... | collective-permute-start | bytes 1966088 | tf_op jit(solution)/shard_map/ppermute | solution.py:884
  97.9 16.2 %all-to-all-start.3 = ((bf16[8,128,128]{2,1,0:T(8,128)(2,1)}), bf16[8,128,128]{2,1,0:T(8,128)(2,1)S(1)}, u32[]{:S(2)}, u32[]{:S(2)}) async-start(bf16[8,128,128]{2,1,0:T(8,128)(2,1)} %get-tuple-element.102), calls=%async_computation.3 | async-start | bytes 524288 | tf_op jit(solution)/shard_map/all_to_all | solution.py:789
  114.1 5.3 %copy-start.5 = (bf16[8,128,128]{2,1,0:T(8,128)(2,1)}, bf16[8,128,128]{2,1,0:T(8,128)(2,1)S(1)}, u32[]{:S(2)}) copy-start(bf16[8,128,128]{2,1,0:T(8,128)(2,1)S(1)} %all-to-all-done.3.refs_0_) | copy-start | bytes 786436
  114.1 36.7 %all-to-all-start.4 = ((bf16[8,320,128]{2,1,0:T(8,128)(2,1)}), bf16[8,320,128]{2,1,0:T(8,128)(2,1)S(1)}, u32[]{:S(2)}, u32[]{:S(2)}) async-start(bf16[8,320,128]{2,1,0:T(8,128)(2,1)} %add_convert_fusion.1.refs_8_), calls=%async_computation.4 | async-start | bytes 1310720 | tf_op jit(solution)/shard_map/all_to_all | solution.py:789
  119.4 100.7 %all-gather.6.cloned.1.call-start = ((), (), s32[]{:S(2)}) async-start(), calls=%async_computation.8 | async-start | bytes 4325376 | tf_op jit(solution)/shard_map/all_gather | solution.py:928
  136.8 10.3 %collective-permute-start.3 = (bf16[16,160,128]{2,1,0:T(8,128)(2,1)}, bf16[16,160,128]{2,1,0:T(8,128)(2,1)S(1)}, u32[]{:S(2)}, u32[]{:S(2)}) collective-permute-start(bf16[16,160,128]{2,1,0:T(8,128)(2,1)} %get-tuple-element.115), channel_id=1, source_target_pairs={{0,8},{8,0},{16,24},{24,16},{1,9},{9,1},{17,25},{25,17},{2,10},{10... | collective-permute-start | bytes 1966088 | tf_op jit(solution)/shard_map/ppermute | solution.py:800
  141.9 5.2 %copy-start.6 = (bf16[16,160,128]{2,1,0:T(8,128)(2,1)S(1)}, bf16[16,160,128]{2,1,0:T(8,128)(2,1)}, u32[]{:S(2)}) copy-start(bf16[16,160,128]{2,1,0:T(8,128)(2,1)} %get-tuple-element.114) | copy-start | bytes 1966084
  144.9 5.9 %copy-start = (bf16[192,128]{1,0:T(8,128)(2,1)S(1)}, bf16[192,128]{1,0:T(8,128)(2,1)}, u32[]{:S(2)}) copy-start(bf16[192,128]{1,0:T(8,128)(2,1)} %get-tuple-element.121.refs_1_) | copy-start | bytes 147460
  144.9 5.9 %copy-start.1 = (bf16[16,128]{1,0:T(8,128)(2,1)S(1)}, bf16[16,128]{1,0:T(8,128)(2,1)}, u32[]{:S(2)}) copy-start(bf16[16,128]{1,0:T(8,128)(2,1)} %get-tuple-element.120.refs_2_.refs_5_.refs_1_) | copy-start | bytes 12292
  144.9 2.4 %collective-permute-start.4 = (bf16[192,128]{1,0:T(8,128)(2,1)}, bf16[192,128]{1,0:T(8,128)(2,1)S(1)}, u32[]{:S(2)}, u32[]{:S(2)}) collective-permute-start(bf16[192,128]{1,0:T(8,128)(2,1)} %get-tuple-element.122), channel_id=1, source_target_pairs={{0,8},{8,0},{16,24},{24,16},{1,9},{9,1},{17,25},{25,17},{2,10},{10... | collective-permute-start | bytes 147464 | tf_op jit(solution)/shard_map/ppermute | solution.py:918
  145.0 3.2 %collective-permute-start.5 = (bf16[192,128]{1,0:T(8,128)(2,1)}, bf16[192,128]{1,0:T(8,128)(2,1)S(1)}, u32[]{:S(2)}, u32[]{:S(2)}) collective-permute-start(bf16[192,128]{1,0:T(8,128)(2,1)} %get-tuple-element.123), channel_id=1, source_target_pairs={{0,16},{8,24},{16,0},{24,8},{1,17},{9,25},{17,1},{25,9},{2,18},{10... | collective-permute-start | bytes 147464 | tf_op jit(solution)/shard_map/ppermute | solution.py:918
  146.3 4.5 %collective-permute-start.6 = (bf16[192,128]{1,0:T(8,128)(2,1)}, bf16[192,128]{1,0:T(8,128)(2,1)S(1)}, u32[]{:S(2)}, u32[]{:S(2)}) collective-permute-start(bf16[192,128]{1,0:T(8,128)(2,1)} %get-tuple-element.124), channel_id=1, source_target_pairs={{0,24},{8,16},{16,8},{24,0},{1,25},{9,17},{17,9},{25,1},{2,26},{10... | collective-permute-start | bytes 147464 | tf_op jit(solution)/shard_map/ppermute | solution.py:918
  176.4 6.6 %copy-start.8 = (f32[8,512]{1,0:T(8,128)S(1)}, f32[8,512]{1,0:T(8,128)}, u32[]{:S(2)}) copy-start(f32[8,512]{1,0:T(8,128)} %get-tuple-element.127) | copy-start | bytes 49156
  177.6 29.7 %all-to-all-start.6 = ((bf16[16,176,128]{2,1,0:T(8,128)(2,1)}), bf16[16,176,128]{2,1,0:T(8,128)(2,1)S(1)}, u32[]{:S(2)}, u32[]{:S(2)}) async-start(bf16[16,176,128]{2,1,0:T(8,128)(2,1)} %late_sum.1), calls=%async_computation.6 | async-start | bytes 1441792 | tf_op jit(solution)/shard_map/all_to_all | solution.py:796
  183.0 22.9 %collective-permute-start.7 = (f32[8,512]{1,0:T(8,128)S(1)}, f32[8,512]{1,0:T(8,128)S(1)}, u32[]{:S(2)}, u32[]{:S(2)}) collective-permute-start(f32[8,512]{1,0:T(8,128)S(1)} %copy-done.8), channel_id=1, source_target_pairs={{1,0},{2,1},{3,2},{4,3},{5,4},{6,5},{7,6},{9,8},{10,9},{11,10},{12... | collective-permute-start | bytes 49160 | tf_op jit(solution)/shard_map/ppermute | solution.py:909
  207.3 5.5 %collective-permute-start.8 = (bf16[16,176,128]{2,1,0:T(8,128)(2,1)S(1)}, bf16[16,176,128]{2,1,0:T(8,128)(2,1)S(1)}, u32[]{:S(2)}, u32[]{:S(2)}) collective-permute-start(bf16[16,176,128]{2,1,0:T(8,128)(2,1)S(1)} %all-to-all-done.6.refs_0_), channel_id=1, source_target_pairs={{0,8},{8,0},{16,24},{24,16},{1,9},{9,1},{17,25},{25,17},{2,10},{10... | collective-permute-start | bytes 2162696 | tf_op jit(solution)/shard_map/ppermute | solution.py:800
Sparse Core Ops, SparseCore 0:
  91.9 47.0 all-gather.3
  152.2 67.7 all-gather.5

commit v5 on v4

--- a/solution.py
+++ b/solution.py
@@ -160,7 +160,7 @@
 
 
 def middle_kernel(
-    msg, a_ref, bc, s_ref, dx_ref, mixed, gate, d_skip, tok, w_out, n2, w_qkv, grad_att,
+    msg, a_ref, bc, s_ref, dx_ref, mixed, gate, d_skip, tok, w_out, n2, w_qkv, cot, w_proj,
     o_qkvg, o_start, o_ssm, o_after, o_gated, o_normed,
     y_ref,
 ):
@@ -209,13 +209,14 @@
     normed = (after * rms_parts(after) * n2[...]).astype(BF)
     o_normed[...] = normed
     sent(o_normed)
-    w_qkv, grad_att = ready(w_qkv, grad_att)
+    w_qkv, cot, w_proj = ready(w_qkv, cot, w_proj)
     qkv = dot(normed, w_qkv[...])
+    grad_att = dot_nt(cot[...], w_proj[...])
     copies = o_qkvg.shape[0] // H
     left = lax.broadcasted_iota(jnp.int32, (count, LANES), 1) < HD
     for p in range(H // 2):
         q, k, v = (qkv[:, i * width + p * LANES : i * width + (p + 1) * LANES] for i in range(3))
-        g = grad_att[:, tile(p)].astype(F32)
+        g = grad_att[:, tile(p)]
         first = (jnp.where(left, q, pltpu.roll(k, HD, 1)), jnp.where(left, v, pltpu.roll(g, HD, 1)))
         second = (jnp.where(left, pltpu.roll(q, HD, 1), k), jnp.where(left, pltpu.roll(v, HD, 1), g))
         for h, pair in ((2 * p, first), (2 * p + 1, second)):
@@ -223,11 +224,6 @@
                 value = value.astype(BF)
                 for r in range(copies):
                     o_qkvg[h * copies + r, :, tile(i)] = value
-
-
-def grad_att_kernel(cot, w_proj, o_grad):
-    cot, w_proj = ready(cot, w_proj)
-    o_grad[...] = dot_nt(cot[...], w_proj[...]).astype(BF)
 
 
 def attention_kernel(qkvg, ends, o_back, qz, kr, gz, vr, dk, dv):
@@ -581,18 +577,17 @@
 
 
 def head_products_kernel(normed, back, *rest):
-    *outs, grad, last = rest
+    *outs, pieces = rest
     normed, back = ready(normed, back)
     both = back[...].reshape(back.shape[0] * back.shape[1], 2 * LANES)
-    grad[...] = dot_tn(normed[...], both[:, :LANES])
-    last[...] = dot_tn(normed[...], both[:, LANES:])
+    grad = dot_tn(both, normed[...])
     left = lax.broadcasted_iota(jnp.int32, (HD, LANES), 1) < HD
+    for g in range(len(outs)):
+        pieces[g, : 2 * HD, :] = jnp.transpose(grad[:LANES, tile(g)])
+        value = jnp.transpose(grad[LANES:, tile(g)])
+        pieces[g, 2 * HD :, :] = jnp.where(left, value[:HD], pltpu.roll(value[HD:], HD, 1))
     for distance, to in enumerate(outs):
-        g = lax.bitwise_xor(lax.axis_index("dp"), distance)
-        to[: 2 * HD, :] = grad[pl.ds(pl.multiple_of(g * LANES, LANES), LANES), :].astype(BF)
-        low = last[pl.ds(pl.multiple_of(g * LANES, LANES), HD), :]
-        high = last[pl.ds(pl.multiple_of(g * LANES + HD, HD), HD), :]
-        to[2 * HD :, :] = jnp.where(left, low, pltpu.roll(high, HD, 1)).astype(BF)
+        to[...] = pieces[lax.bitwise_xor(lax.axis_index("dp"), distance)].astype(BF)
 
 
 def early_sum_kernel(parts, *heads):
@@ -834,9 +829,6 @@
         name="forward", us=0, near=(1,),
     )
     msg = exchange(msg, "seq")
-    (grad_att,) = call(
-        grad_att_kernel, [((count, width), BF)], [], cotangent, w_proj, name="grad_att", us=0
-    )
     qkvg, start, ssm, after, gated, normed_two = call(
         middle_kernel,
         [
@@ -844,7 +836,7 @@
             ((count, width), F32), ((count, inner_width), BF), ((count, width), BF),
         ],
         [vmem(*blocks)],
-        msg, a, bc, s, dx, mixed, gate, skip, tokens, w_out, n2, w_qkv, grad_att,
+        msg, a, bc, s, dx, mixed, gate, skip, tokens, w_out, n2, w_qkv, cotangent, w_proj,
         name="middle", us=0, scalars=(2,), views={0: np.s_[:, : ends_at + 16, :]}, near=(0,),
     )
     qkvg = exchange(qkvg, "seq")
@@ -858,7 +850,7 @@
         attention_kernel,
         [((seq_size, count, 2 * LANES), BF)],
         [vmem((rows, LANES), BF)] * 4 + [vmem((rows, LANES), F32)] * 2,
-        qkvg, msg, name="attention", us=0, views={1: np.s_[:, ends_at + 16 :, :]}, after=(every,), near=(0,),
+        qkvg, msg, name="attention", us=0, views={1: np.s_[:, ends_at + 16 :, :]},  near=(0,),
     )
     back_own = exchange(back, "seq")
     pieces = [((peers, 2 * LANES + HD, LANES), BF)] * 2
@@ -882,6 +874,7 @@
         received = other_core(send, groups)
         across = add(keep[seq_size:], received[seq_size:])
         across = lax.ppermute(across, "dp", [(g, g ^ 2) for g in range(groups)])
+        across, slope = lax.optimization_barrier((across, slope))
         part = add(keep[:seq_size], received[:seq_size], across)
         between = (part,)
         part = exchange(part, "seq")
@@ -911,8 +904,8 @@
     flat = lambda v: v.reshape(-1)
     if tiled:
         head, *heads = call(
-            head_products_kernel, [((3 * HD, LANES), BF)] * groups, [vmem((width, LANES), F32)] * 2,
-            normed_two_all, back, name="head_products", us=0, after=(grad_n1,),
+            head_products_kernel, [((3 * HD, LANES), BF)] * groups, [vmem((groups, 3 * HD, LANES), F32)],
+            normed_two_all, back, name="head_products", us=0, after=(grad_inner,),
         )
         heads = [
             lax.ppermute(piece, "dp", [(g, g ^ distance) for g in range(groups)])
@@ -920,7 +913,7 @@
         ]
         (early,) = call(
             early_sum_kernel, [((part.shape[1] + head.shape[0], LANES), BF)], [], part, head, *heads,
-            name="early_sum", us=0, vmem=40, after=(grad_n1,), near=(0, 2, 3, 4),
+            name="early_sum", us=0, vmem=40, near=(0, 2, 3, 4),
         )
         late = add(sums[0], other_core(small, groups))
         late, early = lax.optimization_barrier((late, early))

time: 234 us -> 232 us (level)
  starting transfers between devices: 44.5 us -> 38.5 us
  blocking collectives: 42 us -> 47.7 us
    all_to_all x1 -> x3, blocking collectives: 17.7 us -> 47.7 us  [exchange(): return lax.all_to_all(value, axes, 0, 0, tiled=True)]
    all_to_all x1 -> x0, blocking collectives: 24.3 us -> none  [own_core(): lax.all_to_all(value, ('dp', 'seq'), 0, 0, tiled=True, axis_index_groups=...]
    all_to_all x1 -> x2, waiting for transfers between devices: 0.01 us -> 15.1 us  [own_core(): lax.all_to_all(value, ('dp', 'seq'), 0, 0, tiled=True, axis_index_groups=...]
    all_to_all x4 -> x2, starting transfers between devices: 22.5 us -> 10.6 us  [exchange(): return lax.all_to_all(value, axes, 0, 0, tiled=True)]
    all_to_all x4 -> x2, waiting for transfers between devices: 8.64 us -> 0.01 us  [exchange(): return lax.all_to_all(value, axes, 0, 0, tiled=True)]
    ppermute x1, waiting for transfers between devices: 9.87 us -> 2.22 us  [body(): across = lax.ppermute(across, 'dp', [(g, g ^ 2) for g in range(groups)])]
    all_to_all x1 -> x2, starting transfers between devices: 5.41 us -> 11.9 us  [own_core(): lax.all_to_all(value, ('dp', 'seq'), 0, 0, tiled=True, axis_index_groups=...]
    pallas_call x14 -> x13, Pallas kernels: 70.5 us -> 68.5 us  [call(): pl.pallas_call(run, out_shape=[jax.ShapeDtypeStruct(s, d) for s, d in out...]
  transfers between devices with their start and end apart: 16 -> 15, of which waited for: 10 -> 10; matrix products, arithmetic and copies ran while one was open for 2% -> 2% of each run, Pallas kernels for 16% -> 15%
where the time goes in v5:
time: 232 us; the launch traced here: 229 us
  Pallas kernels  68.5 us (30%)
  waiting for transfers between devices  52.5 us (23%)
  blocking collectives  47.7 us (21%)
  starting transfers between devices  38.5 us (17%)
  between operations  14.2 us (6%)
  other arithmetic  5.52 us (2%)
    pallas_call x13, Pallas kernels, call(): pl.pallas_call(run, out_shape=[jax.ShapeDtypeStruct(s, d) for s, d in out...  68.5 us
    all_to_all x3, blocking collectives, exchange(): return lax.all_to_all(value, axes, 0, 0, tiled=True)  47.7 us
    ppermute x1, waiting for transfers between devices, body(): lax.ppermute(grad_halo, 'seq', [(i + 1, i) for i in range(seq_size - 1)])  21.9 us
    all_to_all x2, waiting for transfers between devices, own_core(): lax.all_to_all(value, ('dp', 'seq'), 0, 0, tiled=True, axis_index_groups=...  15.1 us
    all_to_all x2, starting transfers between devices, own_core(): lax.all_to_all(value, ('dp', 'seq'), 0, 0, tiled=True, axis_index_groups=...  11.9 us
    all_to_all x2, starting transfers between devices, exchange(): return lax.all_to_all(value, axes, 0, 0, tiled=True)  10.6 us
    ppermute x3, starting transfers between devices, other_core(): return lax.ppermute(value, 'dp', [(g, g ^ 1) for g in range(groups)])  6.16 us
    ppermute x3, waiting for transfers between devices, other_core(): return lax.ppermute(value, 'dp', [(g, g ^ 1) for g in range(groups)])  4.67 us
  transfers between devices with their start and end apart: 15, of which 10 were waited for; matrix products, arithmetic and copies ran while one was open for 2% of the time, Pallas kernels for 15%

profile of v5, /device:TPU:13, one launch (start us, length us, event | category | flops | bytes accessed | tf_op | source)
XLA Modules:
  0.0 228.9 jit_solution(415682842062980005)
XLA Ops:
  7.2 0.0 all-gather.4.cloned.1.call-start
  7.2 0.7 slice.34
  7.9 3.1 %collective-permute-start = (bf16[16,512]{1,0:T(8,128)(2,1)S(1)}, bf16[16,512]{1,0:T(8,128)(2,1)S(1)}, u32[]{:S(2)}, u32[]{:S(2)}) collective-permute-start(bf16[16,512]{1,0:T(8,128)(2,1)S(1)} %slice.34), channel_id=1, source_target_pairs={{0,1},{1,2},{2,3},{3,4},{4,5},{5,6},{6,7},{8,9},{9,10},{10,11},{11... | collective-permute-start | bytes 49160 | tf_op jit(solution)/shard_map/ppermute | solution.py:819
  11.1 1.3 collective-permute-done.refs_1_.refs_4_
  12.4 0.6 copy-done.5
  13.0 7.3 %forward.1 = (bf16[8,160,128]{2,1,0:T(8,128)(2,1)}, bf16[144,512]{1,0:T(8,128)(2,1)}, bf16[144,1024]{1,0:T(8,128)(2,1)}, bf16[128,1024]{1,0:T(8,128)(2,1)}, bf16...) custom-call(bf16[128,512]{1,0:T(8,128)(2,1)} %refs_3_.5, ...), custom_call_target="tpu_custom_call" | custom-call | flops 1000 | bytes 1000 | tf_op jit(solution)/shard_map/forward/pallas_call | solution.py:770
  20.3 12.5 %all_to_all.35.refs_0_.refs_1_ = bf16[8,160,128]{2,1,0:T(8,128)(2,1)} all-to-all(bf16[8,160,128]{2,1,0:T(8,128)(2,1)} %get-tuple-element.88), channel_id=1, replica_groups=mesh['dp'=4,'seq'=8] {'seq'}, dimensions={0} | all-to-all | bytes 655360 | tf_op jit(solution)/shard_map/all_to_all | solution.py:784
  32.8 6.6 %middle.1 = (bf16[8,128,256]{2,1,0:T(8,128)(2,1)}, f32[128,128]{1,0:T(8,128)}, f32[128,1024]{1,0:T(8,128)}, f32[128,512]{1,0:T(8,128)}, bf16[128,1024]{1,0:T(8,128)(2,1)}, /*index=5*/bf16[128,512]{1,0:T(8,128)(2,1)}) custom-call(bf16[8,160,128]{2,1,0:T(8,128)(2,1)} %all_to_all.35.refs_0_.refs_1_, f32[128,128]{1,0:T(8,128)} %get-tuple-element.89.refs_1_.refs_12_.refs_2_, ...), custom_call_target="tpu_custom_call" | custom-call | flops 1000 | bytes 1000 | tf_op jit(solution)/shard_map/middle/pallas_call | solution.py:770
  39.4 17.5 %all_to_all.36.refs_0_ = bf16[8,128,256]{2,1,0:T(8,128)(2,1)} all-to-all(bf16[8,128,256]{2,1,0:T(8,128)(2,1)} %get-tuple-element.95), channel_id=1, replica_groups=mesh['dp'=4,'seq'=8] {'seq'}, dimensions={0} | all-to-all | bytes 1048576 | tf_op jit(solution)/shard_map/all_to_all | solution.py:784
  56.9 6.1 %attention.1.refs_1_ = bf16[8,128,256]{2,1,0:T(8,128)(2,1)} custom-call(bf16[8,128,256]{2,1,0:T(8,128)(2,1)} %all_to_all.36.refs_0_, bf16[8,160,128]{2,1,0:T(8,128)(2,1)} %all_to_all.35.refs_0_.refs_1_), custom_call_target="tpu_custom_call" | custom-call | flops 1000 | bytes 1000 | tf_op jit(solution)/shard_map/attention/pallas_call | solution.py:770
  62.9 17.7 %all_to_all.37.refs_0_ = bf16[8,128,256]{2,1,0:T(8,128)(2,1)} all-to-all(bf16[8,128,256]{2,1,0:T(8,128)(2,1)} %attention.1.refs_1_), channel_id=1, replica_groups=mesh['dp'=4,'seq'=8] {'seq'}, dimensions={0} | all-to-all | bytes 1048576 | tf_op jit(solution)/shard_map/all_to_all | solution.py:784
  80.6 7.0 %backward.1 = (bf16[128,512]{1,0:T(8,128)(2,1)}, f32[128,512]{1,0:T(8,128)}, f32[1,512]{1,0:T(1,128)}, bf16[128,1024]{1,0:T(8,128)(2,1)}, f32[1024,128]{1,0:T(8,...) custom-call(bf16[8,128,256]{2,1,0:T(8,128)(2,1)} %all_to_all.37.refs_0_, ...), custom_call_target="tpu_custom_call" | custom-call | flops 1000 | bytes 1000 | tf_op jit(solution)/shard_map/backward/pallas_call | solution.py:770
  87.6 2.5 %collective-permute-start.1 = (bf16[16,320,128]{2,1,0:T(8,128)(2,1)}, bf16[16,320,128]{2,1,0:T(8,128)(2,1)S(1)}, u32[]{:S(2)}, u32[]{:S(2)}) collective-permute-start(bf16[16,320,128]{2,1,0:T(8,128)(2,1)} %get-tuple-element.107), channel_id=1, source_target_pairs={{0,8},{8,0},{16,24},{24,16},{1,9},{9,1},{17,25},{25,17},{2,10},{10... | collective-permute-start | bytes 3932168 | tf_op jit(solution)/shard_map/ppermute | solution.py:795
  90.1 2.8 %collective-permute-done.1 = bf16[16,320,128]{2,1,0:T(8,128)(2,1)S(1)} collective-permute-done((bf16[16,320,128]{2,1,0:T(8,128)(2,1)}, bf16[16,320,128]{2,1,0:T(8,128)(2,1)S(1)}, u32[]{:S(2)}, u32[]{:S(2)}) %collective-permute-start.1) | collective-permute-done | bytes 1310752 | tf_op jit(solution)/shard_map/ppermute | solution.py:795
  92.9 2.1 add_convert_fusion.2
  95.0 1.2 collective-permute-start.2
  96.3 5.2 %all-to-all-start.3 = ((bf16[8,128,128]{2,1,0:T(8,128)(2,1)}), bf16[8,128,128]{2,1,0:T(8,128)(2,1)S(1)}, u32[]{:S(2)}, u32[]{:S(2)}) async-start(bf16[8,128,128]{2,1,0:T(8,128)(2,1)} %get-tuple-element.101), calls=%async_computation.3 | async-start | bytes 524288 | tf_op jit(solution)/shard_map/all_to_all | solution.py:784
  101.5 7.6 %states.1 = (f32[16512,128]{1,0:T(8,128)}, f32[128,1024]{1,0:T(8,128)}) custom-call(f32[128,128]{1,0:T(8,128)} %get-tuple-element.103.refs_0_, f32[128,128]{1,0:T(8,128)} %get-tuple-element.89.refs_1_.refs_12_.refs_2_, f32[128,32]{1,0:T(8,128)} %get-tuple-element.90.refs_2_.refs_13_.refs_3_, f32[1024,128]{1,0:T(8,128)} %get-tuple-element.91.refs_3_.refs_11_.refs_4_, ...), custom_call_target="tpu_custom_call" | custom-call | flops 1000 | bytes 1000 | tf_op jit(solution)/shard_map/states/pallas_call | solution.py:770
  109.1 2.2 collective-permute-done.2
  111.3 1.1 add_convert_fusion.1.refs_8_
  112.4 5.3 %all-to-all-start.4 = ((bf16[8,320,128]{2,1,0:T(8,128)(2,1)}), bf16[8,320,128]{2,1,0:T(8,128)(2,1)S(1)}, u32[]{:S(2)}, u32[]{:S(2)}) async-start(bf16[8,320,128]{2,1,0:T(8,128)(2,1)} %add_convert_fusion.1.refs_8_), calls=%async_computation.4 | async-start | bytes 1310720 | tf_op jit(solution)/shard_map/all_to_all | solution.py:784
  117.8 11.4 %adjoint.1 = (f32[1024,128]{1,0:T(8,128)}, f32[1024,128]{1,0:T(8,128)}, f32[128,64]{1,0:T(8,128)}, f32[128,128]{1,0:T(8,128)}) custom-call(bf16[8,128,128]{2,1,0:T(8,128)(2,1)} %copy-done.3, bf16[8,160,128]{2,1,0:T(8,128)(2,1)} %all_to_all.35.refs_0_.refs_1_, f32[128,128]{1,0:T(8,128)} %get-tuple-element.89.refs_1_.refs_12_.refs_2_, ...), custom_call_target="tpu_custom_call" | custom-call | flops 1000 | bytes 1000 | tf_op jit(solution)/shard_map/adjoint/pallas_call | solution.py:770
  129.2 6.0 %inner.1 = (bf16[16,160,128]{2,1,0:T(8,128)(2,1)}, bf16[16,160,128]{2,1,0:T(8,128)(2,1)}, bf16[144,1024]{1,0:T(8,128)(2,1)}) custom-call(f32[1024,128]{1,0:T(8,128)} %get-tuple-element.110.refs_0_, f32[1024,128]{1,0:T(8,128)} %get-tuple-element.111.refs_1_, f32[1024,128]{1,0:T(8,128)} %get-tuple-element.102.refs_6_.refs_2_, ...), custom_call_target="tpu_custom_call" | custom-call | flops 1000 | bytes 1000 | tf_op jit(solution)/shard_map/inner/pallas_call | solution.py:770
  135.2 1.6 collective-permute-start.3
  136.8 0.7 all-gather.4.cloned.1.call-done.refs_0_
  137.4 2.9 %head_products.1 = (bf16[192,128]{1,0:T(8,128)(2,1)}, bf16[192,128]{1,0:T(8,128)(2,1)}, bf16[192,128]{1,0:T(8,128)(2,1)}, bf16[192,128]{1,0:T(8,128)(2,1)}) custom-call(bf16[1024,512]{1,0:T(8,128)(2,1)} %all-gather.4.cloned.1.call-done.refs_0_, bf16[8,128,256]{2,1,0:T(8,128)(2,1)} %attention.1.refs_1_, bf16[144,1024]{1,0:T(8,128)(2,1)} %get-tuple-element.121.refs_2_.refs_0_), custom_call_target="tpu_custom_call" | custom-call | flops 1000 | bytes 1000 | tf_op jit(solution)/shard_map/head_products/pallas_call | solution.py:770
  140.3 1.6 collective-permute-start.4
  142.0 1.2 collective-permute-start.5
  143.2 0.5 collective-permute-start.6
  143.7 1.0 add_convert_fusion
  144.7 0.4 collective-permute-done.5.refs_3_
  145.1 2.0 collective-permute-done.6.refs_4_
  147.1 1.3 early_sum.1
  148.4 0.0 all-gather.6.cloned.1.call-update
  148.4 6.5 %all-to-all-start.5 = ((bf16[16,160,128]{2,1,0:T(8,128)(2,1)}), bf16[16,160,128]{2,1,0:T(8,128)(2,1)S(1)}, u32[]{:S(2)}, u32[]{:S(2)}) async-start(bf16[16,160,128]{2,1,0:T(8,128)(2,1)} %add_convert_fusion), calls=%async_computation.5 | async-start | bytes 1310720 | tf_op jit(solution)/shard_map/all_to_all | solution.py:791
  154.9 3.5 %tokens.1 = (f32[128,512]{1,0:T(8,128)}, f32[8,512]{1,0:T(8,128)}, bf16[16,128]{1,0:T(8,128)(2,1)}) custom-call(bf16[144,1024]{1,0:T(8,128)(2,1)} %get-tuple-element.121.refs_2_.refs_0_, bf16[512,2048]{1,0:T(8,128)(2,1)} %refs_1_.1, bf16[128,1024]{1,0:T(8,128)(2,1)} %get-tuple-element.127.refs_2_, bf16[128,512]{1,0:T(8,128)(2,1)} %refs_3_.5, ...), custom_call_target="tpu_custom_call" | custom-call | flops 1000 | bytes 1000 | tf_op jit(solution)/shard_map/tokens/pallas_call | solution.py:770
  158.4 15.1 %all-to-all-done.5.refs_0_ = bf16[16,160,128]{2,1,0:T(8,128)(2,1)S(1)} async-done(((bf16[16,160,128]{2,1,0:T(8,128)(2,1)}), bf16[16,160,128]{2,1,0:T(8,128)(2,1)S(1)}, u32[]{:S(2)}, u32[]{:S(2)}) %all-to-all-start.5) | async-done | bytes 655392 | tf_op jit(solution)/shard_map/all_to_all | solution.py:791
  173.5 0.7 copy-done.1
  174.2 1.2 late_sum.1
  175.4 5.4 %all-to-all-start.6 = ((bf16[16,176,128]{2,1,0:T(8,128)(2,1)}), bf16[16,176,128]{2,1,0:T(8,128)(2,1)S(1)}, u32[]{:S(2)}, u32[]{:S(2)}) async-start(bf16[16,176,128]{2,1,0:T(8,128)(2,1)} %late_sum.1), calls=%async_computation.6 | async-start | bytes 1441792 | tf_op jit(solution)/shard_map/all_to_all | solution.py:791
  180.8 2.2 collective-permute-start.7
  183.0 21.9 %collective-permute-done.7 = f32[8,512]{1,0:T(8,128)S(1)} collective-permute-done((f32[8,512]{1,0:T(8,128)S(1)}, f32[8,512]{1,0:T(8,128)S(1)}, u32[]{:S(2)}, u32[]{:S(2)}) %collective-permute-start.7) | collective-permute-done | bytes 16416 | tf_op jit(solution)/shard_map/ppermute | solution.py:902
  204.8 1.3 add_dynamic-update-slice_fusion
  206.2 2.1 collective-permute-start.8
  208.3 1.8 collective-permute-done.8.refs_1_
  210.1 2.9 %late_assembly.1 = (f32[512,2048]{1,0:T(8,128)}, f32[1,512]{1,0:T(1,128)}, f32[4,1024]{1,0:T(4,128)}, f32[1,1024]{1,0:T(1,128)}, f32[64,1024]{1,0:T(8,128)}, /*i...) custom-call(bf16[16,176,128]{2,1,0:T(8,128)(2,1)S(1)} %all-to-all-done.6., ...), custom_call_target="tpu_custom_call" | custom-call | flops 1000 | bytes 1000 | tf_op jit(solution)/shard_map/late_assembly/pallas_call | solution.py:770
  213.0 4.2 %all-gather.6.cloned.1.call-done = bf16[16384,128]{1,0:T(8,128)(2,1)} async-done(((bf16[512,128]{1,0:T(8,128)(2,1)}), bf16[16384,128]{1,0:T(8,128)(2,1)}) %all-gather.6.cloned.1.call-update) | async-done | bytes 4194320 | tf_op jit(solution)/shard_map/all_gather | solution.py:921
  217.2 4.9 %early_assembly.1 = (f32[1024,512]{1,0:T(8,128)}, f32[512,512]{1,0:T(8,128)}, f32[512,1536]{1,0:T(8,128)}, f32[512,2048]{1,0:T(8,128)}) custom-call(bf16[32,512,128]{2,1,0:T(8,128)(2,1)} %bitcast.16, f32[512,2048]{1,0:T(8,128)} %get-tuple-element.136.refs_1_), custom_call_target="tpu_custom_call", output_to_operand_aliasing={{3}: (1, {})} | custom-call | flops 1000 | bytes 1000 | tf_op jit(solution)/shard_map/early_assembly/pallas_call | solution.py:770
  (19 shorter events, 0.1 us)
Async XLA Ops:
  7.2 130.3 %all-gather.4.cloned.1.call-start = ((), (), s32[]{:S(2)}) async-start(), calls=%async_computation.7 | async-start | bytes 1179648 | tf_op jit(solution)/shard_map/all_gather | solution.py:871
  7.9 4.5 %collective-permute-start = (bf16[16,512]{1,0:T(8,128)(2,1)S(1)}, bf16[16,512]{1,0:T(8,128)(2,1)S(1)}, u32[]{:S(2)}, u32[]{:S(2)}) collective-permute-start(bf16[16,512]{1,0:T(8,128)(2,1)S(1)} %slice.34), channel_id=1, source_target_pairs={{0,1},{1,2},{2,3},{3,4},{4,5},{5,6},{6,7},{8,9},{9,10},{10,11},{11... | collective-permute-start | bytes 49160 | tf_op jit(solution)/shard_map/ppermute | solution.py:819
  12.4 0.6 copy-start.5
  87.6 5.3 %collective-permute-start.1 = (bf16[16,320,128]{2,1,0:T(8,128)(2,1)}, bf16[16,320,128]{2,1,0:T(8,128)(2,1)S(1)}, u32[]{:S(2)}, u32[]{:S(2)}) collective-permute-start(bf16[16,320,128]{2,1,0:T(8,128)(2,1)} %get-tuple-element.107), channel_id=1, source_target_pairs={{0,8},{8,0},{16,24},{24,16},{1,9},{9,1},{17,25},{25,17},{2,10},{10... | collective-permute-start | bytes 3932168 | tf_op jit(solution)/shard_map/ppermute | solution.py:795
  95.0 16.3 %copy-start.2 = (bf16[16,320,128]{2,1,0:T(8,128)(2,1)S(1)}, bf16[16,320,128]{2,1,0:T(8,128)(2,1)}, u32[]{:S(2)}) copy-start(bf16[16,320,128]{2,1,0:T(8,128)(2,1)} %get-tuple-element.106) | copy-start | bytes 3932164
  95.0 16.3 %collective-permute-start.2 = (bf16[8,320,128]{2,1,0:T(8,128)(2,1)}, bf16[8,320,128]{2,1,0:T(8,128)(2,1)S(1)}, u32[]{:S(2)}, u32[]{:S(2)}) collective-permute-start(bf16[8,320,128]{2,1,0:T(8,128)(2,1)} %add_convert_fusion.2), channel_id=1, source_target_pairs={{0,16},{8,24},{16,0},{24,8},{1,17},{9,25},{17,1},{25,9},{2,18},{10... | collective-permute-start | bytes 1966088 | tf_op jit(solution)/shard_map/ppermute | solution.py:876
  96.3 16.2 %all-to-all-start.3 = ((bf16[8,128,128]{2,1,0:T(8,128)(2,1)}), bf16[8,128,128]{2,1,0:T(8,128)(2,1)S(1)}, u32[]{:S(2)}, u32[]{:S(2)}) async-start(bf16[8,128,128]{2,1,0:T(8,128)(2,1)} %get-tuple-element.101), calls=%async_computation.3 | async-start | bytes 524288 | tf_op jit(solution)/shard_map/all_to_all | solution.py:784
  112.4 5.3 %copy-start.3 = (bf16[8,128,128]{2,1,0:T(8,128)(2,1)}, bf16[8,128,128]{2,1,0:T(8,128)(2,1)S(1)}, u32[]{:S(2)}) copy-start(bf16[8,128,128]{2,1,0:T(8,128)(2,1)S(1)} %all-to-all-done.3.refs_0_) | copy-start | bytes 786436
  112.4 34.7 %all-to-all-start.4 = ((bf16[8,320,128]{2,1,0:T(8,128)(2,1)}), bf16[8,320,128]{2,1,0:T(8,128)(2,1)S(1)}, u32[]{:S(2)}, u32[]{:S(2)}) async-start(bf16[8,320,128]{2,1,0:T(8,128)(2,1)} %add_convert_fusion.1.refs_8_), calls=%async_computation.4 | async-start | bytes 1310720 | tf_op jit(solution)/shard_map/all_to_all | solution.py:784
  117.7 99.4 %all-gather.6.cloned.1.call-start = ((), (), s32[]{:S(2)}) async-start(), calls=%async_computation.8 | async-start | bytes 4325376 | tf_op jit(solution)/shard_map/all_gather | solution.py:921
  135.2 8.5 %copy-start.4 = (bf16[16,160,128]{2,1,0:T(8,128)(2,1)S(1)}, bf16[16,160,128]{2,1,0:T(8,128)(2,1)}, u32[]{:S(2)}) copy-start(bf16[16,160,128]{2,1,0:T(8,128)(2,1)} %get-tuple-element.118) | copy-start | bytes 1966084
  135.2 8.5 %collective-permute-start.3 = (bf16[16,160,128]{2,1,0:T(8,128)(2,1)}, bf16[16,160,128]{2,1,0:T(8,128)(2,1)S(1)}, u32[]{:S(2)}, u32[]{:S(2)}) collective-permute-start(bf16[16,160,128]{2,1,0:T(8,128)(2,1)} %get-tuple-element.119), channel_id=1, source_target_pairs={{0,8},{8,0},{16,24},{24,16},{1,9},{9,1},{17,25},{25,17},{2,10},{10... | collective-permute-start | bytes 1966088 | tf_op jit(solution)/shard_map/ppermute | solution.py:795
  140.3 6.8 %copy-start = (bf16[192,128]{1,0:T(8,128)(2,1)S(1)}, bf16[192,128]{1,0:T(8,128)(2,1)}, u32[]{:S(2)}) copy-start(bf16[192,128]{1,0:T(8,128)(2,1)} %get-tuple-element.122.refs_1_) | copy-start | bytes 147460
  140.3 4.4 %collective-permute-start.4 = (bf16[192,128]{1,0:T(8,128)(2,1)}, bf16[192,128]{1,0:T(8,128)(2,1)S(1)}, u32[]{:S(2)}, u32[]{:S(2)}) collective-permute-start(bf16[192,128]{1,0:T(8,128)(2,1)} %get-tuple-element.123), channel_id=1, source_target_pairs={{0,8},{8,0},{16,24},{24,16},{1,9},{9,1},{17,25},{25,17},{2,10},{10... | collective-permute-start | bytes 147464 | tf_op jit(solution)/shard_map/ppermute | solution.py:911
  142.0 3.2 %collective-permute-start.5 = (bf16[192,128]{1,0:T(8,128)(2,1)}, bf16[192,128]{1,0:T(8,128)(2,1)S(1)}, u32[]{:S(2)}, u32[]{:S(2)}) collective-permute-start(bf16[192,128]{1,0:T(8,128)(2,1)} %get-tuple-element.124), channel_id=1, source_target_pairs={{0,16},{8,24},{16,0},{24,8},{1,17},{9,25},{17,1},{25,9},{2,18},{10... | collective-permute-start | bytes 147464 | tf_op jit(solution)/shard_map/ppermute | solution.py:911
  143.2 3.9 %collective-permute-start.6 = (bf16[192,128]{1,0:T(8,128)(2,1)}, bf16[192,128]{1,0:T(8,128)(2,1)S(1)}, u32[]{:S(2)}, u32[]{:S(2)}) collective-permute-start(bf16[192,128]{1,0:T(8,128)(2,1)} %get-tuple-element.125), channel_id=1, source_target_pairs={{0,24},{8,16},{16,8},{24,0},{1,25},{9,17},{17,9},{25,1},{2,26},{10... | collective-permute-start | bytes 147464 | tf_op jit(solution)/shard_map/ppermute | solution.py:911
  148.4 25.1 %all-to-all-start.5 = ((bf16[16,160,128]{2,1,0:T(8,128)(2,1)}), bf16[16,160,128]{2,1,0:T(8,128)(2,1)S(1)}, u32[]{:S(2)}, u32[]{:S(2)}) async-start(bf16[16,160,128]{2,1,0:T(8,128)(2,1)} %add_convert_fusion), calls=%async_computation.5 | async-start | bytes 1310720 | tf_op jit(solution)/shard_map/all_to_all | solution.py:791
  173.5 0.7 copy-start.1
  174.2 6.6 %copy-start.6 = (f32[8,512]{1,0:T(8,128)S(1)}, f32[8,512]{1,0:T(8,128)}, u32[]{:S(2)}) copy-start(f32[8,512]{1,0:T(8,128)} %get-tuple-element.131) | copy-start | bytes 49156
  175.4 30.8 %all-to-all-start.6 = ((bf16[16,176,128]{2,1,0:T(8,128)(2,1)}), bf16[16,176,128]{2,1,0:T(8,128)(2,1)S(1)}, u32[]{:S(2)}, u32[]{:S(2)}) async-start(bf16[16,176,128]{2,1,0:T(8,128)(2,1)} %late_sum.1), calls=%async_computation.6 | async-start | bytes 1441792 | tf_op jit(solution)/shard_map/all_to_all | solution.py:791
  180.8 24.1 %collective-permute-start.7 = (f32[8,512]{1,0:T(8,128)S(1)}, f32[8,512]{1,0:T(8,128)S(1)}, u32[]{:S(2)}, u32[]{:S(2)}) collective-permute-start(f32[8,512]{1,0:T(8,128)S(1)} %copy-done.6), channel_id=1, source_target_pairs={{1,0},{2,1},{3,2},{4,3},{5,4},{6,5},{7,6},{9,8},{10,9},{11,10},{12... | collective-permute-start | bytes 49160 | tf_op jit(solution)/shard_map/ppermute | solution.py:902
  206.2 3.9 %collective-permute-start.8 = (bf16[16,176,128]{2,1,0:T(8,128)(2,1)S(1)}, bf16[16,176,128]{2,1,0:T(8,128)(2,1)S(1)}, u32[]{:S(2)}, u32[]{:S(2)}) collective-permute-start(bf16[16,176,128]{2,1,0:T(8,128)(2,1)S(1)} %all-to-all-done.6.refs_0_), channel_id=1, source_target_pairs={{0,8},{8,0},{16,24},{24,16},{1,9},{9,1},{17,25},{25,17},{2,10},{10... | collective-permute-start | bytes 2162696 | tf_op jit(solution)/shard_map/ppermute | solution.py:795
Sparse Core Ops, SparseCore 0:
  90.2 47.1 all-gather.3
  148.5 68.5 all-gather.5

commit v6 on v5

--- a/solution.py
+++ b/solution.py
@@ -281,8 +281,8 @@
 
 
 def backward_kernel(
-    tiled, back, after, w_proj, w_qkv, n2, cot, w_out, gate, ssm, gated, normed, s_ref, a_ref, bc,
-    o_out, o_after, o_n2, o_gate, o_g, o_msg, *o_more
+    tiled, back, after, w_proj, w_qkv, n2, cot, w_out, gate, ssm, gated, normed,
+    o_out, o_after, o_n2, o_gate, o_g, *o_more
 ):
     back = ready(back)
     seq_size, count = back.shape[0], back.shape[1]
@@ -317,8 +317,6 @@
     w_out, gate, ssm = ready(w_out, gate, ssm)
     inner_width = gate.shape[1]
     tiles = inner_width // LANES
-    a_ref = ready(a_ref)
-    states = a_ref.shape[0] // 8
     grad_gated = dot_nt(branch, w_out[...])
     for j in range(tiles):
         v = gate[:, tile(j)].astype(F32)
@@ -332,11 +330,16 @@
     if tiled:
         partials(seq_size, gated, branch, normed, o_gate, attended, cot, *o_more)
         sent(*o_more[:2])
-    s_ref, smem = ready(s_ref, bc)
+
+
+def leaving_kernel(g_ref, a_ref, bc, s_ref, o_msg):
+    g_ref, a_ref, smem, s_ref = ready(g_ref, a_ref, bc, s_ref)
+    count, states = smem.shape[0], a_ref.shape[0] // 8
+    seq_size = o_msg.shape[0]
 
     def one(i, later):
         t = count - 1 - i
-        s, g = block(s_ref, t), block(o_g, t)
+        s, g = block(s_ref, t), block(g_ref, t)
         return tuple(
             jnp.exp2(s * block(a_ref, n)) * (g * smem[t, states + n] + later[n])
             for n in range(states)
@@ -855,15 +858,17 @@
     back_own = exchange(back, "seq")
     pieces = [((peers, 2 * LANES + HD, LANES), BF)] * 2
     rest = [((count, width), BF), ((count, 3 * width), BF), ((count, width), BF)]
-    out, grad_after, grad_n2, grad_gate, g, adj, *more = call(
+    out, grad_after, grad_n2, grad_gate, g, *more = call(
         functools.partial(backward_kernel, tiled),
         [
             ((count, width), BF), ((count, width), F32), ((1, width), F32), ((count, inner_width), BF), blocks,
-            ((seq_size, states * 8, LANES), BF),
         ] + (pieces if tiled else rest),
         [vmem((inner_width, width), F32), vmem((width, inner_width), F32), vmem((width, width), F32)] if tiled else [],
-        back_own, after, w_proj, w_qkv, n2, cotangent, w_out, gate, ssm, gated, normed, s, a, bc,
-        name="backward", us=0, scalars=(13,), views={10: np.s_[HALO:, :]}, near=(0,),
+        back_own, after, w_proj, w_qkv, n2, cotangent, w_out, gate, ssm, gated, normed,
+        name="backward", us=0, views={10: np.s_[HALO:, :]}, near=(0,),
+    )
+    (adj,) = call(
+        leaving_kernel, [((seq_size, states * 8, LANES), BF)], [], g, a, bc, s, name="leaving", us=0, scalars=(2,)
     )
     adj = exchange(adj, "seq")
     between = ()

time: 232 us -> 232 us (level)
  Pallas kernels: 68.5 us -> 71.7 us
  waiting for transfers between devices: 52.5 us -> 49.6 us
    all_gather x1, waiting for transfers between devices: 4.18 us -> 7.61 us  [body(): early = lax.all_gather(early, ('dp', 'seq'))]
    pallas_call x13 -> x14, Pallas kernels: 68.5 us -> 71.7 us  [call(): pl.pallas_call(run, out_shape=[jax.ShapeDtypeStruct(s, d) for s, d in out...]
    ppermute x1, waiting for transfers between devices: 21.9 us -> 19.3 us  [body(): lax.ppermute(grad_halo, 'seq', [(i + 1, i) for i in range(seq_size - 1)])]
  transfers between devices with their start and end apart: 15 -> 15, of which waited for: 10 -> 8; matrix products, arithmetic and copies ran while one was open for 2% -> 2% of each run, Pallas kernels for 15% -> 17%
where the time goes in v6:
time: 232 us; the launch traced here: 229 us
  Pallas kernels  71.7 us (31%)
  waiting for transfers between devices  49.6 us (21%)
  blocking collectives  47.7 us (21%)
  starting transfers between devices  38.6 us (17%)
  between operations  14.2 us (6%)
  other arithmetic  5.52 us (2%)
    pallas_call x14, Pallas kernels, call(): pl.pallas_call(run, out_shape=[jax.ShapeDtypeStruct(s, d) for s, d in out...  71.7 us
    all_to_all x3, blocking collectives, exchange(): return lax.all_to_all(value, axes, 0, 0, tiled=True)  47.7 us
    ppermute x1, waiting for transfers between devices, body(): lax.ppermute(grad_halo, 'seq', [(i + 1, i) for i in range(seq_size - 1)])  19.3 us
    all_to_all x2, waiting for transfers between devices, own_core(): lax.all_to_all(value, ('dp', 'seq'), 0, 0, tiled=True, axis_index_groups=...  14.6 us
    all_to_all x2, starting transfers between devices, own_core(): lax.all_to_all(value, ('dp', 'seq'), 0, 0, tiled=True, axis_index_groups=...  11.7 us
    all_to_all x2, starting transfers between devices, exchange(): return lax.all_to_all(value, axes, 0, 0, tiled=True)  10.8 us
    all_gather x1, waiting for transfers between devices, body(): early = lax.all_gather(early, ('dp', 'seq'))  7.61 us
    ppermute x3, starting transfers between devices, other_core(): return lax.ppermute(value, 'dp', [(g, g ^ 1) for g in range(groups)])  7.28 us
  transfers between devices with their start and end apart: 15, of which 8 were waited for; matrix products, arithmetic and copies ran while one was open for 2% of the time, Pallas kernels for 17%

profile of v6, /device:TPU:13, one launch (start us, length us, event | category | flops | bytes accessed | tf_op | source)
XLA Modules:
  0.0 229.4 jit_solution(6866589055716184288)
XLA Ops:
  7.2 0.0 all-gather.4.cloned.1.call-start
  7.2 0.7 slice.34
  7.9 3.1 %collective-permute-start = (bf16[16,512]{1,0:T(8,128)(2,1)S(1)}, bf16[16,512]{1,0:T(8,128)(2,1)S(1)}, u32[]{:S(2)}, u32[]{:S(2)}) collective-permute-start(bf16[16,512]{1,0:T(8,128)(2,1)S(1)} %slice.34), channel_id=1, source_target_pairs={{0,1},{1,2},{2,3},{3,4},{4,5},{5,6},{6,7},{8,9},{9,10},{10,11},{11... | collective-permute-start | bytes 49160 | tf_op jit(solution)/shard_map/ppermute | solution.py:822
  11.1 1.3 collective-permute-done.refs_1_.refs_4_
  12.4 0.6 copy-done.5
  13.0 7.3 %forward.1 = (bf16[8,160,128]{2,1,0:T(8,128)(2,1)}, bf16[144,512]{1,0:T(8,128)(2,1)}, bf16[144,1024]{1,0:T(8,128)(2,1)}, bf16[128,1024]{1,0:T(8,128)(2,1)}, bf16...) custom-call(bf16[128,512]{1,0:T(8,128)(2,1)} %refs_3_.5, ...), custom_call_target="tpu_custom_call" | custom-call | flops 1000 | bytes 1000 | tf_op jit(solution)/shard_map/forward/pallas_call | solution.py:773
  20.3 12.5 %all_to_all.35.refs_0_.refs_1_ = bf16[8,160,128]{2,1,0:T(8,128)(2,1)} all-to-all(bf16[8,160,128]{2,1,0:T(8,128)(2,1)} %get-tuple-element.87), channel_id=1, replica_groups=mesh['dp'=4,'seq'=8] {'seq'}, dimensions={0} | all-to-all | bytes 655360 | tf_op jit(solution)/shard_map/all_to_all | solution.py:787
  32.8 6.6 %middle.1 = (bf16[8,128,256]{2,1,0:T(8,128)(2,1)}, f32[128,128]{1,0:T(8,128)}, f32[128,1024]{1,0:T(8,128)}, f32[128,512]{1,0:T(8,128)}, bf16[128,1024]{1,0:T(8,128)(2,1)}, /*index=5*/bf16[128,512]{1,0:T(8,128)(2,1)}) custom-call(bf16[8,160,128]{2,1,0:T(8,128)(2,1)} %all_to_all.35.refs_0_.refs_1_, f32[128,128]{1,0:T(8,128)} %get-tuple-element.88.refs_1_.refs_2_, ...), custom_call_target="tpu_custom_call" | custom-call | flops 1000 | bytes 1000 | tf_op jit(solution)/shard_map/middle/pallas_call | solution.py:773
  39.4 17.5 %all_to_all.36.refs_0_ = bf16[8,128,256]{2,1,0:T(8,128)(2,1)} all-to-all(bf16[8,128,256]{2,1,0:T(8,128)(2,1)} %get-tuple-element.94), channel_id=1, replica_groups=mesh['dp'=4,'seq'=8] {'seq'}, dimensions={0} | all-to-all | bytes 1048576 | tf_op jit(solution)/shard_map/all_to_all | solution.py:787
  56.9 6.1 %attention.1.refs_1_ = bf16[8,128,256]{2,1,0:T(8,128)(2,1)} custom-call(bf16[8,128,256]{2,1,0:T(8,128)(2,1)} %all_to_all.36.refs_0_, bf16[8,160,128]{2,1,0:T(8,128)(2,1)} %all_to_all.35.refs_0_.refs_1_), custom_call_target="tpu_custom_call" | custom-call | flops 1000 | bytes 1000 | tf_op jit(solution)/shard_map/attention/pallas_call | solution.py:773
  62.9 17.7 %all_to_all.37.refs_0_ = bf16[8,128,256]{2,1,0:T(8,128)(2,1)} all-to-all(bf16[8,128,256]{2,1,0:T(8,128)(2,1)} %attention.1.refs_1_), channel_id=1, replica_groups=mesh['dp'=4,'seq'=8] {'seq'}, dimensions={0} | all-to-all | bytes 1048576 | tf_op jit(solution)/shard_map/all_to_all | solution.py:787
  80.6 5.7 %backward.1 = (bf16[128,512]{1,0:T(8,128)(2,1)}, f32[128,512]{1,0:T(8,128)}, f32[1,512]{1,0:T(1,128)}, bf16[128,1024]{1,0:T(8,128)(2,1)}, f32[1024,128]{1,0:T(8,...) custom-call(bf16[8,128,256]{2,1,0:T(8,128)(2,1)} %all_to_all.37.refs_0_, ...), custom_call_target="tpu_custom_call" | custom-call | flops 1000 | bytes 1000 | tf_op jit(solution)/shard_map/backward/pallas_call | solution.py:773
  86.4 2.5 %collective-permute-start.1 = (bf16[16,320,128]{2,1,0:T(8,128)(2,1)}, bf16[16,320,128]{2,1,0:T(8,128)(2,1)S(1)}, u32[]{:S(2)}, u32[]{:S(2)}) collective-permute-start(bf16[16,320,128]{2,1,0:T(8,128)(2,1)} %get-tuple-element.105), channel_id=1, source_target_pairs={{0,8},{8,0},{16,24},{24,16},{1,9},{9,1},{17,25},{25,17},{2,10},{10... | collective-permute-start | bytes 3932168 | tf_op jit(solution)/shard_map/ppermute | solution.py:798
  88.8 0.0 all-gather.4.cloned.1.call-update
  88.8 2.8 %collective-permute-done.1 = bf16[16,320,128]{2,1,0:T(8,128)(2,1)S(1)} collective-permute-done((bf16[16,320,128]{2,1,0:T(8,128)(2,1)}, bf16[16,320,128]{2,1,0:T(8,128)(2,1)S(1)}, u32[]{:S(2)}, u32[]{:S(2)}) %collective-permute-start.1) | collective-permute-done | bytes 1310752 | tf_op jit(solution)/shard_map/ppermute | solution.py:798
  91.7 2.1 add_convert_fusion.2
  93.8 1.2 collective-permute-start.2
  95.0 4.5 %leaving.1 = bf16[8,128,128]{2,1,0:T(8,128)(2,1)} custom-call(f32[1024,128]{1,0:T(8,128)} %get-tuple-element.100.refs_0_.refs_6_.refs_2_, f32[128,128]{1,0:T(8,128)} %get-tuple-element.88.refs_1_.refs_2_, f32[128,32]{1,0:T(8,128)} %get-tuple-element.89.refs_2_.refs_3_, f32[1024,128]{1,0:T(8,128)} %get-tuple-element.90.refs_3_.refs_4_), custom_call_target="tpu_custom_call" | custom-call | flops 1000 | bytes 1000 | tf_op jit(solution)/shard_map/leaving/pallas_call | solution.py:773
  99.5 5.4 %all-to-all-start.3 = ((bf16[8,128,128]{2,1,0:T(8,128)(2,1)}), bf16[8,128,128]{2,1,0:T(8,128)(2,1)S(1)}, u32[]{:S(2)}, u32[]{:S(2)}) async-start(bf16[8,128,128]{2,1,0:T(8,128)(2,1)} %leaving.1), calls=%async_computation.3 | async-start | bytes 524288 | tf_op jit(solution)/shard_map/all_to_all | solution.py:787
  104.9 7.6 %states.1 = (f32[16512,128]{1,0:T(8,128)}, f32[128,1024]{1,0:T(8,128)}) custom-call(f32[128,128]{1,0:T(8,128)} %get-tuple-element.101.refs_0_, f32[128,128]{1,0:T(8,128)} %get-tuple-element.88.refs_1_.refs_2_, f32[128,32]{1,0:T(8,128)} %get-tuple-element.89.refs_2_.refs_3_, f32[1024,128]{1,0:T(8,128)} %get-tuple-element.90.refs_3_.refs_4_, ...), custom_call_target="tpu_custom_call" | custom-call | flops 1000 | bytes 1000 | tf_op jit(solution)/shard_map/states/pallas_call | solution.py:773
  112.5 1.1 add_convert_fusion.1.refs_8_
  113.6 5.4 %all-to-all-start.4 = ((bf16[8,320,128]{2,1,0:T(8,128)(2,1)}), bf16[8,320,128]{2,1,0:T(8,128)(2,1)S(1)}, u32[]{:S(2)}, u32[]{:S(2)}) async-start(bf16[8,320,128]{2,1,0:T(8,128)(2,1)} %add_convert_fusion.1.refs_8_), calls=%async_computation.4 | async-start | bytes 1310720 | tf_op jit(solution)/shard_map/all_to_all | solution.py:787
  119.1 11.4 %adjoint.1 = (f32[1024,128]{1,0:T(8,128)}, f32[1024,128]{1,0:T(8,128)}, f32[128,64]{1,0:T(8,128)}, f32[128,128]{1,0:T(8,128)}) custom-call(bf16[8,128,128]{2,1,0:T(8,128)(2,1)} %copy-done.3, bf16[8,160,128]{2,1,0:T(8,128)(2,1)} %all_to_all.35.refs_0_.refs_1_, f32[128,128]{1,0:T(8,128)} %get-tuple-element.88.refs_1_.refs_2_, ...), custom_call_target="tpu_custom_call" | custom-call | flops 1000 | bytes 1000 | tf_op jit(solution)/shard_map/adjoint/pallas_call | solution.py:773
  130.5 5.9 %inner.1 = (bf16[16,160,128]{2,1,0:T(8,128)(2,1)}, bf16[16,160,128]{2,1,0:T(8,128)(2,1)}, bf16[144,1024]{1,0:T(8,128)(2,1)}) custom-call(f32[1024,128]{1,0:T(8,128)} %get-tuple-element.108.refs_0_, f32[1024,128]{1,0:T(8,128)} %get-tuple-element.109.refs_1_, f32[1024,128]{1,0:T(8,128)} %get-tuple-element.100.refs_0_.refs_6_.refs_2_, ...), custom_call_target="tpu_custom_call" | custom-call | flops 1000 | bytes 1000 | tf_op jit(solution)/shard_map/inner/pallas_call | solution.py:773
  136.5 1.8 collective-permute-start.3
  138.3 2.9 %head_products.1 = (bf16[192,128]{1,0:T(8,128)(2,1)}, bf16[192,128]{1,0:T(8,128)(2,1)}, bf16[192,128]{1,0:T(8,128)(2,1)}, bf16[192,128]{1,0:T(8,128)(2,1)}) custom-call(bf16[1024,512]{1,0:T(8,128)(2,1)} %all-gather.4.cloned.1.call-done.refs_0_, bf16[8,128,256]{2,1,0:T(8,128)(2,1)} %attention.1.refs_1_, bf16[144,1024]{1,0:T(8,128)(2,1)} %get-tuple-element.119.refs_2_.refs_0_), custom_call_target="tpu_custom_call" | custom-call | flops 1000 | bytes 1000 | tf_op jit(solution)/shard_map/head_products/pallas_call | solution.py:773
  141.2 0.2 collective-permute-start.4
  141.3 0.7 collective-permute-start.5
  142.1 1.3 collective-permute-start.6
  143.4 1.0 add_convert_fusion
  144.4 0.1 collective-permute-done.5.refs_3_
  144.5 1.9 collective-permute-done.6.refs_4_
  146.4 1.3 early_sum.1
  147.7 0.0 all-gather.6.cloned.1.call-update
  147.7 6.1 %all-to-all-start.5 = ((bf16[16,160,128]{2,1,0:T(8,128)(2,1)}), bf16[16,160,128]{2,1,0:T(8,128)(2,1)S(1)}, u32[]{:S(2)}, u32[]{:S(2)}) async-start(bf16[16,160,128]{2,1,0:T(8,128)(2,1)} %add_convert_fusion), calls=%async_computation.5 | async-start | bytes 1310720 | tf_op jit(solution)/shard_map/all_to_all | solution.py:794
  153.8 3.5 %tokens.1 = (f32[128,512]{1,0:T(8,128)}, f32[8,512]{1,0:T(8,128)}, bf16[16,128]{1,0:T(8,128)(2,1)}) custom-call(bf16[144,1024]{1,0:T(8,128)(2,1)} %get-tuple-element.119.refs_2_.refs_0_, bf16[512,2048]{1,0:T(8,128)(2,1)} %refs_1_.1, bf16[128,1024]{1,0:T(8,128)(2,1)} %get-tuple-element.125.refs_2_, bf16[128,512]{1,0:T(8,128)(2,1)} %refs_3_.5, ...), custom_call_target="tpu_custom_call" | custom-call | flops 1000 | bytes 1000 | tf_op jit(solution)/shard_map/tokens/pallas_call | solution.py:773
  157.3 14.6 %all-to-all-done.5.refs_0_ = bf16[16,160,128]{2,1,0:T(8,128)(2,1)S(1)} async-done(((bf16[16,160,128]{2,1,0:T(8,128)(2,1)}), bf16[16,160,128]{2,1,0:T(8,128)(2,1)S(1)}, u32[]{:S(2)}, u32[]{:S(2)}) %all-to-all-start.5) | async-done | bytes 655392 | tf_op jit(solution)/shard_map/all_to_all | solution.py:794
  172.0 0.7 copy-done.1
  172.7 1.2 late_sum.1
  173.9 5.6 %all-to-all-start.6 = ((bf16[16,176,128]{2,1,0:T(8,128)(2,1)}), bf16[16,176,128]{2,1,0:T(8,128)(2,1)S(1)}, u32[]{:S(2)}, u32[]{:S(2)}) async-start(bf16[16,176,128]{2,1,0:T(8,128)(2,1)} %late_sum.1), calls=%async_computation.6 | async-start | bytes 1441792 | tf_op jit(solution)/shard_map/all_to_all | solution.py:794
  179.5 2.2 collective-permute-start.7
  181.7 19.3 %collective-permute-done.7 = f32[8,512]{1,0:T(8,128)S(1)} collective-permute-done((f32[8,512]{1,0:T(8,128)S(1)}, f32[8,512]{1,0:T(8,128)S(1)}, u32[]{:S(2)}, u32[]{:S(2)}) %collective-permute-start.7) | collective-permute-done | bytes 16416 | tf_op jit(solution)/shard_map/ppermute | solution.py:907
  201.0 1.3 add_dynamic-update-slice_fusion
  202.4 3.0 %collective-permute-start.8 = (bf16[16,176,128]{2,1,0:T(8,128)(2,1)S(1)}, bf16[16,176,128]{2,1,0:T(8,128)(2,1)S(1)}, u32[]{:S(2)}, u32[]{:S(2)}) collective-permute-start(bf16[16,176,128]{2,1,0:T(8,128)(2,1)S(1)} %all-to-all-done.6.refs_0_), channel_id=1, source_target_pairs={{0,8},{8,0},{16,24},{24,16},{1,9},{9,1},{17,25},{25,17},{2,10},{10... | collective-permute-start | bytes 2162696 | tf_op jit(solution)/shard_map/ppermute | solution.py:798
  205.4 1.8 collective-permute-done.8.refs_1_
  207.2 2.9 %late_assembly.1 = (f32[512,2048]{1,0:T(8,128)}, f32[1,512]{1,0:T(1,128)}, f32[4,1024]{1,0:T(4,128)}, f32[1,1024]{1,0:T(1,128)}, f32[64,1024]{1,0:T(8,128)}, /*i...) custom-call(bf16[16,176,128]{2,1,0:T(8,128)(2,1)S(1)} %all-to-all-done.6., ...), custom_call_target="tpu_custom_call" | custom-call | flops 1000 | bytes 1000 | tf_op jit(solution)/shard_map/late_assembly/pallas_call | solution.py:773
  210.1 7.6 %all-gather.6.cloned.1.call-done = bf16[16384,128]{1,0:T(8,128)(2,1)} async-done(((bf16[512,128]{1,0:T(8,128)(2,1)}), bf16[16384,128]{1,0:T(8,128)(2,1)}) %all-gather.6.cloned.1.call-update) | async-done | bytes 4194320 | tf_op jit(solution)/shard_map/all_gather | solution.py:926
  217.7 4.9 %early_assembly.1 = (f32[1024,512]{1,0:T(8,128)}, f32[512,512]{1,0:T(8,128)}, f32[512,1536]{1,0:T(8,128)}, f32[512,2048]{1,0:T(8,128)}) custom-call(bf16[32,512,128]{2,1,0:T(8,128)(2,1)} %bitcast.16, f32[512,2048]{1,0:T(8,128)} %get-tuple-element.134.refs_1_), custom_call_target="tpu_custom_call", output_to_operand_aliasing={{3}: (1, {})} | custom-call | flops 1000 | bytes 1000 | tf_op jit(solution)/shard_map/early_assembly/pallas_call | solution.py:773
  (20 shorter events, 0.0 us)
Async XLA Ops:
  7.2 131.1 %all-gather.4.cloned.1.call-start = ((), (), s32[]{:S(2)}) async-start(), calls=%async_computation.7 | async-start | bytes 1179648 | tf_op jit(solution)/shard_map/all_gather | solution.py:876
  7.9 4.5 %collective-permute-start = (bf16[16,512]{1,0:T(8,128)(2,1)S(1)}, bf16[16,512]{1,0:T(8,128)(2,1)S(1)}, u32[]{:S(2)}, u32[]{:S(2)}) collective-permute-start(bf16[16,512]{1,0:T(8,128)(2,1)S(1)} %slice.34), channel_id=1, source_target_pairs={{0,1},{1,2},{2,3},{3,4},{4,5},{5,6},{6,7},{8,9},{9,10},{10,11},{11... | collective-permute-start | bytes 49160 | tf_op jit(solution)/shard_map/ppermute | solution.py:822
  12.4 0.6 copy-start.5
  86.4 5.3 %collective-permute-start.1 = (bf16[16,320,128]{2,1,0:T(8,128)(2,1)}, bf16[16,320,128]{2,1,0:T(8,128)(2,1)S(1)}, u32[]{:S(2)}, u32[]{:S(2)}) collective-permute-start(bf16[16,320,128]{2,1,0:T(8,128)(2,1)} %get-tuple-element.105), channel_id=1, source_target_pairs={{0,8},{8,0},{16,24},{24,16},{1,9},{9,1},{17,25},{25,17},{2,10},{10... | collective-permute-start | bytes 3932168 | tf_op jit(solution)/shard_map/ppermute | solution.py:798
  93.8 18.7 %collective-permute-start.2 = (bf16[8,320,128]{2,1,0:T(8,128)(2,1)}, bf16[8,320,128]{2,1,0:T(8,128)(2,1)S(1)}, u32[]{:S(2)}, u32[]{:S(2)}) collective-permute-start(bf16[8,320,128]{2,1,0:T(8,128)(2,1)} %add_convert_fusion.2), channel_id=1, source_target_pairs={{0,16},{8,24},{16,0},{24,8},{1,17},{9,25},{17,1},{25,9},{2,18},{10... | collective-permute-start | bytes 1966088 | tf_op jit(solution)/shard_map/ppermute | solution.py:881
  99.5 13.0 %copy-start.2 = (bf16[16,320,128]{2,1,0:T(8,128)(2,1)S(1)}, bf16[16,320,128]{2,1,0:T(8,128)(2,1)}, u32[]{:S(2)}) copy-start(bf16[16,320,128]{2,1,0:T(8,128)(2,1)} %get-tuple-element.104) | copy-start | bytes 3932164
  99.5 14.1 %all-to-all-start.3 = ((bf16[8,128,128]{2,1,0:T(8,128)(2,1)}), bf16[8,128,128]{2,1,0:T(8,128)(2,1)S(1)}, u32[]{:S(2)}, u32[]{:S(2)}) async-start(bf16[8,128,128]{2,1,0:T(8,128)(2,1)} %leaving.1), calls=%async_computation.3 | async-start | bytes 524288 | tf_op jit(solution)/shard_map/all_to_all | solution.py:787
  113.6 5.5 %copy-start.3 = (bf16[8,128,128]{2,1,0:T(8,128)(2,1)}, bf16[8,128,128]{2,1,0:T(8,128)(2,1)S(1)}, u32[]{:S(2)}) copy-start(bf16[8,128,128]{2,1,0:T(8,128)(2,1)S(1)} %all-to-all-done.3.refs_0_) | copy-start | bytes 786436
  113.6 32.8 %all-to-all-start.4 = ((bf16[8,320,128]{2,1,0:T(8,128)(2,1)}), bf16[8,320,128]{2,1,0:T(8,128)(2,1)S(1)}, u32[]{:S(2)}, u32[]{:S(2)}) async-start(bf16[8,320,128]{2,1,0:T(8,128)(2,1)} %add_convert_fusion.1.refs_8_), calls=%async_computation.4 | async-start | bytes 1310720 | tf_op jit(solution)/shard_map/all_to_all | solution.py:787
  119.1 98.6 %all-gather.6.cloned.1.call-start = ((), (), s32[]{:S(2)}) async-start(), calls=%async_computation.8 | async-start | bytes 4325376 | tf_op jit(solution)/shard_map/all_gather | solution.py:926
  136.5 6.9 %copy-start.4 = (bf16[16,160,128]{2,1,0:T(8,128)(2,1)S(1)}, bf16[16,160,128]{2,1,0:T(8,128)(2,1)}, u32[]{:S(2)}) copy-start(bf16[16,160,128]{2,1,0:T(8,128)(2,1)} %get-tuple-element.116) | copy-start | bytes 1966084
  136.5 6.9 %collective-permute-start.3 = (bf16[16,160,128]{2,1,0:T(8,128)(2,1)}, bf16[16,160,128]{2,1,0:T(8,128)(2,1)S(1)}, u32[]{:S(2)}, u32[]{:S(2)}) collective-permute-start(bf16[16,160,128]{2,1,0:T(8,128)(2,1)} %get-tuple-element.117), channel_id=1, source_target_pairs={{0,8},{8,0},{16,24},{24,16},{1,9},{9,1},{17,25},{25,17},{2,10},{10... | collective-permute-start | bytes 1966088 | tf_op jit(solution)/shard_map/ppermute | solution.py:798
  141.2 5.3 %copy-start = (bf16[192,128]{1,0:T(8,128)(2,1)S(1)}, bf16[192,128]{1,0:T(8,128)(2,1)}, u32[]{:S(2)}) copy-start(bf16[192,128]{1,0:T(8,128)(2,1)} %get-tuple-element.120.refs_1_) | copy-start | bytes 147460
  141.2 3.2 %collective-permute-start.4 = (bf16[192,128]{1,0:T(8,128)(2,1)}, bf16[192,128]{1,0:T(8,128)(2,1)S(1)}, u32[]{:S(2)}, u32[]{:S(2)}) collective-permute-start(bf16[192,128]{1,0:T(8,128)(2,1)} %get-tuple-element.121), channel_id=1, source_target_pairs={{0,8},{8,0},{16,24},{24,16},{1,9},{9,1},{17,25},{25,17},{2,10},{10... | collective-permute-start | bytes 147464 | tf_op jit(solution)/shard_map/ppermute | solution.py:916
  141.3 3.2 %collective-permute-start.5 = (bf16[192,128]{1,0:T(8,128)(2,1)}, bf16[192,128]{1,0:T(8,128)(2,1)S(1)}, u32[]{:S(2)}, u32[]{:S(2)}) collective-permute-start(bf16[192,128]{1,0:T(8,128)(2,1)} %get-tuple-element.122), channel_id=1, source_target_pairs={{0,16},{8,24},{16,0},{24,8},{1,17},{9,25},{17,1},{25,9},{2,18},{10... | collective-permute-start | bytes 147464 | tf_op jit(solution)/shard_map/ppermute | solution.py:916
  142.1 4.3 %collective-permute-start.6 = (bf16[192,128]{1,0:T(8,128)(2,1)}, bf16[192,128]{1,0:T(8,128)(2,1)S(1)}, u32[]{:S(2)}, u32[]{:S(2)}) collective-permute-start(bf16[192,128]{1,0:T(8,128)(2,1)} %get-tuple-element.123), channel_id=1, source_target_pairs={{0,24},{8,16},{16,8},{24,0},{1,25},{9,17},{17,9},{25,1},{2,26},{10... | collective-permute-start | bytes 147464 | tf_op jit(solution)/shard_map/ppermute | solution.py:916
  147.7 24.2 %all-to-all-start.5 = ((bf16[16,160,128]{2,1,0:T(8,128)(2,1)}), bf16[16,160,128]{2,1,0:T(8,128)(2,1)S(1)}, u32[]{:S(2)}, u32[]{:S(2)}) async-start(bf16[16,160,128]{2,1,0:T(8,128)(2,1)} %add_convert_fusion), calls=%async_computation.5 | async-start | bytes 1310720 | tf_op jit(solution)/shard_map/all_to_all | solution.py:794
  172.0 0.7 copy-start.1
  172.7 6.8 %copy-start.6 = (f32[8,512]{1,0:T(8,128)S(1)}, f32[8,512]{1,0:T(8,128)}, u32[]{:S(2)}) copy-start(f32[8,512]{1,0:T(8,128)} %get-tuple-element.129) | copy-start | bytes 49156
  173.9 28.5 %all-to-all-start.6 = ((bf16[16,176,128]{2,1,0:T(8,128)(2,1)}), bf16[16,176,128]{2,1,0:T(8,128)(2,1)S(1)}, u32[]{:S(2)}, u32[]{:S(2)}) async-start(bf16[16,176,128]{2,1,0:T(8,128)(2,1)} %late_sum.1), calls=%async_computation.6 | async-start | bytes 1441792 | tf_op jit(solution)/shard_map/all_to_all | solution.py:794
  179.5 21.5 %collective-permute-start.7 = (f32[8,512]{1,0:T(8,128)S(1)}, f32[8,512]{1,0:T(8,128)S(1)}, u32[]{:S(2)}, u32[]{:S(2)}) collective-permute-start(f32[8,512]{1,0:T(8,128)S(1)} %copy-done.6), channel_id=1, source_target_pairs={{1,0},{2,1},{3,2},{4,3},{5,4},{6,5},{7,6},{9,8},{10,9},{11,10},{12... | collective-permute-start | bytes 49160 | tf_op jit(solution)/shard_map/ppermute | solution.py:907
  202.4 4.8 %collective-permute-start.8 = (bf16[16,176,128]{2,1,0:T(8,128)(2,1)S(1)}, bf16[16,176,128]{2,1,0:T(8,128)(2,1)S(1)}, u32[]{:S(2)}, u32[]{:S(2)}) collective-permute-start(bf16[16,176,128]{2,1,0:T(8,128)(2,1)S(1)} %all-to-all-done.6.refs_0_), channel_id=1, source_target_pairs={{0,8},{8,0},{16,24},{24,16},{1,9},{9,1},{17,25},{25,17},{2,10},{10... | collective-permute-start | bytes 2162696 | tf_op jit(solution)/shard_map/ppermute | solution.py:798
Sparse Core Ops, SparseCore 0:
  89.0 47.6 all-gather.3
  147.9 69.7 all-gather.5
